TPU v7x, 512 devices: a whole 4x4x16 slice. The times are simulated.
512 devices in a mesh: inner: 8 (over y, x_hi), outer: 32 (over z, core), head: 2 (over x_lo).
Axes of the slice: x: 4 (x_hi: 2, x_lo: 2; x = x_hi * 2 + x_lo), y: 4, z: 16, core: 2. Of those that a mesh axis runs over, the one named last changes fastest.
Arguments:
- queries: bfloat16 [65536, 2048], P(('inner', 'outer'), 'head'), may hold values from -6 to 6
- keys: bfloat16 [65536, 512], P(('inner', 'outer')), may hold values from -6 to 6
- values: bfloat16 [65536, 512], P(('inner', 'outer')), may hold values from -6 to 6
- attn_out: bfloat16 [65536, 2048], P(('inner', 'outer'), 'head'), may hold values from -6 to 6
- grad_out: bfloat16 [65536, 2048], P(('inner', 'outer'), 'head'), may hold values from -96 to 96
- row_total: float32 [16, 65536], P('head', ('inner', 'outer')), may hold values from 2048 to 8192
- block_ids: int32 [512], replicated, may hold values from 0 to 511, each once
Outputs:
- grad_queries: bfloat16 [65536, 2048], P(('inner', 'outer'), 'head')
- grad_keys: bfloat16 [65536, 512], P(('inner', 'outer'), 'head')
- grad_values: bfloat16 [65536, 512], P(('inner', 'outer'), 'head')
Inputs may be any that keep to these rules, and one draw needn't show every extreme that they name: `block_ids`: A permutation: every sequence block is stored exactly once.
All inputs are finite; a program needn't handle non-finite values.
Results may differ from a plain program's by a relative error of at most 0.005.
Values may be sent and summed in bfloat16 or wider, within the bound.
No kernel may reach another device: no remote copies, remote signals or barrier semaphores. Data moves between devices by JAX's collectives and lax.ppermute only.
A program may use at most 64 MiB of HBM per device.

v0:
```python
import math

import jax
import jax.numpy as jnp
from jax import lax
from jax.sharding import PartitionSpec as P

KVH = 4
HD = 128


def from_behind(block, axis, distance):
    devices = range(lax.axis_size(axis))
    route = [((i - distance) % len(devices), i) for i in devices]
    return lax.ppermute(block, axis, route)


def per_device(queries, keys, values, attn_out, grad_out, row_total, block_ids):
    row_count = queries.shape[0]
    block_rows = row_count // 2
    local_heads = queries.shape[1] // HD
    per_kv = local_heads // KVH
    inner_count = lax.axis_size("inner")
    outer_count = lax.axis_size("outer")
    inner_pos = lax.axis_index("inner")
    outer_pos = lax.axis_index("outer")
    scale = 1.0 / math.sqrt(HD)
    query_heads = queries.reshape(row_count, per_kv, KVH, HD)
    grad_heads = grad_out.reshape(row_count, per_kv, KVH, HD)
    out_heads = attn_out.reshape(row_count, per_kv, KVH, HD)
    delta = jnp.transpose(
        jnp.sum(grad_heads.astype(jnp.float32) * out_heads.astype(jnp.float32), axis=-1), (1, 2, 0)
    )
    log_total = jnp.log(row_total).reshape(per_kv, KVH, row_count)

    def shard_blocks(shard):
        stored = lax.dynamic_slice(block_ids, (2 * shard,), (2,))
        return jnp.repeat(stored, block_rows, total_repeat_length=row_count)

    query_blocks = shard_blocks(inner_pos * outer_count + outer_pos)
    source_group = jnp.mod(outer_pos - 1, outer_count)

    def tile(first_head, last_head, key_value, grad_pair, source_pos):
        count = last_head - first_head
        key_blocks = shard_blocks(source_pos * outer_count + source_group)
        visible = key_blocks[None, :] < query_blocks[:, None]
        key_part = key_value[0].reshape(row_count, count, HD)
        value_part = key_value[1].reshape(row_count, count, HD)
        scores = (
            jnp.einsum("qgnd,knd->gnqk", query_heads, key_part, preferred_element_type=jnp.float32)
            * scale
        )
        shifted = scores - log_total[:, first_head:last_head, :, None]
        prob = jnp.where(visible[None, None], jnp.exp(shifted), jnp.float32(0.0))
        dprob = jnp.einsum(
            "qgnd,knd->gnqk", grad_heads, value_part, preferred_element_type=jnp.float32
        )
        dscore = prob * (dprob - delta[:, first_head:last_head, :, None])
        prob_low = prob.astype(jnp.bfloat16)
        dscore_low = dscore.astype(jnp.bfloat16)
        grad_v = jnp.einsum(
            "gnqk,qgnd->knd", prob_low, grad_heads, preferred_element_type=jnp.float32
        )
        grad_k = (
            jnp.einsum(
                "gnqk,qgnd->knd", dscore_low, query_heads, preferred_element_type=jnp.float32
            )
            * scale
        )
        grad_q = (
            jnp.einsum("gnqk,knd->qgnd", dscore_low, key_part, preferred_element_type=jnp.float32)
            * scale
        )
        update = jnp.stack([grad_k, grad_v]).reshape(2, row_count, count * HD)
        return (grad_q, grad_pair + update)

    key_value = jnp.stack([keys, values])
    key_value = from_behind(key_value, "outer", 1)
    zero_grads = jnp.zeros((2, row_count, KVH * HD), jnp.float32)
    zero_query = jnp.zeros((row_count, per_kv, KVH, HD), jnp.float32)

    def step(turn, carry):
        visiting, grad_pair, grad_query = carry
        source_pos = jnp.mod(inner_pos - turn, inner_count)
        part, grad_pair = tile(0, KVH, visiting, grad_pair, source_pos)
        visiting = from_behind(visiting, "inner", 1)
        grad_pair = from_behind(grad_pair, "inner", 1)
        return (visiting, grad_pair, grad_query + part)

    _, grad_pair, grad_query = lax.fori_loop(
        0, inner_count, step, (key_value, zero_grads, zero_query)
    )
    returned = from_behind(grad_pair, "outer", -1)
    summed = lax.psum_scatter(returned, "head", scatter_dimension=2, tiled=True)
    grad_queries = grad_query.reshape(row_count, local_heads * HD).astype(jnp.bfloat16)
    return (grad_queries, summed[0].astype(jnp.bfloat16), summed[1].astype(jnp.bfloat16))


def solution(mesh):
    in_specs = (
        P(("inner", "outer"), "head"),
        P(("inner", "outer"), None),
        P(("inner", "outer"), None),
        P(("inner", "outer"), "head"),
        P(("inner", "outer"), "head"),
        P("head", ("inner", "outer")),
        P(),
    )
    out_specs = (
        P(("inner", "outer"), "head"),
        P(("inner", "outer"), "head"),
        P(("inner", "outer"), "head"),
    )
    return jax.shard_map(
        per_device, mesh=mesh, in_specs=in_specs, out_specs=out_specs, check_vma=False
    )
```

profile of v0, /device:TPU:1, one launch (start us, length us, event | category | flops | bytes accessed | tf_op | source)
XLA Modules:
  0.0 457.7 jit_solution(9535936240475011994)
XLA Ops:
  9.6 3.0 collective-permute-start.2
  16.5 2.3 collective-permute-done.2
  18.8 308.0 %while.24 = (s32[]{:T(128)}, bf16[2,256,512]{1,2,0:T(8,128)(2,1)}, f32[2,256,512]{1,2,0:T(8,128)S(1)}, f32[256,2,4,128]{3,0,1,2:T(8,128)}, s32[]{:T(128)}, /*ind...) while((s32[]{:T(128)}, bf16[2,256,512]{1,2,0:T(8,128)(2,1)}, ...), condition=%wide.wide.region_2.0_spmd.clone, body=%wide.wide.region_1.0_spmd.clone.sunk | while | flops 676268800 | bytes 27168248 | solution.py:90
  22.1 1.7 fusion.68
  24.8 1.5 fusion.71
  27.5 4.6 %collective-permute-start.1 = (f32[2,256,512]{1,2,0:T(8,128)}, f32[2,256,512]{1,2,0:T(8,128)S(1)}, u32[]{:S(2)}, u32[]{:S(2)}) collective-permute-start(f32[2,256,512]{1,2,0:T(8,128)} %maximum_add_fusion.3), channel_id=1, source_target_pairs={{448,0},{0,64},{64,128},{128,192},{192,256},{256,320},{320,384},{3... | collective-permute-start | bytes 3145736 | tf_op jit(solution)/shard_map/while/body/eval_jaxpr/ppermute | solution.py:15
  32.1 3.1 collective-permute-start
  35.3 1.5 fusion.72
  36.8 24.3 %collective-permute-done = bf16[2,256,512]{1,2,0:T(8,128)(2,1)} collective-permute-done((bf16[2,256,512]{1,2,0:T(8,128)(2,1)S(1)}, bf16[2,256,512]{1,2,0:T(8,128)(2,1)}, u32[]{:S(2)}, u32[]{:S(2)}) %collective-permute-start) | collective-permute-done | bytes 524320 | tf_op jit(solution)/shard_map/while/body/eval_jaxpr/ppermute | solution.py:15
  64.3 1.7 fusion.68
  67.0 1.5 fusion.71
  69.7 2.3 collective-permute-start.1
  71.9 4.0 collective-permute-start
  76.0 2.7 fusion.72
  78.7 23.3 %collective-permute-done = bf16[2,256,512]{1,2,0:T(8,128)(2,1)} collective-permute-done((bf16[2,256,512]{1,2,0:T(8,128)(2,1)S(1)}, bf16[2,256,512]{1,2,0:T(8,128)(2,1)}, u32[]{:S(2)}, u32[]{:S(2)}) %collective-permute-start) | collective-permute-done | bytes 524320 | tf_op jit(solution)/shard_map/while/body/eval_jaxpr/ppermute | solution.py:15
  105.4 1.7 fusion.68
  110.7 1.9 collective-permute-start.1
  112.6 3.1 collective-permute-start
  115.7 2.7 fusion.72
  118.5 23.7 %collective-permute-done = bf16[2,256,512]{1,2,0:T(8,128)(2,1)} collective-permute-done((bf16[2,256,512]{1,2,0:T(8,128)(2,1)S(1)}, bf16[2,256,512]{1,2,0:T(8,128)(2,1)}, u32[]{:S(2)}, u32[]{:S(2)}) %collective-permute-start) | collective-permute-done | bytes 524320 | tf_op jit(solution)/shard_map/while/body/eval_jaxpr/ppermute | solution.py:15
  145.4 1.7 fusion.68
  150.7 1.9 collective-permute-start.1
  152.7 1.9 collective-permute-start
  154.6 2.7 fusion.72
  157.3 23.8 %collective-permute-done = bf16[2,256,512]{1,2,0:T(8,128)(2,1)} collective-permute-done((bf16[2,256,512]{1,2,0:T(8,128)(2,1)S(1)}, bf16[2,256,512]{1,2,0:T(8,128)(2,1)}, u32[]{:S(2)}, u32[]{:S(2)}) %collective-permute-start) | collective-permute-done | bytes 524320 | tf_op jit(solution)/shard_map/while/body/eval_jaxpr/ppermute | solution.py:15
  184.4 1.7 fusion.68
  189.7 1.9 collective-permute-start.1
  191.6 1.9 collective-permute-start
  193.6 2.7 fusion.72
  196.3 22.8 %collective-permute-done = bf16[2,256,512]{1,2,0:T(8,128)(2,1)} collective-permute-done((bf16[2,256,512]{1,2,0:T(8,128)(2,1)S(1)}, bf16[2,256,512]{1,2,0:T(8,128)(2,1)}, u32[]{:S(2)}, u32[]{:S(2)}) %collective-permute-start) | collective-permute-done | bytes 524320 | tf_op jit(solution)/shard_map/while/body/eval_jaxpr/ppermute | solution.py:15
  222.4 1.7 fusion.68
  227.7 1.9 collective-permute-start.1
  229.6 1.9 collective-permute-start
  231.6 2.7 fusion.72
  234.3 21.7 %collective-permute-done = bf16[2,256,512]{1,2,0:T(8,128)(2,1)} collective-permute-done((bf16[2,256,512]{1,2,0:T(8,128)(2,1)S(1)}, bf16[2,256,512]{1,2,0:T(8,128)(2,1)}, u32[]{:S(2)}, u32[]{:S(2)}) %collective-permute-start) | collective-permute-done | bytes 524320 | tf_op jit(solution)/shard_map/while/body/eval_jaxpr/ppermute | solution.py:15
  259.3 1.7 fusion.68
  264.6 1.9 collective-permute-start.1
  266.6 1.9 collective-permute-start
  268.5 2.7 fusion.72
  271.2 20.7 %collective-permute-done = bf16[2,256,512]{1,2,0:T(8,128)(2,1)} collective-permute-done((bf16[2,256,512]{1,2,0:T(8,128)(2,1)S(1)}, bf16[2,256,512]{1,2,0:T(8,128)(2,1)}, u32[]{:S(2)}, u32[]{:S(2)}) %collective-permute-start) | collective-permute-done | bytes 524320 | tf_op jit(solution)/shard_map/while/body/eval_jaxpr/ppermute | solution.py:15
  295.2 1.7 fusion.68
  300.6 1.9 collective-permute-start.1
  302.5 1.9 collective-permute-start
  304.4 2.7 fusion.72
  307.2 19.7 %collective-permute-done = bf16[2,256,512]{1,2,0:T(8,128)(2,1)} collective-permute-done((bf16[2,256,512]{1,2,0:T(8,128)(2,1)S(1)}, bf16[2,256,512]{1,2,0:T(8,128)(2,1)}, u32[]{:S(2)}, u32[]{:S(2)}) %collective-permute-start) | collective-permute-done | bytes 524320 | tf_op jit(solution)/shard_map/while/body/eval_jaxpr/ppermute | solution.py:15
  328.2 16.3 %collective-permute-start.3 = (f32[2,256,512]{2,1,0:T(8,128)}, f32[2,256,512]{2,1,0:T(8,128)S(1)}, u32[]{:S(2)}, u32[]{:S(2)}) collective-permute-start(f32[2,256,512]{2,1,0:T(8,128)} %copy.54), channel_id=1, source_target_pairs={{2,0},{4,2},{6,4},{8,6},{10,8},{12,10},{14,12},{16,14},{18,16},{20... | collective-permute-start | bytes 3145736 | tf_op jit(solution)/shard_map/ppermute | solution.py:15
  344.5 67.2 %collective-permute-done.3 = f32[2,256,512]{2,1,0:T(8,128)S(1)} collective-permute-done((f32[2,256,512]{2,1,0:T(8,128)}, f32[2,256,512]{2,1,0:T(8,128)S(1)}, u32[]{:S(2)}, u32[]{:S(2)}) %collective-permute-start.3) | collective-permute-done | bytes 1048608 | tf_op jit(solution)/shard_map/ppermute | solution.py:15
  414.5 34.7 %reduce-scatter.2.cloned.1.call-done = f32[2,256,256]{2,1,0:T(8,128)} async-done(((f32[2,256,512]{2,1,0:T(8,128)}), f32[2,256,256]{2,1,0:T(8,128)}) %reduce-scatter.2.cloned.1.call-update) | async-done | bytes 524304 | tf_op jit(solution)/shard_map/reduce_scatter | solution.py:94
  (135 shorter events, 63.8 us)
Async XLA Ops:
  7.2 5.4 %copy-start.6 = (f32[8,256]{1,0:T(8,128)S(1)}, f32[8,256]{1,0:T(8,128)}, u32[]{:S(2)}) copy-start(f32[8,256]{1,0:T(8,128)} %param.20) | copy-start | bytes 24580
  7.2 5.5 %copy-start.2 = (bf16[256,1024]{1,0:T(8,128)(2,1)S(1)}, bf16[256,1024]{1,0:T(8,128)(2,1)}, u32[]{:S(2)}) copy-start(bf16[256,1024]{1,0:T(8,128)(2,1)} %param.19) | copy-start | bytes 1572868
  7.2 5.7 %copy-start.3 = (bf16[256,1024]{1,0:T(8,128)(2,1)S(1)}, bf16[256,1024]{1,0:T(8,128)(2,1)}, u32[]{:S(2)}) copy-start(bf16[256,1024]{1,0:T(8,128)(2,1)} %param.15) | copy-start | bytes 1572868
  7.2 441.9 %reduce-scatter.2.cloned.1.call-start = ((), (), s32[]{:S(2)}) async-start(), calls=%async_computation.1 | async-start | bytes 1572864 | tf_op jit(solution)/shard_map/reduce_scatter | solution.py:94
  9.6 9.2 %collective-permute-start.2 = (bf16[2,256,512]{1,2,0:T(8,128)(2,1)S(1)}, bf16[2,256,512]{1,2,0:T(8,128)(2,1)}, u32[]{:S(2)}, u32[]{:S(2)}) collective-permute-start(bf16[2,256,512]{1,2,0:T(8,128)(2,1)S(1)} %pad_maximum_fusion), channel_id=1, source_target_pairs={{62,0},{0,2},{2,4},{4,6},{6,8},{8,10},{10,12},{12,14},{14,16},{16,... | collective-permute-start | bytes 1572872 | tf_op jit(solution)/shard_map/ppermute | solution.py:15
  12.6 1.4 copy-start.5
  12.6 1.3 copy-start.4
  12.9 1.5 copy-start.7
  27.5 33.6 %collective-permute-start.1 = (f32[2,256,512]{1,2,0:T(8,128)}, f32[2,256,512]{1,2,0:T(8,128)S(1)}, u32[]{:S(2)}, u32[]{:S(2)}) collective-permute-start(f32[2,256,512]{1,2,0:T(8,128)} %maximum_add_fusion.3), channel_id=1, source_target_pairs={{448,0},{0,64},{64,128},{128,192},{192,256},{256,320},{320,384},{3... | collective-permute-start | bytes 3145736 | tf_op jit(solution)/shard_map/while/body/eval_jaxpr/ppermute | solution.py:15
  32.1 28.9 %collective-permute-start = (bf16[2,256,512]{1,2,0:T(8,128)(2,1)S(1)}, bf16[2,256,512]{1,2,0:T(8,128)(2,1)}, u32[]{:S(2)}, u32[]{:S(2)}) collective-permute-start(bf16[2,256,512]{1,2,0:T(8,128)(2,1)S(1)} %copy.79), channel_id=1, source_target_pairs={{448,0},{0,64},{64,128},{128,192},{192,256},{256,320},{320,384},{3... | collective-permute-start | bytes 1572872 | tf_op jit(solution)/shard_map/while/body/eval_jaxpr/ppermute | solution.py:15
  69.7 32.4 %collective-permute-start.1 = (f32[2,256,512]{1,2,0:T(8,128)}, f32[2,256,512]{1,2,0:T(8,128)S(1)}, u32[]{:S(2)}, u32[]{:S(2)}) collective-permute-start(f32[2,256,512]{1,2,0:T(8,128)} %maximum_add_fusion.3), channel_id=1, source_target_pairs={{448,0},{0,64},{64,128},{128,192},{192,256},{256,320},{320,384},{3... | collective-permute-start | bytes 3145736 | tf_op jit(solution)/shard_map/while/body/eval_jaxpr/ppermute | solution.py:15
  71.9 30.2 %collective-permute-start = (bf16[2,256,512]{1,2,0:T(8,128)(2,1)S(1)}, bf16[2,256,512]{1,2,0:T(8,128)(2,1)}, u32[]{:S(2)}, u32[]{:S(2)}) collective-permute-start(bf16[2,256,512]{1,2,0:T(8,128)(2,1)S(1)} %copy.79), channel_id=1, source_target_pairs={{448,0},{0,64},{64,128},{128,192},{192,256},{256,320},{320,384},{3... | collective-permute-start | bytes 1572872 | tf_op jit(solution)/shard_map/while/body/eval_jaxpr/ppermute | solution.py:15
  110.7 31.4 %collective-permute-start.1 = (f32[2,256,512]{1,2,0:T(8,128)}, f32[2,256,512]{1,2,0:T(8,128)S(1)}, u32[]{:S(2)}, u32[]{:S(2)}) collective-permute-start(f32[2,256,512]{1,2,0:T(8,128)} %maximum_add_fusion.3), channel_id=1, source_target_pairs={{448,0},{0,64},{64,128},{128,192},{192,256},{256,320},{320,384},{3... | collective-permute-start | bytes 3145736 | tf_op jit(solution)/shard_map/while/body/eval_jaxpr/ppermute | solution.py:15
  112.6 29.5 %collective-permute-start = (bf16[2,256,512]{1,2,0:T(8,128)(2,1)S(1)}, bf16[2,256,512]{1,2,0:T(8,128)(2,1)}, u32[]{:S(2)}, u32[]{:S(2)}) collective-permute-start(bf16[2,256,512]{1,2,0:T(8,128)(2,1)S(1)} %copy.79), channel_id=1, source_target_pairs={{448,0},{0,64},{64,128},{128,192},{192,256},{256,320},{320,384},{3... | collective-permute-start | bytes 1572872 | tf_op jit(solution)/shard_map/while/body/eval_jaxpr/ppermute | solution.py:15
  150.7 30.4 %collective-permute-start.1 = (f32[2,256,512]{1,2,0:T(8,128)}, f32[2,256,512]{1,2,0:T(8,128)S(1)}, u32[]{:S(2)}, u32[]{:S(2)}) collective-permute-start(f32[2,256,512]{1,2,0:T(8,128)} %maximum_add_fusion.3), channel_id=1, source_target_pairs={{448,0},{0,64},{64,128},{128,192},{192,256},{256,320},{320,384},{3... | collective-permute-start | bytes 3145736 | tf_op jit(solution)/shard_map/while/body/eval_jaxpr/ppermute | solution.py:15
  152.7 28.5 %collective-permute-start = (bf16[2,256,512]{1,2,0:T(8,128)(2,1)S(1)}, bf16[2,256,512]{1,2,0:T(8,128)(2,1)}, u32[]{:S(2)}, u32[]{:S(2)}) collective-permute-start(bf16[2,256,512]{1,2,0:T(8,128)(2,1)S(1)} %copy.79), channel_id=1, source_target_pairs={{448,0},{0,64},{64,128},{128,192},{192,256},{256,320},{320,384},{3... | collective-permute-start | bytes 1572872 | tf_op jit(solution)/shard_map/while/body/eval_jaxpr/ppermute | solution.py:15
  189.7 29.4 %collective-permute-start.1 = (f32[2,256,512]{1,2,0:T(8,128)}, f32[2,256,512]{1,2,0:T(8,128)S(1)}, u32[]{:S(2)}, u32[]{:S(2)}) collective-permute-start(f32[2,256,512]{1,2,0:T(8,128)} %maximum_add_fusion.3), channel_id=1, source_target_pairs={{448,0},{0,64},{64,128},{128,192},{192,256},{256,320},{320,384},{3... | collective-permute-start | bytes 3145736 | tf_op jit(solution)/shard_map/while/body/eval_jaxpr/ppermute | solution.py:15
  191.6 27.4 %collective-permute-start = (bf16[2,256,512]{1,2,0:T(8,128)(2,1)S(1)}, bf16[2,256,512]{1,2,0:T(8,128)(2,1)}, u32[]{:S(2)}, u32[]{:S(2)}) collective-permute-start(bf16[2,256,512]{1,2,0:T(8,128)(2,1)S(1)} %copy.79), channel_id=1, source_target_pairs={{448,0},{0,64},{64,128},{128,192},{192,256},{256,320},{320,384},{3... | collective-permute-start | bytes 1572872 | tf_op jit(solution)/shard_map/while/body/eval_jaxpr/ppermute | solution.py:15
  227.7 28.3 %collective-permute-start.1 = (f32[2,256,512]{1,2,0:T(8,128)}, f32[2,256,512]{1,2,0:T(8,128)S(1)}, u32[]{:S(2)}, u32[]{:S(2)}) collective-permute-start(f32[2,256,512]{1,2,0:T(8,128)} %maximum_add_fusion.3), channel_id=1, source_target_pairs={{448,0},{0,64},{64,128},{128,192},{192,256},{256,320},{320,384},{3... | collective-permute-start | bytes 3145736 | tf_op jit(solution)/shard_map/while/body/eval_jaxpr/ppermute | solution.py:15
  229.6 26.4 %collective-permute-start = (bf16[2,256,512]{1,2,0:T(8,128)(2,1)S(1)}, bf16[2,256,512]{1,2,0:T(8,128)(2,1)}, u32[]{:S(2)}, u32[]{:S(2)}) collective-permute-start(bf16[2,256,512]{1,2,0:T(8,128)(2,1)S(1)} %copy.79), channel_id=1, source_target_pairs={{448,0},{0,64},{64,128},{128,192},{192,256},{256,320},{320,384},{3... | collective-permute-start | bytes 1572872 | tf_op jit(solution)/shard_map/while/body/eval_jaxpr/ppermute | solution.py:15
  264.6 27.3 %collective-permute-start.1 = (f32[2,256,512]{1,2,0:T(8,128)}, f32[2,256,512]{1,2,0:T(8,128)S(1)}, u32[]{:S(2)}, u32[]{:S(2)}) collective-permute-start(f32[2,256,512]{1,2,0:T(8,128)} %maximum_add_fusion.3), channel_id=1, source_target_pairs={{448,0},{0,64},{64,128},{128,192},{192,256},{256,320},{320,384},{3... | collective-permute-start | bytes 3145736 | tf_op jit(solution)/shard_map/while/body/eval_jaxpr/ppermute | solution.py:15
  266.6 25.4 %collective-permute-start = (bf16[2,256,512]{1,2,0:T(8,128)(2,1)S(1)}, bf16[2,256,512]{1,2,0:T(8,128)(2,1)}, u32[]{:S(2)}, u32[]{:S(2)}) collective-permute-start(bf16[2,256,512]{1,2,0:T(8,128)(2,1)S(1)} %copy.79), channel_id=1, source_target_pairs={{448,0},{0,64},{64,128},{128,192},{192,256},{256,320},{320,384},{3... | collective-permute-start | bytes 1572872 | tf_op jit(solution)/shard_map/while/body/eval_jaxpr/ppermute | solution.py:15
  300.6 26.3 %collective-permute-start.1 = (f32[2,256,512]{1,2,0:T(8,128)}, f32[2,256,512]{1,2,0:T(8,128)S(1)}, u32[]{:S(2)}, u32[]{:S(2)}) collective-permute-start(f32[2,256,512]{1,2,0:T(8,128)} %maximum_add_fusion.3), channel_id=1, source_target_pairs={{448,0},{0,64},{64,128},{128,192},{192,256},{256,320},{320,384},{3... | collective-permute-start | bytes 3145736 | tf_op jit(solution)/shard_map/while/body/eval_jaxpr/ppermute | solution.py:15
  302.5 24.4 %collective-permute-start = (bf16[2,256,512]{1,2,0:T(8,128)(2,1)S(1)}, bf16[2,256,512]{1,2,0:T(8,128)(2,1)}, u32[]{:S(2)}, u32[]{:S(2)}) collective-permute-start(bf16[2,256,512]{1,2,0:T(8,128)(2,1)S(1)} %copy.79), channel_id=1, source_target_pairs={{448,0},{0,64},{64,128},{128,192},{192,256},{256,320},{320,384},{3... | collective-permute-start | bytes 1572872 | tf_op jit(solution)/shard_map/while/body/eval_jaxpr/ppermute | solution.py:15
  326.8 85.9 %copy-start = (f32[256,2,4,128]{3,0,1,2:T(8,128)S(1)}, f32[256,2,4,128]{3,0,1,2:T(8,128)}, u32[]{:S(2)}) copy-start(f32[256,2,4,128]{3,0,1,2:T(8,128)} %get-tuple-element.376) | copy-start | bytes 3145732
  328.2 83.6 %collective-permute-start.3 = (f32[2,256,512]{2,1,0:T(8,128)}, f32[2,256,512]{2,1,0:T(8,128)S(1)}, u32[]{:S(2)}, u32[]{:S(2)}) collective-permute-start(f32[2,256,512]{2,1,0:T(8,128)} %copy.54), channel_id=1, source_target_pairs={{2,0},{4,2},{6,4},{8,6},{10,8},{12,10},{14,12},{16,14},{18,16},{20... | collective-permute-start | bytes 3145736 | tf_op jit(solution)/shard_map/ppermute | solution.py:15
  411.8 1.0 copy-start.1
Sparse Core Ops, SparseCore 0:
  412.9 36.1 reduce-scatter.1
where the time goes:
time: 460 us; the launch traced here: 458 us
  waiting for transfers between devices  284 us (62%)
  starting transfers between devices  57.7 us (13%)
  matrix products  54.1 us (12%)
  local copies, waits for them, and re-layouts  23.8 us (5%)
  other arithmetic  23.2 us (5%)
  between operations  14.2 us (3%)
    ppermute x18, waiting for transfers between devices, from_behind(): return lax.ppermute(block, axis, route)  249 us
    ppermute x18, starting transfers between devices, from_behind(): return lax.ppermute(block, axis, route)  57.6 us
    reduce_scatter x1, waiting for transfers between devices, per_device(): summed = lax.psum_scatter(returned, 'head', scatter_dimension=2, tiled=True)  34.7 us
    dot_general x8, matrix products, tile(): jnp.einsum('gnqk,knd->qgnd', dscore_low, key_part, preferred_element_type...  20.7 us
    dot_general x8, matrix products, tile(): jnp.einsum('qgnd,knd->gnqk', query_heads, key_part, preferred_element_typ...  13.6 us
    dot_general x8, matrix products, tile(): jnp.einsum('gnqk,qgnd->knd', dscore_low, query_heads, preferred_element_t...  12.1 us
    select_n x9, other arithmetic, shard_blocks(): return jnp.repeat(stored, block_rows, total_repeat_length=row_count)  11.9 us
  transfers between devices with their start and end apart: 19, of which 11 were waited for; matrix products, arithmetic and copies ran while one was open for 6% of the time, Pallas kernels for 0%

commit v1 on v0

v1 whole, which is shorter than its diff:
```python
import math

import jax
import jax.numpy as jnp
from jax import lax
from jax.experimental import pallas as pl
from jax.experimental.pallas import tpu as pltpu
from jax.sharding import Mesh
from jax.sharding import PartitionSpec as P

KVH = 4
HD = 128
TOK = 256
HALF = 128
SCALE = 1.0 / math.sqrt(HD)
EXP2_SCALE = SCALE * math.log2(math.e)
HIDDEN = 1.0e30
ROWS = 2 * TOK
AUX = 32
NT = (((1,), (1,)), ((), ()))
NN = (((1,), (0,)), ((), ()))
VMEM = pl.BlockSpec(memory_space=pltpu.VMEM)
SMEM = pl.BlockSpec(memory_space=pltpu.SMEM)
f32 = jnp.float32
bf16 = jnp.bfloat16
PARAMS = pltpu.CompilerParams(vmem_limit_bytes=40 * 2**20)


def dot(a, b, dims):
    return lax.dot_general(a, b, dims, preferred_element_type=f32)


def split3(x):
    a = x.astype(bf16)
    r = x - a.astype(f32)
    b = r.astype(bf16)
    c = (r - b.astype(f32)).astype(bf16)
    return a, b, c


def head_of(x):
    return 2 * (x % 2) + x // 2


def pack_kv(where, keys, values, own, other):
    mine = 2 * where[3] + where[1]
    opposite = 2 * (1 - where[3]) + (1 - where[1])
    for head, out in ((mine, own), (opposite, other)):
        columns = pl.ds(pl.multiple_of(head * HD, HD), HD)
        out[0] = keys[:, columns]
        out[1] = values[:, columns]


def pack_queries(queries, attn_out, grad_out, row_total, message):
    log_total = jnp.log(row_total[...]) * f32(math.log2(math.e))
    ones = jnp.ones((8, HD), bf16)
    for x in range(4):
        head = head_of(x)
        parts = []
        for n in range(2):
            h = n * KVH + head
            columns = slice(h * HD, (h + 1) * HD)
            grad = grad_out[:, columns]
            product = grad.astype(f32) * attn_out[:, columns].astype(f32)
            high = product.astype(bf16)
            low = (product - high.astype(f32)).astype(bf16)
            delta = (dot(ones, high, NT) + dot(ones, low, NT))[0:1]
            parts.append((log_total[h : h + 1], delta))
            for half in range(2):
                rows = slice(half * HALF, (half + 1) * HALF)
                at = (half * 2 + n) * HALF
                message[x, at : at + HALF] = queries[rows, columns]
                message[x, ROWS + at : ROWS + at + HALF] = grad[rows]
        table = []
        for which in range(2):
            for half in range(2):
                for n in range(2):
                    table.append(parts[n][which][:, half * HALF : (half + 1) * HALF])
        table = jnp.concatenate(table, axis=0)
        a, b, c = split3(table)
        pad = jnp.zeros((8, HALF), bf16)
        message[x, 2 * ROWS : 2 * ROWS + AUX] = jnp.concatenate([a, b, c, pad], axis=0)


def attend(ids, message, kv, dq, dkv, dqt, aux):
    for x in range(4):
        table = message[x, 2 * ROWS : 2 * ROWS + AUX, :].astype(f32)
        aux[x] = table[0:8] + table[8:16] + table[16:24]
    dqt[...] = jnp.zeros_like(dqt)

    def row(x, which, half):
        at = which * 4 + half * 2
        return jnp.concatenate([aux[x, at : at + 1, :], aux[x, at + 1 : at + 2, :]], axis=1)

    def shard(j, carry):
        k = kv[j, 0]
        v = kv[j, 1]
        kt = k.T
        dk = jnp.zeros((TOK, HD), f32)
        dv = jnp.zeros((TOK, HD), f32)
        for x_hi in range(2):
            for half in range(2):
                query_block = ids[x_hi * 2 + half]
                hide = [
                    jnp.where(ids[4 + 2 * j + i] < query_block, 0.0, HIDDEN).astype(f32)
                    for i in range(2)
                ]
                for x_lo in range(2):
                    x = x_hi * 2 + x_lo
                    at = half * TOK
                    q = message[x, at : at + TOK, :]
                    g = message[x, ROWS + at : ROWS + at + TOK, :]
                    scores = dot(k, q, NT)
                    dprob = dot(v, g, NT)
                    shift = row(x, 0, half)
                    delta = row(x, 1, half)
                    prob = jnp.concatenate(
                        [
                            jnp.exp2(scores[:HALF] * EXP2_SCALE - (shift + hide[0])),
                            jnp.exp2(scores[HALF:] * EXP2_SCALE - (shift + hide[1])),
                        ],
                        axis=0,
                    )
                    ds = (prob * (dprob - delta)).astype(bf16)
                    dv = dv + dot(prob.astype(bf16), g, NN)
                    dk = dk + dot(ds, q, NN)
                    at = (x * 2 + half) * TOK
                    dqt[:, at : at + TOK] += dot(kt, ds, NN)
        dkv[j, 0] = (dk * SCALE).astype(bf16)
        dkv[j, 1] = dv.astype(bf16)
        return carry

    lax.fori_loop(0, kv.shape[0], shard, 0)
    for x in range(4):
        for half in range(2):
            at = (x * 2 + half) * TOK
            dq[x, half * TOK : (half + 1) * TOK, :] = (dqt[:, at : at + TOK] * SCALE).T.astype(bf16)


def add_partials(parts, own, other):
    for j, out in ((0, own), (1, other)):
        for i in range(2):
            total = parts[0, j, i].astype(f32)
            for y in range(1, parts.shape[0]):
                total = total + parts[y, j, i].astype(f32)
            out[i] = total.astype(bf16)


def unpack(where, dq, own, other, grad_queries, grad_keys, grad_values):
    for x in range(4):
        for n in range(2):
            h = n * KVH + head_of(x)
            for half in range(2):
                at = (half * 2 + n) * HALF
                grad_queries[half * HALF : (half + 1) * HALF, h * HD : (h + 1) * HD] = dq[x, at : at + HALF, :]
    mine = pl.ds(pl.multiple_of(where[1] * HD, HD), HD)
    rest = pl.ds(pl.multiple_of((1 - where[1]) * HD, HD), HD)
    for i, out in ((0, grad_keys), (1, grad_values)):
        out[:, mine] = own[i]
        out[:, rest] = other[i]


def shape(*dims):
    return jax.ShapeDtypeStruct(dims, bf16)


def per_device(queries, keys, values, attn_out, grad_out, row_total, block_ids):
    y_count = lax.axis_size("y")
    outer = lax.axis_size("outer")
    y = lax.axis_index("y")
    x_hi = lax.axis_index("x_hi")
    o = lax.axis_index("outer")
    x_lo = lax.axis_index("x_lo")
    where = jnp.stack([y, x_hi, o, x_lo]).astype(jnp.int32)
    names = ("x_hi", "outer", "x_lo")

    def route(step, turn):
        pairs = []
        for a in range(2):
            for b in range(outer):
                for c in range(2):
                    to_a, to_c = turn(a, c)
                    pairs.append(((a * outer + b) * 2 + c, (to_a * outer + (b + step) % outer) * 2 + to_c))
        return pairs

    own, other = pl.pallas_call(
        pack_kv,
        out_shape=(shape(2, TOK, HD), shape(2, TOK, HD)),
        in_specs=[SMEM, VMEM, VMEM],
        out_specs=(VMEM, VMEM),
        compiler_params=PARAMS,
        name="pack_kv",
    )(where, keys, values)
    own = lax.ppermute(own, names, route(1, lambda a, c: (a, c)))
    other = lax.ppermute(other, names, route(1, lambda a, c: (1 - a, 1 - c)))

    message = pl.pallas_call(
        pack_queries,
        out_shape=shape(4, 2 * ROWS + AUX, HD),
        in_specs=[VMEM] * 4,
        out_specs=VMEM,
        compiler_params=PARAMS,
        name="pack_queries",
    )(queries, attn_out, grad_out, row_total)
    message = lax.all_to_all(message, ("x_hi", "x_lo"), 0, 0, tiled=True)

    kv = lax.all_gather(jnp.stack([own, other]), "y", axis=0, tiled=True)

    stored = block_ids.reshape(y_count, 2, outer, 2)
    query_ids = lax.dynamic_slice(stored, (y, 0, o, 0), (1, 2, 1, 2)).reshape(4)
    key_ids = lax.dynamic_slice(stored, (0, 0, (o - 1) % outer, 0), (y_count, 2, 1, 2)).reshape(y_count, 2, 2)
    key_ids = jnp.where(x_hi == 0, key_ids, key_ids[:, ::-1]).reshape(-1)
    ids = jnp.concatenate([query_ids, key_ids])

    dq, dkv = pl.pallas_call(
        attend,
        out_shape=(shape(4, ROWS, HD), shape(2 * y_count, 2, TOK, HD)),
        in_specs=[SMEM, VMEM, VMEM],
        out_specs=(VMEM, VMEM),
        scratch_shapes=[pltpu.VMEM((HD, 4 * ROWS), f32), pltpu.VMEM((4, 8, HALF), f32)],
        compiler_params=PARAMS,
        name="attend",
    )(ids, message, kv)

    parts = lax.all_to_all(dkv.reshape(y_count, 2, 2, TOK, HD), "y", 0, 0, tiled=True)
    dq = lax.all_to_all(dq, ("x_hi", "x_lo"), 0, 0, tiled=True)
    own, other = pl.pallas_call(
        add_partials,
        out_shape=(shape(2, TOK, HD), shape(2, TOK, HD)),
        in_specs=[VMEM],
        out_specs=(VMEM, VMEM),
        compiler_params=PARAMS,
        name="add_partials",
    )(parts)
    own = lax.ppermute(own, names, route(-1, lambda a, c: (a, c)))
    other = lax.ppermute(other, names, route(-1, lambda a, c: (1 - a, c)))
    return pl.pallas_call(
        unpack,
        out_shape=(shape(TOK, 2 * KVH * HD), shape(TOK, 2 * HD), shape(TOK, 2 * HD)),
        in_specs=[SMEM, VMEM, VMEM, VMEM],
        out_specs=(VMEM, VMEM, VMEM),
        compiler_params=PARAMS,
        name="unpack",
    )(where, dq, own, other)


def solution(mesh):
    inner, outer, head = (mesh.shape[name] for name in ("inner", "outer", "head"))
    fine = Mesh(mesh.devices.reshape(inner // 2, 2, outer, head), ("y", "x_hi", "outer", "x_lo"))
    rows = ("y", "x_hi", "outer")
    in_specs = (
        P(rows, "x_lo"),
        P(rows, None),
        P(rows, None),
        P(rows, "x_lo"),
        P(rows, "x_lo"),
        P("x_lo", rows),
        P(),
    )
    out_specs = (P(rows, "x_lo"), P(rows, "x_lo"), P(rows, "x_lo"))
    return jax.shard_map(per_device, mesh=fine, in_specs=in_specs, out_specs=out_specs, check_vma=False)
```

time: 460 us -> 117 us (0.25)
  waiting for transfers between devices: 284 us -> 33.5 us
  matrix products: 54.1 us -> 0 us
  starting transfers between devices: 57.7 us -> 25.3 us
  other arithmetic: 23.2 us -> 0.89 us
  Pallas kernels: 0 us -> 21.7 us
  local copies, waits for them, and re-layouts: 23.8 us -> 4.8 us
  blocking collectives: 0 us -> 16.2 us
    ppermute x18 -> x4, waiting for transfers between devices: 249 us -> 6.64 us  [the longest x1 3.27 us: per_device(): other = lax.ppermute(other, names, route(-1, lambda a, c: (1 - a, c)))]
    dot_general x40 -> x0, matrix products: 54.1 us -> none  [the longest x8 20.7 us: tile(): jnp.einsum('gnqk,knd->qgnd', dscore_low, key_part, preferred_element_type...]
    ppermute x18 -> x4, starting transfers between devices: 57.6 us -> 16.1 us  [the longest x1 5.92 us: per_device(): other = lax.ppermute(other, names, route(-1, lambda a, c: (1 - a, c)))]
    reduce_scatter x1 -> x0, waiting for transfers between devices: 34.7 us -> none  [per_device(): summed = lax.psum_scatter(returned, 'head', scatter_dimension=2, tiled=True)]
    pallas_call x0 -> x5, Pallas kernels: none -> 21.7 us  [the longest x1 18 us: per_device(): pl.pallas_call(attend, out_shape=(shape(4, ROWS, HD), shape(2 * y_count,...]
    all_gather x0 -> x1, waiting for transfers between devices: none -> 17.4 us  [per_device(): kv = lax.all_gather(jnp.stack([own, other]), 'y', axis=0, tiled=True)]
    all_to_all x0 -> x1, blocking collectives: none -> 16.2 us  [per_device(): lax.all_to_all(dkv.reshape(y_count, 2, 2, TOK, HD), 'y', 0, 0, tiled=True)]
    select_n x9 -> x1, other arithmetic: 11.9 us -> 0.01 us  [per_device(): key_ids = jnp.where(x_hi == 0, key_ids, key_ids[:, ::-1]).reshape(-1)]
  transfers between devices with their start and end apart: 19 -> 7, of which waited for: 11 -> 5; matrix products, arithmetic and copies ran while one was open for 6% -> 1% of each run, Pallas kernels for 0% -> 1%
where the time goes in v1:
time: 117 us
  waiting for transfers between devices  33.5 us (29%)
  starting transfers between devices  25.3 us (22%)
  Pallas kernels  21.7 us (19%)
  blocking collectives  16.2 us (14%)
  between operations  14.2 us (12%)
  local copies, waits for them, and re-layouts  4.8 us (4%)
    pallas_call x1, Pallas kernels, per_device(): pl.pallas_call(attend, out_shape=(shape(4, ROWS, HD), shape(2 * y_count,...  18 us
    all_gather x1, waiting for transfers between devices, per_device(): kv = lax.all_gather(jnp.stack([own, other]), 'y', axis=0, tiled=True)  17.4 us
    all_to_all x1, blocking collectives, per_device(): lax.all_to_all(dkv.reshape(y_count, 2, 2, TOK, HD), 'y', 0, 0, tiled=True)  16.2 us
    all_to_all x1, waiting for transfers between devices, per_device(): message = lax.all_to_all(message, ('x_hi', 'x_lo'), 0, 0, tiled=True)  9.41 us
    ppermute x1, starting transfers between devices, per_device(): other = lax.ppermute(other, names, route(-1, lambda a, c: (1 - a, c)))  5.92 us
    all_to_all x1, starting transfers between devices, per_device(): message = lax.all_to_all(message, ('x_hi', 'x_lo'), 0, 0, tiled=True)  5.19 us
    unnamed x16, local copies, waits for them, and re-layouts  4.25 us
    ppermute x1, starting transfers between devices, per_device(): other = lax.ppermute(other, names, route(1, lambda a, c: (1 - a, 1 - c)))  4.12 us
  transfers between devices with their start and end apart: 7, of which 5 were waited for; matrix products, arithmetic and copies ran while one was open for 1% of the time, Pallas kernels for 1%

profile of v1, /device:TPU:1, one launch (start us, length us, event | category | flops | bytes accessed | tf_op | source)
XLA Modules:
  0.0 116.5 jit_solution(11261157310348885629)
XLA Ops:
  7.2 0.0 copy-start.2
  7.2 0.0 copy-start.1
  7.2 0.0 all-gather.2.cloned.1.call-start
  7.2 0.1 pad_add_fusion.where
  7.3 0.0 copy-start.4
  7.3 1.0 copy-done.4
  8.3 0.0 copy-start.5
  8.3 0.9 copy-done.5
  9.3 0.0 copy-start.6
  9.3 0.6 pack_kv.1
  9.9 3.0 %collective-permute-start = (bf16[2,256,128]{2,1,0:T(8,128)(2,1)S(1)}, bf16[2,256,128]{2,1,0:T(8,128)(2,1)S(1)}, u32[]{:S(2)}, u32[]{:S(2)}) collective-permute-start(bf16[2,256,128]{2,1,0:T(8,128)(2,1)S(1)} %get-tuple-element.9), channel_id=1, source_target_pairs={{0,2},{1,3},{2,4},{3,5},{4,6},{5,7},{6,8},{7,9},{8,10},{9,11},{10,... | collective-permute-start | bytes 393224 | tf_op jit(solution)/shard_map/ppermute | solution.py:194
  12.9 4.1 %collective-permute-start.1 = (bf16[2,256,128]{2,1,0:T(8,128)(2,1)S(1)}, bf16[2,256,128]{2,1,0:T(8,128)(2,1)S(1)}, u32[]{:S(2)}, u32[]{:S(2)}) collective-permute-start(bf16[2,256,128]{2,1,0:T(8,128)(2,1)S(1)} %get-tuple-element.10), channel_id=1, source_target_pairs={{0,67},{1,66},{2,69},{3,68},{4,71},{5,70},{6,73},{7,72},{8,75},{9,... | collective-permute-start | bytes 393224 | tf_op jit(solution)/shard_map/ppermute | solution.py:195
  17.1 0.6 collective-permute-done
  17.6 2.8 %collective-permute-done.1 = bf16[2,256,128]{2,1,0:T(8,128)(2,1)S(1)} collective-permute-done((bf16[2,256,128]{2,1,0:T(8,128)(2,1)S(1)}, bf16[2,256,128]{2,1,0:T(8,128)(2,1)S(1)}, u32[]{:S(2)}, u32[]{:S(2)}) %collective-permute-start.1) | collective-permute-done | bytes 131104 | tf_op jit(solution)/shard_map/ppermute | solution.py:195
  20.4 0.7 pad_maximum_fusion
  21.1 0.0 all-gather.2.cloned.1.call-update
  21.2 0.0 copy-done.2
  21.2 0.0 copy-done.1
  21.2 0.0 copy-done.6
  21.2 0.0 copy-start.3
  21.2 1.0 copy-done.3
  22.2 1.4 %pack_queries.1 = bf16[4,1056,128]{2,1,0:T(8,128)(2,1)} custom-call(bf16[256,1024]{1,0:T(8,128)(2,1)S(1)} %copy-done.1, bf16[256,1024]{1,0:T(8,128)(2,1)S(1)} %copy-done.2, bf16[256,1024]{1,0:T(8,128)(2,1)S(1)} %copy-done.3, f32[8,256]{1,0:T(8,128)S(1)} %copy-done.6), custom_call_target="tpu_custom_call" | custom-call | tf_op jit(solution)/shard_map/pack_queries/pallas_call | solution.py:197
  23.7 0.0 copy-start.7
  23.7 5.2 %all-to-all-start = ((bf16[4,1056,128]{2,1,0:T(8,128)(2,1)}), bf16[4,1056,128]{2,1,0:T(8,128)(2,1)S(1)}, u32[]{:S(2)}, u32[]{:S(2)}) async-start(bf16[4,1056,128]{2,1,0:T(8,128)(2,1)} %pack_queries.1), calls=%async_computation | async-start | bytes 2162688 | tf_op jit(solution)/shard_map/all_to_all | solution.py:205
  28.9 0.0 copy-done.7
  28.9 0.1 reshape.21
  29.0 0.1 copy.13
  29.2 0.1 reshape.22
  29.3 0.1 copy.14
  29.4 0.1 reshape.24
  29.5 0.1 pad_add_fusion.1.ids
  29.5 9.4 %all-to-all-done.message = bf16[4,1056,128]{2,1,0:T(8,128)(2,1)S(1)} async-done(((bf16[4,1056,128]{2,1,0:T(8,128)(2,1)}), bf16[4,1056,128]{2,1,0:T(8,128)(2,1)S(1)}, u32[]{:S(2)}, u32[]{:S(2)}) %all-to-all-start) | async-done | bytes 1081376 | tf_op jit(solution)/shard_map/all_to_all | solution.py:205
  38.9 17.4 %all-gather.2.cloned.1.call-done.kv = bf16[8,2,256,128]{3,2,1,0:T(8,128)(2,1)} async-done(((bf16[2,2,256,128]{3,2,1,0:T(8,128)(2,1)}), bf16[8,2,256,128]{3,2,1,0:T(8,128)(2,1)}) %all-gather.2.cloned.1.call-update) | async-done | bytes 1048592 | tf_op jit(solution)/shard_map/all_gather | solution.py:207
  56.3 0.0 copy-start
  56.3 1.2 %copy-done = bf16[8,2,256,128]{3,2,1,0:T(8,128)(2,1)S(1)} copy-done((bf16[8,2,256,128]{3,2,1,0:T(8,128)(2,1)S(1)}, bf16[8,2,256,128]{3,2,1,0:T(8,128)(2,1)}, u32[]{:S(2)}) %copy-start) | copy-done | bytes 1048600
  57.6 18.0 %attend.1 = (bf16[4,512,128]{2,1,0:T(8,128)(2,1)}, bf16[8,2,256,128]{3,2,1,0:T(8,128)(2,1)S(1)}) custom-call(s32[20]{0:T(128)S(1)} %pad_add_fusion.1.ids, bf16[4,1056,128]{2,1,0:T(8,128)(2,1)S(1)} %all-to-all-done.message, bf16[8,2,256,128]{3,2,1,0:T(8,128)(2,1)S(1)} %copy-done), custom_call_target="tpu_custom_call" | custom-call | tf_op jit(solution)/shard_map/attend/pallas_call | solution.py:215
  75.5 16.2 %all_to_all.15.parts = bf16[4,2,2,256,128]{4,3,2,1,0:T(8,128)(2,1)S(1)} all-to-all(bf16[4,2,2,256,128]{4,3,2,1,0:T(8,128)(2,1)S(1)} %bitcast.8), channel_id=1, replica_groups=mesh['y'=4,'x_hi'=2,'outer'=32,'x_lo'=2] {'y'}, dimensions={0} | all-to-all | bytes 2097152 | tf_op jit(solution)/shard_map/all_to_all | solution.py:225
  91.7 4.0 %all-to-all-start.1 = ((bf16[4,512,128]{2,1,0:T(8,128)(2,1)}), bf16[4,512,128]{2,1,0:T(8,128)(2,1)S(1)}, u32[]{:S(2)}, u32[]{:S(2)}) async-start(bf16[4,512,128]{2,1,0:T(8,128)(2,1)} %get-tuple-element.11), calls=%async_computation.1 | async-start | bytes 1048576 | tf_op jit(solution)/shard_map/all_to_all | solution.py:226
  95.7 0.1 add_partials.1
  95.8 3.1 %collective-permute-start.2 = (bf16[2,256,128]{2,1,0:T(8,128)(2,1)S(1)}, bf16[2,256,128]{2,1,0:T(8,128)(2,1)S(1)}, u32[]{:S(2)}, u32[]{:S(2)}) collective-permute-start(bf16[2,256,128]{2,1,0:T(8,128)(2,1)S(1)} %get-tuple-element.13), channel_id=1, source_target_pairs={{0,62},{1,63},{2,0},{3,1},{4,2},{5,3},{6,4},{7,5},{8,6},{9,7},{10,... | collective-permute-start | bytes 393224 | tf_op jit(solution)/shard_map/ppermute | solution.py:235
  98.9 5.9 %collective-permute-start.3 = (bf16[2,256,128]{2,1,0:T(8,128)(2,1)S(1)}, bf16[2,256,128]{2,1,0:T(8,128)(2,1)S(1)}, u32[]{:S(2)}, u32[]{:S(2)}) collective-permute-start(bf16[2,256,128]{2,1,0:T(8,128)(2,1)S(1)} %get-tuple-element.14), channel_id=1, source_target_pairs={{0,126},{1,127},{2,64},{3,65},{4,66},{5,67},{6,68},{7,69},{8,70},{... | collective-permute-start | bytes 393224 | tf_op jit(solution)/shard_map/ppermute | solution.py:236
  104.8 0.0 all-to-all-done.1.dq
  104.8 0.0 collective-permute-done.2.own
  104.8 3.3 %collective-permute-done.3.other = bf16[2,256,128]{2,1,0:T(8,128)(2,1)S(1)} collective-permute-done((bf16[2,256,128]{2,1,0:T(8,128)(2,1)S(1)}, bf16[2,256,128]{2,1,0:T(8,128)(2,1)S(1)}, u32[]{:S(2)}, u32[]{:S(2)}) %collective-permute-start.3) | collective-permute-done | bytes 131104 | tf_op jit(solution)/shard_map/ppermute | solution.py:236
  108.1 1.6 %unpack.1 = (bf16[256,1024]{1,0:T(8,128)(2,1)}, bf16[256,256]{1,0:T(8,128)(2,1)}, bf16[256,256]{1,0:T(8,128)(2,1)}) custom-call(s32[4]{0:T(128)S(1)} %pad_add_fusion.where, bf16[4,512,128]{2,1,0:T(8,128)(2,1)S(1)} %all-to-all-done.1.dq, bf16[2,256,128]{2,1,0:T(8,128)(2,1)S(1)} %collective-permute-done.2.own, ...), custom_call_target="tpu_custom_call" | custom-call | tf_op jit(solution)/shard_map/unpack/pallas_call | solution.py:237
  (3 shorter events, 0.0 us)
Async XLA Ops:
  7.2 14.0 %copy-start.2 = (bf16[256,1024]{1,0:T(8,128)(2,1)S(1)}, bf16[256,1024]{1,0:T(8,128)(2,1)}, u32[]{:S(2)}) copy-start(bf16[256,1024]{1,0:T(8,128)(2,1)} %attn_out.1) | copy-start | bytes 1572868
  7.2 14.0 %copy-start.1 = (bf16[256,1024]{1,0:T(8,128)(2,1)S(1)}, bf16[256,1024]{1,0:T(8,128)(2,1)}, u32[]{:S(2)}) copy-start(bf16[256,1024]{1,0:T(8,128)(2,1)} %queries.1) | copy-start | bytes 1572868
  7.2 49.2 %all-gather.2.cloned.1.call-start = ((), (), s32[]{:S(2)}) async-start(), calls=%async_computation.3 | async-start | bytes 1310720 | tf_op jit(solution)/shard_map/all_gather | solution.py:207
  7.3 1.0 copy-start.4
  8.3 0.9 copy-start.5
  9.3 11.9 %copy-start.6 = (f32[8,256]{1,0:T(8,128)S(1)}, f32[8,256]{1,0:T(8,128)}, u32[]{:S(2)}) copy-start(f32[8,256]{1,0:T(8,128)} %row_total.1) | copy-start | bytes 24580
  9.9 7.7 %collective-permute-start = (bf16[2,256,128]{2,1,0:T(8,128)(2,1)S(1)}, bf16[2,256,128]{2,1,0:T(8,128)(2,1)S(1)}, u32[]{:S(2)}, u32[]{:S(2)}) collective-permute-start(bf16[2,256,128]{2,1,0:T(8,128)(2,1)S(1)} %get-tuple-element.9), channel_id=1, source_target_pairs={{0,2},{1,3},{2,4},{3,5},{4,6},{5,7},{6,8},{7,9},{8,10},{9,11},{10,... | collective-permute-start | bytes 393224 | tf_op jit(solution)/shard_map/ppermute | solution.py:194
  12.9 7.5 %collective-permute-start.1 = (bf16[2,256,128]{2,1,0:T(8,128)(2,1)S(1)}, bf16[2,256,128]{2,1,0:T(8,128)(2,1)S(1)}, u32[]{:S(2)}, u32[]{:S(2)}) collective-permute-start(bf16[2,256,128]{2,1,0:T(8,128)(2,1)S(1)} %get-tuple-element.10), channel_id=1, source_target_pairs={{0,67},{1,66},{2,69},{3,68},{4,71},{5,70},{6,73},{7,72},{8,75},{9,... | collective-permute-start | bytes 393224 | tf_op jit(solution)/shard_map/ppermute | solution.py:195
  21.2 1.0 copy-start.3
  23.7 5.2 %copy-start.7 = (s32[512]{0:T(512)S(1)}, s32[512]{0:T(512)}, u32[]{:S(2)}) copy-start(s32[512]{0:T(512)} %param.13) | copy-start | bytes 6148
  23.7 15.3 %all-to-all-start = ((bf16[4,1056,128]{2,1,0:T(8,128)(2,1)}), bf16[4,1056,128]{2,1,0:T(8,128)(2,1)S(1)}, u32[]{:S(2)}, u32[]{:S(2)}) async-start(bf16[4,1056,128]{2,1,0:T(8,128)(2,1)} %pack_queries.1), calls=%async_computation | async-start | bytes 2162688 | tf_op jit(solution)/shard_map/all_to_all | solution.py:205
  56.3 1.2 %copy-start = (bf16[8,2,256,128]{3,2,1,0:T(8,128)(2,1)S(1)}, bf16[8,2,256,128]{3,2,1,0:T(8,128)(2,1)}, u32[]{:S(2)}) copy-start(bf16[8,2,256,128]{3,2,1,0:T(8,128)(2,1)} %all-gather.2.cloned.1.call-done.kv) | copy-start | bytes 3145732
  91.7 13.1 %all-to-all-start.1 = ((bf16[4,512,128]{2,1,0:T(8,128)(2,1)}), bf16[4,512,128]{2,1,0:T(8,128)(2,1)S(1)}, u32[]{:S(2)}, u32[]{:S(2)}) async-start(bf16[4,512,128]{2,1,0:T(8,128)(2,1)} %get-tuple-element.11), calls=%async_computation.1 | async-start | bytes 1048576 | tf_op jit(solution)/shard_map/all_to_all | solution.py:226
  95.8 9.0 %collective-permute-start.2 = (bf16[2,256,128]{2,1,0:T(8,128)(2,1)S(1)}, bf16[2,256,128]{2,1,0:T(8,128)(2,1)S(1)}, u32[]{:S(2)}, u32[]{:S(2)}) collective-permute-start(bf16[2,256,128]{2,1,0:T(8,128)(2,1)S(1)} %get-tuple-element.13), channel_id=1, source_target_pairs={{0,62},{1,63},{2,0},{3,1},{4,2},{5,3},{6,4},{7,5},{8,6},{9,7},{10,... | collective-permute-start | bytes 393224 | tf_op jit(solution)/shard_map/ppermute | solution.py:235
  98.9 9.2 %collective-permute-start.3 = (bf16[2,256,128]{2,1,0:T(8,128)(2,1)S(1)}, bf16[2,256,128]{2,1,0:T(8,128)(2,1)S(1)}, u32[]{:S(2)}, u32[]{:S(2)}) collective-permute-start(bf16[2,256,128]{2,1,0:T(8,128)(2,1)S(1)} %get-tuple-element.14), channel_id=1, source_target_pairs={{0,126},{1,127},{2,64},{3,65},{4,66},{5,67},{6,68},{7,69},{8,70},{... | collective-permute-start | bytes 393224 | tf_op jit(solution)/shard_map/ppermute | solution.py:236
Sparse Core Ops, SparseCore 0:
  21.3 35.0 all-gather.1

commit v2 on v1

v2 whole, which is shorter than its diff:
```python
import functools
import math

import jax
import jax.numpy as jnp
from jax import lax
from jax.experimental import pallas as pl
from jax.experimental.pallas import tpu as pltpu
from jax.sharding import Mesh
from jax.sharding import PartitionSpec as P

KVH = 4
HD = 128
TOK = 256
HALF = 128
SCALE = 1.0 / math.sqrt(HD)
EXP2_SCALE = SCALE * math.log2(math.e)
HIDDEN = 1.0e30
ROWS = 2 * TOK
AUX = 32
NT = (((1,), (1,)), ((), ()))
NN = (((1,), (0,)), ((), ()))
VMEM = pl.BlockSpec(memory_space=pltpu.VMEM)
HBM = pl.BlockSpec(memory_space=pltpu.HBM)
SMEM = pl.BlockSpec(memory_space=pltpu.SMEM)
f32 = jnp.float32
bf16 = jnp.bfloat16
FREE = pl.CostEstimate(flops=0, bytes_accessed=0, transcendentals=0)
PARAMS = pltpu.CompilerParams(vmem_limit_bytes=24 * 2**20)


def dot(a, b, dims):
    return lax.dot_general(a, b, dims, preferred_element_type=f32)


def split3(x):
    a = x.astype(bf16)
    r = x - a.astype(f32)
    b = r.astype(bf16)
    c = (r - b.astype(f32)).astype(bf16)
    return a, b, c


def head_of(x):
    return 2 * (x % 2) + x // 2


def pack_kv(where, keys, values, own, other, sems):
    mine = 2 * where[3] + where[1]
    opposite = 2 * (1 - where[3]) + (1 - where[1])
    copies = []
    for head, out in ((mine, own), (opposite, other)):
        columns = pl.ds(pl.multiple_of(head * HD, HD), HD)
        for i, source in ((0, keys), (1, values)):
            copies.append(pltpu.make_async_copy(source.at[:, columns], out.at[i], sems.at[len(copies)]))
    for copy in copies:
        copy.start()
    for copy in copies:
        copy.wait()


def pack_queries(queries, attn_out, grad_out, row_total, message, q_in, o_in, g_in, t_in, sems):
    copies = [
        pltpu.make_async_copy(source, target, sems.at[i])
        for i, (source, target) in enumerate(((row_total, t_in), (grad_out, g_in), (attn_out, o_in), (queries, q_in)))
    ]
    for copy in copies:
        copy.start()
    ones = jnp.ones((8, HD), bf16)
    copies[0].wait()
    log_total = jnp.log(t_in[...]) * f32(math.log2(math.e))
    copies[1].wait()
    copies[2].wait()
    for x in range(4):
        parts = []
        for n in range(2):
            h = n * KVH + head_of(x)
            columns = slice(h * HD, (h + 1) * HD)
            grad = g_in[:, columns]
            product = grad.astype(f32) * o_in[:, columns].astype(f32)
            high = product.astype(bf16)
            low = (product - high.astype(f32)).astype(bf16)
            delta = (dot(ones, high, NT) + dot(ones, low, NT))[0:1]
            parts.append((log_total[h : h + 1], delta))
            for half in range(2):
                at = ROWS + (half * 2 + n) * HALF
                message[x, at : at + HALF] = grad[half * HALF : (half + 1) * HALF]
        table = []
        for which in range(2):
            for half in range(2):
                for n in range(2):
                    table.append(parts[n][which][:, half * HALF : (half + 1) * HALF])
        table = jnp.concatenate(table, axis=0)
        a, b, c = split3(table)
        pad = jnp.zeros((8, HALF), bf16)
        message[x, 2 * ROWS : 2 * ROWS + AUX] = jnp.concatenate([a, b, c, pad], axis=0)
    copies[3].wait()
    for x in range(4):
        for n in range(2):
            h = n * KVH + head_of(x)
            for half in range(2):
                at = (half * 2 + n) * HALF
                message[x, at : at + HALF] = q_in[half * HALF : (half + 1) * HALF, h * HD : (h + 1) * HD]


def attend(first, last, turn, *refs):
    if first:
        where, ids, message, kv, dq_out, dkv = refs
    else:
        where, ids, message, kv, dq_in, dq_out, dkv = refs
    y, x_hi, o, outer = where[0], where[1], where[2], where[4]
    key_y = (y - turn) & 3
    key_o = jnp.where(o == 0, outer - 1, o - 1)
    k = kv[:, 0].reshape(2 * TOK, HD)
    v = kv[:, 1].reshape(2 * TOK, HD)
    kt = k.T
    key_blocks = []
    for j in range(2):
        key_x = x_hi if j == 0 else 1 - x_hi
        for half in range(2):
            key_blocks.append(ids[((key_y * 2 + key_x) * outer + key_o) * 2 + half])
    dk = jnp.zeros((2 * TOK, HD), f32)
    dv = jnp.zeros((2 * TOK, HD), f32)
    for x in range(4):
        table = message[x, 2 * ROWS : 2 * ROWS + AUX, :].astype(f32)
        table = table[0:8] + table[8:16] + table[16:24]
        shift = jnp.concatenate([table[i : i + 1] for i in range(4)], axis=1)
        delta = jnp.concatenate([table[i : i + 1] for i in range(4, 8)], axis=1)
        query_blocks = [ids[((y * 2 + x // 2) * outer + o) * 2 + half] for half in range(2)]
        q = message[x, 0:ROWS, :]
        g = message[x, ROWS : 2 * ROWS, :]
        scores = dot(k, q, NT)
        dprob = dot(v, g, NT)
        prob = []
        for i in range(4):
            hide = [
                jnp.full((1, TOK), jnp.where(key_blocks[i] < query_blocks[half], 0.0, HIDDEN).astype(f32))
                for half in range(2)
            ]
            row = shift + jnp.concatenate(hide, axis=1)
            prob.append(jnp.exp2(scores[i * HALF : (i + 1) * HALF] * EXP2_SCALE - row))
        prob = jnp.concatenate(prob, axis=0)
        ds = (prob * (dprob - delta)).astype(bf16)
        dv = dv + dot(prob.astype(bf16), g, NN)
        dk = dk + dot(ds, q, NN)
        at = x * ROWS
        dq = dot(kt, ds, NN)
        if not first:
            dq = dq + dq_in[:, at : at + ROWS]
        if last:
            dq_out[x] = (dq * SCALE).T.astype(bf16)
        else:
            dq_out[:, at : at + ROWS] = dq
    dkv[:, 0] = (dk * SCALE).astype(bf16).reshape(2, TOK, HD)
    dkv[:, 1] = dv.astype(bf16).reshape(2, TOK, HD)


def add_partials(a, b, c, d, own, other):
    for j, out in ((0, own), (1, other)):
        for i in range(2):
            total = a[j, i].astype(f32) + b[j, i].astype(f32)
            total = total + (c[j, i].astype(f32) + d[j, i].astype(f32))
            out[i] = total.astype(bf16)


def unpack_queries(dq, grad_queries):
    for x in range(4):
        for n in range(2):
            h = n * KVH + head_of(x)
            for half in range(2):
                at = (half * 2 + n) * HALF
                grad_queries[half * HALF : (half + 1) * HALF, h * HD : (h + 1) * HD] = dq[x, at : at + HALF, :]


def unpack_kv(where, own, other, grad_keys, grad_values, sems):
    mine = pl.ds(pl.multiple_of(where[1] * HD, HD), HD)
    rest = pl.ds(pl.multiple_of((1 - where[1]) * HD, HD), HD)
    copies = []
    for i, out in ((0, grad_keys), (1, grad_values)):
        for columns, part in ((mine, own), (rest, other)):
            copies.append(pltpu.make_async_copy(part.at[i], out.at[:, columns], sems.at[len(copies)]))
    for copy in copies:
        copy.start()
    for copy in copies:
        copy.wait()


def shape(*dims):
    return jax.ShapeDtypeStruct(dims, bf16)


def per_device(queries, keys, values, attn_out, grad_out, row_total, block_ids):
    y_count = lax.axis_size("y")
    outer = lax.axis_size("outer")
    y = lax.axis_index("y")
    x_hi = lax.axis_index("x_hi")
    o = lax.axis_index("outer")
    x_lo = lax.axis_index("x_lo")
    where = jnp.stack([y, x_hi, o, x_lo, jnp.int32(outer)]).astype(jnp.int32)
    names = ("x_hi", "outer", "x_lo")

    def route(step, turn):
        pairs = []
        for a in range(2):
            for b in range(outer):
                for c in range(2):
                    to_a, to_c = turn(a, c)
                    pairs.append(((a * outer + b) * 2 + c, (to_a * outer + (b + step) % outer) * 2 + to_c))
        return pairs

    def along_y(block, turn):
        return lax.ppermute(block, "y", [(i, (i + turn) % y_count) for i in range(y_count)])

    own, other = pl.pallas_call(
        pack_kv,
        out_shape=(shape(2, TOK, HD), shape(2, TOK, HD)),
        in_specs=[SMEM, HBM, HBM],
        out_specs=(VMEM, VMEM),
        scratch_shapes=[pltpu.SemaphoreType.DMA((4,))],
        compiler_params=PARAMS,
        name="pack_kv",
    )(where, keys, values)
    own = lax.ppermute(own, names, route(1, lambda a, c: (a, c)))
    other = lax.ppermute(other, names, route(1, lambda a, c: (1 - a, 1 - c)))

    message = pl.pallas_call(
        pack_queries,
        out_shape=shape(4, 2 * ROWS + AUX, HD),
        in_specs=[HBM] * 4,
        out_specs=VMEM,
        scratch_shapes=[pltpu.VMEM((TOK, 2 * KVH * HD), bf16)] * 3
        + [pltpu.VMEM((2 * KVH, TOK), f32), pltpu.SemaphoreType.DMA((4,))],
        compiler_params=PARAMS,
        name="pack_queries",
    )(queries, attn_out, grad_out, row_total)
    own, other, message = lax.optimization_barrier((own, other, message))
    message = lax.all_to_all(message, ("x_hi", "x_lo"), 0, 0, tiled=True)

    kv = jnp.stack([own, other])
    order = (1, 3, 2, 0)
    blocks = {turn: along_y(kv, turn) for turn in order[:-1]}
    blocks[0] = kv

    dq = None
    partials = {}
    for turn in order:
        first, last = turn == order[0], turn == order[-1]
        dq_shape = shape(4, ROWS, HD) if last else jax.ShapeDtypeStruct((HD, 4 * ROWS), f32)
        dq, dkv = pl.pallas_call(
            functools.partial(attend, first, last, turn),
            out_shape=(dq_shape, shape(2, 2, TOK, HD)),
            in_specs=[SMEM, SMEM] + [VMEM] * (2 if first else 3),
            out_specs=(VMEM, VMEM),
            compiler_params=PARAMS,
            cost_estimate=FREE,
            name="attend_%d" % turn,
        )(where, block_ids, message, blocks[turn], *(() if first else (dq,)))
        partials[turn] = dkv if turn == 0 else along_y(dkv, -turn)

    dq = lax.all_to_all(dq, ("x_hi", "x_lo"), 0, 0, tiled=True)
    own, other = pl.pallas_call(
        add_partials,
        out_shape=(shape(2, TOK, HD), shape(2, TOK, HD)),
        in_specs=[VMEM] * 4,
        out_specs=(VMEM, VMEM),
        compiler_params=PARAMS,
        name="add_partials",
    )(*(partials[turn] for turn in range(4)))
    own = lax.ppermute(own, names, route(-1, lambda a, c: (a, c)))
    other = lax.ppermute(other, names, route(-1, lambda a, c: (1 - a, c)))
    grad_queries = pl.pallas_call(
        unpack_queries,
        out_shape=shape(TOK, 2 * KVH * HD),
        in_specs=[VMEM],
        out_specs=VMEM,
        compiler_params=PARAMS,
        name="unpack_queries",
    )(dq)
    grad_keys, grad_values = pl.pallas_call(
        unpack_kv,
        out_shape=(shape(TOK, 2 * HD), shape(TOK, 2 * HD)),
        in_specs=[SMEM, VMEM, VMEM],
        out_specs=(HBM, HBM),
        scratch_shapes=[pltpu.SemaphoreType.DMA((4,))],
        compiler_params=PARAMS,
        name="unpack_kv",
    )(where, own, other)
    return grad_queries, grad_keys, grad_values


def solution(mesh):
    inner, outer, head = (mesh.shape[name] for name in ("inner", "outer", "head"))
    fine = Mesh(mesh.devices.reshape(inner // 2, 2, outer, head), ("y", "x_hi", "outer", "x_lo"))
    rows = ("y", "x_hi", "outer")
    in_specs = (
        P(rows, "x_lo"),
        P(rows, None),
        P(rows, None),
        P(rows, "x_lo"),
        P(rows, "x_lo"),
        P("x_lo", rows),
        P(),
    )
    out_specs = (P(rows, "x_lo"), P(rows, "x_lo"), P(rows, "x_lo"))
    return jax.shard_map(per_device, mesh=fine, in_specs=in_specs, out_specs=out_specs, check_vma=False)
```

time: 117 us -> 79.7 us (0.68)
  the two profiles are of different devices: /device:TPU:1 before, /device:TPU:2 now
where the time goes in v2:
time: 79.7 us; the launch traced here: 79 us
  starting transfers between devices  48.1 us (60%)
  Pallas kernels  18.8 us (24%)
  local copies, waits for them, and re-layouts  5.81 us (7%)
  waiting for transfers between devices  5.41 us (7%)
  between operations  0.83 us (1%)
    ppermute x6, starting transfers between devices, along_y(): lax.ppermute(block, 'y', [(i, (i + turn) % y_count) for i in range(y_coun...  23.2 us
    pallas_call x4, Pallas kernels, per_device(): pl.pallas_call(functools.partial(attend, first, last, turn), out_shape=(d...  14.1 us
    ppermute x1, starting transfers between devices, per_device(): other = lax.ppermute(other, names, route(-1, lambda a, c: (1 - a, c)))  6.66 us
    unnamed x14, local copies, waits for them, and re-layouts  5.72 us
    all_to_all x1, starting transfers between devices, per_device(): message = lax.all_to_all(message, ('x_hi', 'x_lo'), 0, 0, tiled=True)  5.29 us
    ppermute x1, starting transfers between devices, per_device(): other = lax.ppermute(other, names, route(1, lambda a, c: (1 - a, 1 - c)))  5.01 us
    all_to_all x1, starting transfers between devices, per_device(): dq = lax.all_to_all(dq, ('x_hi', 'x_lo'), 0, 0, tiled=True)  4.81 us
    ppermute x1, starting transfers between devices, per_device(): own = lax.ppermute(own, names, route(-1, lambda a, c: (a, c)))  3.1 us
  transfers between devices with their start and end apart: 12, of which 3 were waited for; matrix products, arithmetic and copies ran while one was open for 0% of the time, Pallas kernels for 17%

profile of v2, /device:TPU:2, one launch (start us, length us, event | category | flops | bytes accessed | tf_op | source)
XLA Modules:
  0.0 79.0 jit_solution(9786517588731689414)
XLA Ops:
  0.6 0.1 stack.28.where.refs_0_
  0.7 0.0 copy-start.3
  0.7 0.9 %copy-done.3 = bf16[256,512]{1,0:T(8,128)(2,1)S(1)} copy-done((bf16[256,512]{1,0:T(8,128)(2,1)S(1)}, bf16[256,512]{1,0:T(8,128)(2,1)}, u32[]{:S(2)}) %copy-start.3) | copy-done | bytes 262168
  1.7 0.0 copy-start.4
  1.7 0.9 %copy-done.4 = bf16[256,512]{1,0:T(8,128)(2,1)S(1)} copy-done((bf16[256,512]{1,0:T(8,128)(2,1)S(1)}, bf16[256,512]{1,0:T(8,128)(2,1)}, u32[]{:S(2)}) %copy-start.4) | copy-done | bytes 262168
  2.6 0.6 pack_kv.1
  3.3 0.0 collective-permute-start
  3.3 5.0 %collective-permute-start.1 = (bf16[2,256,128]{2,1,0:T(8,128)(2,1)S(1)}, bf16[2,256,128]{2,1,0:T(8,128)(2,1)S(1)}, u32[]{:S(2)}, u32[]{:S(2)}) collective-permute-start(bf16[2,256,128]{2,1,0:T(8,128)(2,1)S(1)} %get-tuple-element.21), channel_id=1, source_target_pairs={{0,67},{1,66},{2,69},{3,68},{4,71},{5,70},{6,73},{7,72},{8,75},{9,... | collective-permute-start | bytes 393224 | tf_op jit(solution)/shard_map/ppermute | solution.py:224
  8.3 0.0 copy-start
  8.3 1.0 %copy-done = bf16[256,1024]{1,0:T(8,128)(2,1)S(1)} copy-done((bf16[256,1024]{1,0:T(8,128)(2,1)S(1)}, bf16[256,1024]{1,0:T(8,128)(2,1)}, u32[]{:S(2)}) %copy-start) | copy-done | bytes 524312
  9.4 0.0 copy-start.1
  9.4 1.0 %copy-done.1 = bf16[256,1024]{1,0:T(8,128)(2,1)S(1)} copy-done((bf16[256,1024]{1,0:T(8,128)(2,1)S(1)}, bf16[256,1024]{1,0:T(8,128)(2,1)}, u32[]{:S(2)}) %copy-start.1) | copy-done | bytes 524312
  10.4 0.0 copy-start.2
  10.4 1.0 %copy-done.2 = bf16[256,1024]{1,0:T(8,128)(2,1)S(1)} copy-done((bf16[256,1024]{1,0:T(8,128)(2,1)S(1)}, bf16[256,1024]{1,0:T(8,128)(2,1)}, u32[]{:S(2)}) %copy-start.2) | copy-done | bytes 524312
  11.4 0.0 copy-start.6
  11.4 0.7 copy-done.6
  12.1 1.7 %pack_queries.1 = bf16[4,1056,128]{2,1,0:T(8,128)(2,1)} custom-call(bf16[256,1024]{1,0:T(8,128)(2,1)S(1)} %copy-done, bf16[256,1024]{1,0:T(8,128)(2,1)S(1)} %copy-done.1, bf16[256,1024]{1,0:T(8,128)(2,1)S(1)} %copy-done.2, f32[8,256]{1,0:T(8,128)S(1)} %copy-done.6), custom_call_target="tpu_custom_call" | custom-call | tf_op jit(solution)/shard_map/pack_queries/pallas_call | solution.py:226
  13.9 0.0 copy-start.5
  13.9 1.0 %collective-permute-done = bf16[2,256,128]{2,1,0:T(8,128)(2,1)S(1)} collective-permute-done((bf16[2,256,128]{2,1,0:T(8,128)(2,1)S(1)}, bf16[2,256,128]{2,1,0:T(8,128)(2,1)S(1)}, u32[]{:S(2)}, u32[]{:S(2)}) %collective-permute-start) | collective-permute-done | bytes 131104 | tf_op jit(solution)/shard_map/ppermute | solution.py:223
  14.9 2.8 %collective-permute-done.1 = bf16[2,256,128]{2,1,0:T(8,128)(2,1)S(1)} collective-permute-done((bf16[2,256,128]{2,1,0:T(8,128)(2,1)S(1)}, bf16[2,256,128]{2,1,0:T(8,128)(2,1)S(1)}, u32[]{:S(2)}, u32[]{:S(2)}) %collective-permute-start.1) | collective-permute-done | bytes 131104 | tf_op jit(solution)/shard_map/ppermute | solution.py:224
  17.7 5.3 %all-to-all-start = ((bf16[4,1056,128]{2,1,0:T(8,128)(2,1)}), bf16[4,1056,128]{2,1,0:T(8,128)(2,1)S(1)}, u32[]{:S(2)}, u32[]{:S(2)}) async-start(bf16[4,1056,128]{2,1,0:T(8,128)(2,1)} %pack_queries.1), calls=%async_computation | async-start | bytes 2162688 | tf_op jit(solution)/shard_map/all_to_all | solution.py:237
  23.0 3.5 %collective-permute-start.4 = (bf16[2,2,256,128]{3,2,1,0:T(8,128)(2,1)S(1)}, bf16[2,2,256,128]{3,2,1,0:T(8,128)(2,1)S(1)}, u32[]{:S(2)}, u32[]{:S(2)}) collective-permute-start(bf16[2,2,256,128]{3,2,1,0:T(8,128)(2,1)S(1)} %pad_maximum_fusion.refs_3_), channel_id=1, source_target_pairs={{0,128},{128,256},{256,384},{384,0},{1,129},{129,257},{257,385},{3... | collective-permute-start | bytes 786440 | tf_op jit(solution)/shard_map/ppermute | solution.py:212
  26.5 3.6 %collective-permute-start.3 = (bf16[2,2,256,128]{3,2,1,0:T(8,128)(2,1)S(1)}, bf16[2,2,256,128]{3,2,1,0:T(8,128)(2,1)S(1)}, u32[]{:S(2)}, u32[]{:S(2)}) collective-permute-start(bf16[2,2,256,128]{3,2,1,0:T(8,128)(2,1)S(1)} %pad_maximum_fusion.refs_3_), channel_id=1, source_target_pairs={{0,384},{128,0},{256,128},{384,256},{1,385},{129,1},{257,129},{385... | collective-permute-start | bytes 786440 | tf_op jit(solution)/shard_map/ppermute | solution.py:212
  30.1 3.9 %collective-permute-start.2 = (bf16[2,2,256,128]{3,2,1,0:T(8,128)(2,1)S(1)}, bf16[2,2,256,128]{3,2,1,0:T(8,128)(2,1)S(1)}, u32[]{:S(2)}, u32[]{:S(2)}) collective-permute-start(bf16[2,2,256,128]{3,2,1,0:T(8,128)(2,1)S(1)} %pad_maximum_fusion.refs_3_), channel_id=1, source_target_pairs={{0,256},{128,384},{256,0},{384,128},{1,257},{129,385},{257,1},{385... | collective-permute-start | bytes 786440 | tf_op jit(solution)/shard_map/ppermute | solution.py:212
  34.0 0.0 collective-permute-done.4.refs_3_
  34.0 0.0 all-to-all-done.refs_2_
  34.0 0.0 copy-done.5
  34.0 3.3 %attend_1.1 = (f32[128,2048]{1,0:T(8,128)S(1)}, bf16[2,2,256,128]{3,2,1,0:T(8,128)(2,1)S(1)}) custom-call(s32[5]{0:T(128)S(1)} %stack.28.where.refs_0_, s32[512]{0:T(512)S(1)} %copy-done.5, bf16[4,1056,128]{2,1,0:T(8,128)(2,1)S(1)} %all-to-all-done.refs_2_, bf16[2,2,256,128]{3,2,1,0:T(8,128)(2,1)S(1)} %collective-permute-done.4.refs_3_), custom_call_target="tpu_custom_call" | custom-call | tf_op jit(solution)/shard_map/attend_1/pallas_call | solution.py:249
  37.3 0.0 collective-permute-done.3.refs_3_
  37.4 3.3 %attend_3.1 = (f32[128,2048]{1,0:T(8,128)S(1)}, bf16[2,2,256,128]{3,2,1,0:T(8,128)(2,1)S(1)}) custom-call(s32[5]{0:T(128)S(1)} %stack.28.where.refs_0_, s32[512]{0:T(512)S(1)} %copy-done.5, bf16[4,1056,128]{2,1,0:T(8,128)(2,1)S(1)} %all-to-all-done.refs_2_, bf16[2,2,256,128]{3,2,1,0:T(8,128)(2,1)S(1)} %collective-permute-done.3.refs_3_, ...), custom_call_target="tpu_custom_call" | custom-call | tf_op jit(solution)/shard_map/attend_3/pallas_call | solution.py:249
  40.7 0.0 collective-permute-done.2.refs_3_
  40.7 3.3 %attend_2.1 = (f32[128,2048]{1,0:T(8,128)S(1)}, bf16[2,2,256,128]{3,2,1,0:T(8,128)(2,1)S(1)}) custom-call(s32[5]{0:T(128)S(1)} %stack.28.where.refs_0_, s32[512]{0:T(512)S(1)} %copy-done.5, bf16[4,1056,128]{2,1,0:T(8,128)(2,1)S(1)} %all-to-all-done.refs_2_, bf16[2,2,256,128]{3,2,1,0:T(8,128)(2,1)S(1)} %collective-permute-done.2.refs_3_, ...), custom_call_target="tpu_custom_call" | custom-call | tf_op jit(solution)/shard_map/attend_2/pallas_call | solution.py:249
  44.0 5.2 %collective-permute-start.6 = (bf16[2,2,256,128]{3,2,1,0:T(8,128)(2,1)S(1)}, bf16[2,2,256,128]{3,2,1,0:T(8,128)(2,1)S(1)}, u32[]{:S(2)}, u32[]{:S(2)}) collective-permute-start(bf16[2,2,256,128]{3,2,1,0:T(8,128)(2,1)S(1)} %get-tuple-element.31), channel_id=1, source_target_pairs={{0,256},{128,384},{256,0},{384,128},{1,257},{129,385},{257,1},{385... | collective-permute-start | bytes 786440 | tf_op jit(solution)/shard_map/ppermute | solution.py:212
  49.2 2.2 %collective-permute-start.7 = (bf16[2,2,256,128]{3,2,1,0:T(8,128)(2,1)S(1)}, bf16[2,2,256,128]{3,2,1,0:T(8,128)(2,1)S(1)}, u32[]{:S(2)}, u32[]{:S(2)}) collective-permute-start(bf16[2,2,256,128]{3,2,1,0:T(8,128)(2,1)S(1)} %get-tuple-element.32), channel_id=1, source_target_pairs={{0,128},{128,256},{256,384},{384,0},{1,129},{129,257},{257,385},{3... | collective-permute-start | bytes 786440 | tf_op jit(solution)/shard_map/ppermute | solution.py:212
  51.5 4.8 %collective-permute-start.5 = (bf16[2,2,256,128]{3,2,1,0:T(8,128)(2,1)S(1)}, bf16[2,2,256,128]{3,2,1,0:T(8,128)(2,1)S(1)}, u32[]{:S(2)}, u32[]{:S(2)}) collective-permute-start(bf16[2,2,256,128]{3,2,1,0:T(8,128)(2,1)S(1)} %get-tuple-element.30), channel_id=1, source_target_pairs={{0,384},{128,0},{256,128},{384,256},{1,385},{129,1},{257,129},{385... | collective-permute-start | bytes 786440 | tf_op jit(solution)/shard_map/ppermute | solution.py:212
  56.3 4.2 %attend_0.1 = (bf16[4,512,128]{2,1,0:T(8,128)(2,1)}, bf16[2,2,256,128]{3,2,1,0:T(8,128)(2,1)S(1)}) custom-call(s32[5]{0:T(128)S(1)} %stack.28.where.refs_0_, s32[512]{0:T(512)S(1)} %copy-done.5, bf16[4,1056,128]{2,1,0:T(8,128)(2,1)S(1)} %all-to-all-done.refs_2_, bf16[2,2,256,128]{3,2,1,0:T(8,128)(2,1)S(1)} %pad_maximum_fusion.refs_3_, ...), custom_call_target="tpu_custom_call" | custom-call | tf_op jit(solution)/shard_map/attend_0/pallas_call | solution.py:249
  60.5 4.8 %all-to-all-start.1 = ((bf16[4,512,128]{2,1,0:T(8,128)(2,1)}), bf16[4,512,128]{2,1,0:T(8,128)(2,1)S(1)}, u32[]{:S(2)}, u32[]{:S(2)}) async-start(bf16[4,512,128]{2,1,0:T(8,128)(2,1)} %get-tuple-element.28), calls=%async_computation.1 | async-start | bytes 1048576 | tf_op jit(solution)/shard_map/all_to_all | solution.py:260
  65.3 0.0 collective-permute-done.6.c
  65.3 0.0 collective-permute-done.7.d
  65.3 0.0 collective-permute-done.5.b
  65.3 0.1 add_partials.1
  65.4 3.1 %collective-permute-start.8 = (bf16[2,256,128]{2,1,0:T(8,128)(2,1)S(1)}, bf16[2,256,128]{2,1,0:T(8,128)(2,1)S(1)}, u32[]{:S(2)}, u32[]{:S(2)}) collective-permute-start(bf16[2,256,128]{2,1,0:T(8,128)(2,1)S(1)} %get-tuple-element.33), channel_id=1, source_target_pairs={{0,62},{1,63},{2,0},{3,1},{4,2},{5,3},{6,4},{7,5},{8,6},{9,7},{10,... | collective-permute-start | bytes 393224 | tf_op jit(solution)/shard_map/ppermute | solution.py:269
  68.5 6.7 %collective-permute-start.9 = (bf16[2,256,128]{2,1,0:T(8,128)(2,1)S(1)}, bf16[2,256,128]{2,1,0:T(8,128)(2,1)S(1)}, u32[]{:S(2)}, u32[]{:S(2)}) collective-permute-start(bf16[2,256,128]{2,1,0:T(8,128)(2,1)S(1)} %get-tuple-element.34), channel_id=1, source_target_pairs={{0,126},{1,127},{2,64},{3,65},{4,66},{5,67},{6,68},{7,69},{8,70},{... | collective-permute-start | bytes 393224 | tf_op jit(solution)/shard_map/ppermute | solution.py:270
  75.2 0.0 all-to-all-done.1.dq
  75.2 0.9 %unpack_queries.1 = bf16[256,1024]{1,0:T(8,128)(2,1)} custom-call(bf16[4,512,128]{2,1,0:T(8,128)(2,1)S(1)} %all-to-all-done.1.dq), custom_call_target="tpu_custom_call" | custom-call | tf_op jit(solution)/shard_map/unpack_queries/pallas_call | solution.py:271
  76.1 0.0 collective-permute-done.8.own
  76.2 1.5 %collective-permute-done.9.other = bf16[2,256,128]{2,1,0:T(8,128)(2,1)S(1)} collective-permute-done((bf16[2,256,128]{2,1,0:T(8,128)(2,1)S(1)}, bf16[2,256,128]{2,1,0:T(8,128)(2,1)S(1)}, u32[]{:S(2)}, u32[]{:S(2)}) %collective-permute-start.9) | collective-permute-done | bytes 131104 | tf_op jit(solution)/shard_map/ppermute | solution.py:270
  77.7 1.3 %unpack_kv.1 = (bf16[256,256]{1,0:T(8,128)(2,1)}, bf16[256,256]{1,0:T(8,128)(2,1)}) custom-call(s32[5]{0:T(128)S(1)} %stack.28.where.refs_0_, bf16[2,256,128]{2,1,0:T(8,128)(2,1)S(1)} %collective-permute-done.8.own, bf16[2,256,128]{2,1,0:T(8,128)(2,1)S(1)} %collective-permute-done.9.other), custom_call_target="tpu_custom_call" | custom-call | tf_op jit(solution)/shard_map/unpack_kv/pallas_call | solution.py:279
  (1 shorter events, 0.0 us)
Async XLA Ops:
  0.7 1.0 %copy-start.3 = (bf16[256,512]{1,0:T(8,128)(2,1)S(1)}, bf16[256,512]{1,0:T(8,128)(2,1)}, u32[]{:S(2)}) copy-start(bf16[256,512]{1,0:T(8,128)(2,1)} %keys.1) | copy-start | bytes 786436
  1.7 0.9 %copy-start.4 = (bf16[256,512]{1,0:T(8,128)(2,1)S(1)}, bf16[256,512]{1,0:T(8,128)(2,1)}, u32[]{:S(2)}) copy-start(bf16[256,512]{1,0:T(8,128)(2,1)} %values.1) | copy-start | bytes 786436
  3.3 11.6 %collective-permute-start = (bf16[2,256,128]{2,1,0:T(8,128)(2,1)S(1)}, bf16[2,256,128]{2,1,0:T(8,128)(2,1)S(1)}, u32[]{:S(2)}, u32[]{:S(2)}) collective-permute-start(bf16[2,256,128]{2,1,0:T(8,128)(2,1)S(1)} %get-tuple-element.20), channel_id=1, source_target_pairs={{0,2},{1,3},{2,4},{3,5},{4,6},{5,7},{6,8},{7,9},{8,10},{9,11},{10,... | collective-permute-start | bytes 393224 | tf_op jit(solution)/shard_map/ppermute | solution.py:223
  3.3 14.4 %collective-permute-start.1 = (bf16[2,256,128]{2,1,0:T(8,128)(2,1)S(1)}, bf16[2,256,128]{2,1,0:T(8,128)(2,1)S(1)}, u32[]{:S(2)}, u32[]{:S(2)}) collective-permute-start(bf16[2,256,128]{2,1,0:T(8,128)(2,1)S(1)} %get-tuple-element.21), channel_id=1, source_target_pairs={{0,67},{1,66},{2,69},{3,68},{4,71},{5,70},{6,73},{7,72},{8,75},{9,... | collective-permute-start | bytes 393224 | tf_op jit(solution)/shard_map/ppermute | solution.py:224
  8.3 1.0 %copy-start = (bf16[256,1024]{1,0:T(8,128)(2,1)S(1)}, bf16[256,1024]{1,0:T(8,128)(2,1)}, u32[]{:S(2)}) copy-start(bf16[256,1024]{1,0:T(8,128)(2,1)} %queries.1) | copy-start | bytes 1572868
  9.4 1.0 %copy-start.1 = (bf16[256,1024]{1,0:T(8,128)(2,1)S(1)}, bf16[256,1024]{1,0:T(8,128)(2,1)}, u32[]{:S(2)}) copy-start(bf16[256,1024]{1,0:T(8,128)(2,1)} %attn_out.1) | copy-start | bytes 1572868
  10.4 1.0 %copy-start.2 = (bf16[256,1024]{1,0:T(8,128)(2,1)S(1)}, bf16[256,1024]{1,0:T(8,128)(2,1)}, u32[]{:S(2)}) copy-start(bf16[256,1024]{1,0:T(8,128)(2,1)} %grad_out.1) | copy-start | bytes 1572868
  11.4 0.7 copy-start.6
  13.9 20.2 %copy-start.5 = (s32[512]{0:T(512)S(1)}, s32[512]{0:T(512)}, u32[]{:S(2)}) copy-start(s32[512]{0:T(512)} %refs_1_.7) | copy-start | bytes 6148
  17.7 16.3 %all-to-all-start = ((bf16[4,1056,128]{2,1,0:T(8,128)(2,1)}), bf16[4,1056,128]{2,1,0:T(8,128)(2,1)S(1)}, u32[]{:S(2)}, u32[]{:S(2)}) async-start(bf16[4,1056,128]{2,1,0:T(8,128)(2,1)} %pack_queries.1), calls=%async_computation | async-start | bytes 2162688 | tf_op jit(solution)/shard_map/all_to_all | solution.py:237
  23.0 11.0 %collective-permute-start.4 = (bf16[2,2,256,128]{3,2,1,0:T(8,128)(2,1)S(1)}, bf16[2,2,256,128]{3,2,1,0:T(8,128)(2,1)S(1)}, u32[]{:S(2)}, u32[]{:S(2)}) collective-permute-start(bf16[2,2,256,128]{3,2,1,0:T(8,128)(2,1)S(1)} %pad_maximum_fusion.refs_3_), channel_id=1, source_target_pairs={{0,128},{128,256},{256,384},{384,0},{1,129},{129,257},{257,385},{3... | collective-permute-start | bytes 786440 | tf_op jit(solution)/shard_map/ppermute | solution.py:212
  26.5 10.8 %collective-permute-start.3 = (bf16[2,2,256,128]{3,2,1,0:T(8,128)(2,1)S(1)}, bf16[2,2,256,128]{3,2,1,0:T(8,128)(2,1)S(1)}, u32[]{:S(2)}, u32[]{:S(2)}) collective-permute-start(bf16[2,2,256,128]{3,2,1,0:T(8,128)(2,1)S(1)} %pad_maximum_fusion.refs_3_), channel_id=1, source_target_pairs={{0,384},{128,0},{256,128},{384,256},{1,385},{129,1},{257,129},{385... | collective-permute-start | bytes 786440 | tf_op jit(solution)/shard_map/ppermute | solution.py:212
  30.1 10.6 %collective-permute-start.2 = (bf16[2,2,256,128]{3,2,1,0:T(8,128)(2,1)S(1)}, bf16[2,2,256,128]{3,2,1,0:T(8,128)(2,1)S(1)}, u32[]{:S(2)}, u32[]{:S(2)}) collective-permute-start(bf16[2,2,256,128]{3,2,1,0:T(8,128)(2,1)S(1)} %pad_maximum_fusion.refs_3_), channel_id=1, source_target_pairs={{0,256},{128,384},{256,0},{384,128},{1,257},{129,385},{257,1},{385... | collective-permute-start | bytes 786440 | tf_op jit(solution)/shard_map/ppermute | solution.py:212
  44.0 21.3 %collective-permute-start.6 = (bf16[2,2,256,128]{3,2,1,0:T(8,128)(2,1)S(1)}, bf16[2,2,256,128]{3,2,1,0:T(8,128)(2,1)S(1)}, u32[]{:S(2)}, u32[]{:S(2)}) collective-permute-start(bf16[2,2,256,128]{3,2,1,0:T(8,128)(2,1)S(1)} %get-tuple-element.31), channel_id=1, source_target_pairs={{0,256},{128,384},{256,0},{384,128},{1,257},{129,385},{257,1},{385... | collective-permute-start | bytes 786440 | tf_op jit(solution)/shard_map/ppermute | solution.py:212
  49.2 16.1 %collective-permute-start.7 = (bf16[2,2,256,128]{3,2,1,0:T(8,128)(2,1)S(1)}, bf16[2,2,256,128]{3,2,1,0:T(8,128)(2,1)S(1)}, u32[]{:S(2)}, u32[]{:S(2)}) collective-permute-start(bf16[2,2,256,128]{3,2,1,0:T(8,128)(2,1)S(1)} %get-tuple-element.32), channel_id=1, source_target_pairs={{0,128},{128,256},{256,384},{384,0},{1,129},{129,257},{257,385},{3... | collective-permute-start | bytes 786440 | tf_op jit(solution)/shard_map/ppermute | solution.py:212
  51.5 13.8 %collective-permute-start.5 = (bf16[2,2,256,128]{3,2,1,0:T(8,128)(2,1)S(1)}, bf16[2,2,256,128]{3,2,1,0:T(8,128)(2,1)S(1)}, u32[]{:S(2)}, u32[]{:S(2)}) collective-permute-start(bf16[2,2,256,128]{3,2,1,0:T(8,128)(2,1)S(1)} %get-tuple-element.30), channel_id=1, source_target_pairs={{0,384},{128,0},{256,128},{384,256},{1,385},{129,1},{257,129},{385... | collective-permute-start | bytes 786440 | tf_op jit(solution)/shard_map/ppermute | solution.py:212
  60.5 14.7 %all-to-all-start.1 = ((bf16[4,512,128]{2,1,0:T(8,128)(2,1)}), bf16[4,512,128]{2,1,0:T(8,128)(2,1)S(1)}, u32[]{:S(2)}, u32[]{:S(2)}) async-start(bf16[4,512,128]{2,1,0:T(8,128)(2,1)} %get-tuple-element.28), calls=%async_computation.1 | async-start | bytes 1048576 | tf_op jit(solution)/shard_map/all_to_all | solution.py:260
  65.4 10.7 %collective-permute-start.8 = (bf16[2,256,128]{2,1,0:T(8,128)(2,1)S(1)}, bf16[2,256,128]{2,1,0:T(8,128)(2,1)S(1)}, u32[]{:S(2)}, u32[]{:S(2)}) collective-permute-start(bf16[2,256,128]{2,1,0:T(8,128)(2,1)S(1)} %get-tuple-element.33), channel_id=1, source_target_pairs={{0,62},{1,63},{2,0},{3,1},{4,2},{5,3},{6,4},{7,5},{8,6},{9,7},{10,... | collective-permute-start | bytes 393224 | tf_op jit(solution)/shard_map/ppermute | solution.py:269
  68.5 9.2 %collective-permute-start.9 = (bf16[2,256,128]{2,1,0:T(8,128)(2,1)S(1)}, bf16[2,256,128]{2,1,0:T(8,128)(2,1)S(1)}, u32[]{:S(2)}, u32[]{:S(2)}) collective-permute-start(bf16[2,256,128]{2,1,0:T(8,128)(2,1)S(1)} %get-tuple-element.34), channel_id=1, source_target_pairs={{0,126},{1,127},{2,64},{3,65},{4,66},{5,67},{6,68},{7,69},{8,70},{... | collective-permute-start | bytes 393224 | tf_op jit(solution)/shard_map/ppermute | solution.py:270

commit v3 on v2

--- a/solution.py
+++ b/solution.py
@@ -26,6 +26,8 @@
 f32 = jnp.float32
 bf16 = jnp.bfloat16
 FREE = pl.CostEstimate(flops=0, bytes_accessed=0, transcendentals=0)
+LONG = pl.CostEstimate(flops=10**10, bytes_accessed=0, transcendentals=0)
+WIDE = pltpu.CompilerParams(vmem_limit_bytes=60 * 2**20)
 PARAMS = pltpu.CompilerParams(vmem_limit_bytes=24 * 2**20)
 
 
@@ -45,21 +47,7 @@
     return 2 * (x % 2) + x // 2
 
 
-def pack_kv(where, keys, values, own, other, sems):
-    mine = 2 * where[3] + where[1]
-    opposite = 2 * (1 - where[3]) + (1 - where[1])
-    copies = []
-    for head, out in ((mine, own), (opposite, other)):
-        columns = pl.ds(pl.multiple_of(head * HD, HD), HD)
-        for i, source in ((0, keys), (1, values)):
-            copies.append(pltpu.make_async_copy(source.at[:, columns], out.at[i], sems.at[len(copies)]))
-    for copy in copies:
-        copy.start()
-    for copy in copies:
-        copy.wait()
-
-
-def pack_queries(queries, attn_out, grad_out, row_total, message, q_in, o_in, g_in, t_in, sems):
+def pack_queries(queries, attn_out, grad_out, row_total, message, q_in, o_in, g_in, t_in, staged, sems, out_sems):
     copies = [
         pltpu.make_async_copy(source, target, sems.at[i])
         for i, (source, target) in enumerate(((row_total, t_in), (grad_out, g_in), (attn_out, o_in), (queries, q_in)))
@@ -71,6 +59,7 @@
     log_total = jnp.log(t_in[...]) * f32(math.log2(math.e))
     copies[1].wait()
     copies[2].wait()
+    sends = []
     for x in range(4):
         parts = []
         for n in range(2):
@@ -84,7 +73,7 @@
             parts.append((log_total[h : h + 1], delta))
             for half in range(2):
                 at = ROWS + (half * 2 + n) * HALF
-                message[x, at : at + HALF] = grad[half * HALF : (half + 1) * HALF]
+                staged[x, at : at + HALF] = grad[half * HALF : (half + 1) * HALF]
         table = []
         for which in range(2):
             for half in range(2):
@@ -93,21 +82,24 @@
         table = jnp.concatenate(table, axis=0)
         a, b, c = split3(table)
         pad = jnp.zeros((8, HALF), bf16)
-        message[x, 2 * ROWS : 2 * ROWS + AUX] = jnp.concatenate([a, b, c, pad], axis=0)
-    copies[3].wait()
-    for x in range(4):
+        staged[x, 2 * ROWS : 2 * ROWS + AUX] = jnp.concatenate([a, b, c, pad], axis=0)
+        if x == 0:
+            copies[3].wait()
         for n in range(2):
             h = n * KVH + head_of(x)
             for half in range(2):
                 at = (half * 2 + n) * HALF
-                message[x, at : at + HALF] = q_in[half * HALF : (half + 1) * HALF, h * HD : (h + 1) * HD]
-
-
-def attend(first, last, turn, *refs):
-    if first:
-        where, ids, message, kv, dq_out, dkv = refs
-    else:
-        where, ids, message, kv, dq_in, dq_out, dkv = refs
+                staged[x, at : at + HALF] = q_in[half * HALF : (half + 1) * HALF, h * HD : (h + 1) * HD]
+        sends.append(pltpu.make_async_copy(staged.at[x], message.at[x], out_sems.at[x]))
+        sends[-1].start()
+    for send in sends:
+        send.wait()
+
+
+def attend(turn, first, last, *refs):
+    where, ids, message, kv = refs[:4]
+    dq_in = None if first else refs[4]
+    dq_out, dkv = refs[-2:]
     y, x_hi, o, outer = where[0], where[1], where[2], where[4]
     key_y = (y - turn) & 3
     key_o = jnp.where(o == 0, outer - 1, o - 1)
@@ -116,7 +108,7 @@
     kt = k.T
     key_blocks = []
     for j in range(2):
-        key_x = x_hi if j == 0 else 1 - x_hi
+        key_x = 1 - x_hi if j == 0 else x_hi
         for half in range(2):
             key_blocks.append(ids[((key_y * 2 + key_x) * outer + key_o) * 2 + half])
     dk = jnp.zeros((2 * TOK, HD), f32)
@@ -148,31 +140,30 @@
         if not first:
             dq = dq + dq_in[:, at : at + ROWS]
         if last:
-            dq_out[x] = (dq * SCALE).T.astype(bf16)
+            dq_out[x] = (dq * SCALE).astype(bf16)
         else:
             dq_out[:, at : at + ROWS] = dq
-    dkv[:, 0] = (dk * SCALE).astype(bf16).reshape(2, TOK, HD)
-    dkv[:, 1] = dv.astype(bf16).reshape(2, TOK, HD)
-
-
-def add_partials(a, b, c, d, own, other):
-    for j, out in ((0, own), (1, other)):
+    dkv[:, 0] = (dk * SCALE).astype(dkv.dtype).reshape(2, TOK, HD)
+    dkv[:, 1] = dv.astype(dkv.dtype).reshape(2, TOK, HD)
+
+
+def add_partials(a, b, c, mine, other, own):
+    for j, out in ((0, other), (1, own)):
         for i in range(2):
-            total = a[j, i].astype(f32) + b[j, i].astype(f32)
-            total = total + (c[j, i].astype(f32) + d[j, i].astype(f32))
-            out[i] = total.astype(bf16)
+            out[i] = (a[j, i].astype(f32) + b[j, i].astype(f32) + c[j, i].astype(f32) + mine[j, i]).astype(bf16)
 
 
 def unpack_queries(dq, grad_queries):
     for x in range(4):
+        part = dq[x].T
         for n in range(2):
             h = n * KVH + head_of(x)
             for half in range(2):
                 at = (half * 2 + n) * HALF
-                grad_queries[half * HALF : (half + 1) * HALF, h * HD : (h + 1) * HD] = dq[x, at : at + HALF, :]
-
-
-def unpack_kv(where, own, other, grad_keys, grad_values, sems):
+                grad_queries[half * HALF : (half + 1) * HALF, h * HD : (h + 1) * HD] = part[at : at + HALF]
+
+
+def unpack_kv(where, other, own, grad_keys, grad_values, sems):
     mine = pl.ds(pl.multiple_of(where[1] * HD, HD), HD)
     rest = pl.ds(pl.multiple_of((1 - where[1]) * HD, HD), HD)
     copies = []
@@ -211,63 +202,64 @@
     def along_y(block, turn):
         return lax.ppermute(block, "y", [(i, (i + turn) % y_count) for i in range(y_count)])
 
-    own, other = pl.pallas_call(
-        pack_kv,
-        out_shape=(shape(2, TOK, HD), shape(2, TOK, HD)),
-        in_specs=[SMEM, HBM, HBM],
-        out_specs=(VMEM, VMEM),
-        scratch_shapes=[pltpu.SemaphoreType.DMA((4,))],
-        compiler_params=PARAMS,
-        name="pack_kv",
-    )(where, keys, values)
+    def columns(head):
+        at = head * HD
+        return jnp.stack([lax.dynamic_slice(x, (0, at), (TOK, HD)) for x in (keys, values)])
+
+    other = columns(2 * (1 - x_lo) + (1 - x_hi))
+    own = columns(2 * x_lo + x_hi)
+    other = lax.ppermute(other, names, route(1, lambda a, c: (1 - a, 1 - c)))
     own = lax.ppermute(own, names, route(1, lambda a, c: (a, c)))
-    other = lax.ppermute(other, names, route(1, lambda a, c: (1 - a, 1 - c)))
 
     message = pl.pallas_call(
         pack_queries,
         out_shape=shape(4, 2 * ROWS + AUX, HD),
         in_specs=[HBM] * 4,
-        out_specs=VMEM,
+        out_specs=HBM,
         scratch_shapes=[pltpu.VMEM((TOK, 2 * KVH * HD), bf16)] * 3
-        + [pltpu.VMEM((2 * KVH, TOK), f32), pltpu.SemaphoreType.DMA((4,))],
-        compiler_params=PARAMS,
+        + [
+            pltpu.VMEM((2 * KVH, TOK), f32),
+            pltpu.VMEM((4, 2 * ROWS + AUX, HD), bf16),
+            pltpu.SemaphoreType.DMA((4,)),
+            pltpu.SemaphoreType.DMA((4,)),
+        ],
+        compiler_params=WIDE,
         name="pack_queries",
     )(queries, attn_out, grad_out, row_total)
-    own, other, message = lax.optimization_barrier((own, other, message))
+    other, own, message = lax.optimization_barrier((other, own, message))
     message = lax.all_to_all(message, ("x_hi", "x_lo"), 0, 0, tiled=True)
 
-    kv = jnp.stack([own, other])
-    order = (1, 3, 2, 0)
-    blocks = {turn: along_y(kv, turn) for turn in order[:-1]}
-    blocks[0] = kv
-
+    kv = jnp.stack([other, own])
+    turns = (1, 3, 2)
+    blocks = [along_y(kv, turn) for turn in turns] + [kv]
     dq = None
-    partials = {}
-    for turn in order:
-        first, last = turn == order[0], turn == order[-1]
-        dq_shape = shape(4, ROWS, HD) if last else jax.ShapeDtypeStruct((HD, 4 * ROWS), f32)
+    parts = []
+    for turn, block in zip(turns + (0,), blocks):
+        first, last = turn == turns[0], turn == 0
         dq, dkv = pl.pallas_call(
-            functools.partial(attend, first, last, turn),
-            out_shape=(dq_shape, shape(2, 2, TOK, HD)),
+            functools.partial(attend, turn, first, last),
+            out_shape=(
+                shape(4, HD, ROWS) if last else jax.ShapeDtypeStruct((HD, 4 * ROWS), f32),
+                jax.ShapeDtypeStruct((2, 2, TOK, HD), f32 if last else bf16),
+            ),
             in_specs=[SMEM, SMEM] + [VMEM] * (2 if first else 3),
             out_specs=(VMEM, VMEM),
             compiler_params=PARAMS,
             cost_estimate=FREE,
             name="attend_%d" % turn,
-        )(where, block_ids, message, blocks[turn], *(() if first else (dq,)))
-        partials[turn] = dkv if turn == 0 else along_y(dkv, -turn)
-
+        )(where, block_ids, message, block, *(() if first else (dq,)))
+        parts.append(dkv if last else along_y(dkv, -turn))
     dq = lax.all_to_all(dq, ("x_hi", "x_lo"), 0, 0, tiled=True)
-    own, other = pl.pallas_call(
+    other, own = pl.pallas_call(
         add_partials,
         out_shape=(shape(2, TOK, HD), shape(2, TOK, HD)),
         in_specs=[VMEM] * 4,
         out_specs=(VMEM, VMEM),
         compiler_params=PARAMS,
         name="add_partials",
-    )(*(partials[turn] for turn in range(4)))
+    )(*parts)
+    other = lax.ppermute(other, names, route(-1, lambda a, c: (1 - a, c)))
     own = lax.ppermute(own, names, route(-1, lambda a, c: (a, c)))
-    other = lax.ppermute(other, names, route(-1, lambda a, c: (1 - a, c)))
     grad_queries = pl.pallas_call(
         unpack_queries,
         out_shape=shape(TOK, 2 * KVH * HD),
@@ -284,7 +276,7 @@
         scratch_shapes=[pltpu.SemaphoreType.DMA((4,))],
         compiler_params=PARAMS,
         name="unpack_kv",
-    )(where, own, other)
+    )(where, other, own)
     return grad_queries, grad_keys, grad_values
 
 

time: 79.7 us -> 78 us (0.979)
  local copies, waits for them, and re-layouts: 5.81 us -> 1.06 us
  waiting for transfers between devices: 5.41 us -> 9.95 us
  starting transfers between devices: 48.1 us -> 46.4 us
    unnamed x14 -> x2, local copies, waits for them, and re-layouts: 5.72 us -> 0.01 us
    ppermute x1, waiting for transfers between devices: 2.84 us -> 6.8 us  [per_device(): other = lax.ppermute(other, names, route(1, lambda a, c: (1 - a, 1 - c)))]
    ppermute x1, starting transfers between devices: 5.01 us -> 2.84 us  [per_device(): other = lax.ppermute(other, names, route(1, lambda a, c: (1 - a, 1 - c)))]
    ppermute x1, starting transfers between devices: 0.02 us -> 2.04 us  [per_device(): own = lax.ppermute(own, names, route(1, lambda a, c: (a, c)))]
    ppermute x6, starting transfers between devices: 23.2 us -> 21.4 us  [along_y(): lax.ppermute(block, 'y', [(i, (i + turn) % y_count) for i in range(y_coun...]
    ppermute x1, waiting for transfers between devices: 1.55 us -> 0.01 us  [per_device(): other = lax.ppermute(other, names, route(-1, lambda a, c: (1 - a, c)))]
    ppermute x1, waiting for transfers between devices: 0.01 us -> 1.53 us  [per_device(): own = lax.ppermute(own, names, route(-1, lambda a, c: (a, c)))]
    ppermute x6, waiting for transfers between devices: 0.02 us -> 1.13 us  [along_y(): lax.ppermute(block, 'y', [(i, (i + turn) % y_count) for i in range(y_coun...]
  transfers between devices with their start and end apart: 12 -> 12, of which waited for: 3 -> 4; matrix products, arithmetic and copies ran while one was open for 0% -> 0% of each run, Pallas kernels for 17% -> 19%
where the time goes in v3:
time: 78 us; the launch traced here: 77.5 us
  starting transfers between devices  46.4 us (59%)
  Pallas kernels  19.2 us (25%)
  waiting for transfers between devices  9.95 us (13%)
  local copies, waits for them, and re-layouts  1.06 us (1%)
  between operations  0.81 us (1%)
    ppermute x6, starting transfers between devices, along_y(): lax.ppermute(block, 'y', [(i, (i + turn) % y_count) for i in range(y_coun...  21.4 us
    pallas_call x4, Pallas kernels, per_device(): pl.pallas_call(functools.partial(attend, turn, first, last), out_shape=(s...  14.1 us
    ppermute x1, starting transfers between devices, per_device(): other = lax.ppermute(other, names, route(-1, lambda a, c: (1 - a, c)))  6.83 us
    ppermute x1, waiting for transfers between devices, per_device(): other = lax.ppermute(other, names, route(1, lambda a, c: (1 - a, 1 - c)))  6.8 us
    all_to_all x1, starting transfers between devices, per_device(): message = lax.all_to_all(message, ('x_hi', 'x_lo'), 0, 0, tiled=True)  4.83 us
    all_to_all x1, starting transfers between devices, per_device(): dq = lax.all_to_all(dq, ('x_hi', 'x_lo'), 0, 0, tiled=True)  4.81 us
    ppermute x1, starting transfers between devices, per_device(): own = lax.ppermute(own, names, route(-1, lambda a, c: (a, c)))  3.68 us
    ppermute x1, starting transfers between devices, per_device(): other = lax.ppermute(other, names, route(1, lambda a, c: (1 - a, 1 - c)))  2.84 us
  transfers between devices with their start and end apart: 12, of which 4 were waited for; matrix products, arithmetic and copies ran while one was open for 0% of the time, Pallas kernels for 19%

profile of v3, /device:TPU:2, one launch (start us, length us, event | category | flops | bytes accessed | tf_op | source)
XLA Modules:
  0.0 77.5 jit_solution(6141122614690243262)
XLA Ops:
  0.6 1.0 %dynamic-slice_bitcast_fusion = (bf16[1,256,128]{2,1,0:T(8,128)(2,1)S(1)}, bf16[1,256,128]{2,1,0:T(8,128)(2,1)S(1)}, bf16[1,256,128]{2,1,0:T(8,128)(2,1)S(1)}, bf16[1,256,128]{2,1,0:T(8,128)(2,1)S(1)}) fusion(bf16[256,512]{1,0:T(8,128)(2,1)} %param.9, s32[]{:T(128)S(6)} %select_n.9, s32[]{:T(128)S(6)} %select_n.8, bf16[256,512]{1,0:T(8,128)(2,1)} %param.8), kind=kLoop, calls=%fused_computation.3 | loop fusion | bytes 524296 | tf_op jit(solution)/shard_map/stack | solution.py:207
  1.6 2.8 %collective-permute-start = (bf16[2,256,128]{2,1,0:T(8,128)(2,1)S(1)}, bf16[2,256,128]{2,1,0:T(8,128)(2,1)S(1)}, u32[]{:S(2)}, u32[]{:S(2)}) collective-permute-start(bf16[2,256,128]{2,1,0:T(8,128)(2,1)S(1)} %pad_maximum_fusion.1), channel_id=1, source_target_pairs={{0,67},{1,66},{2,69},{3,68},{4,71},{5,70},{6,73},{7,72},{8,75},{9,... | collective-permute-start | bytes 393224 | tf_op jit(solution)/shard_map/ppermute | solution.py:211
  4.5 2.0 %collective-permute-start.1 = (bf16[2,256,128]{2,1,0:T(8,128)(2,1)S(1)}, bf16[2,256,128]{2,1,0:T(8,128)(2,1)S(1)}, u32[]{:S(2)}, u32[]{:S(2)}) collective-permute-start(bf16[2,256,128]{2,1,0:T(8,128)(2,1)S(1)} %pad_maximum_fusion.2), channel_id=1, source_target_pairs={{0,2},{1,3},{2,4},{3,5},{4,6},{5,7},{6,8},{7,9},{8,10},{9,11},{10,... | collective-permute-start | bytes 393224 | tf_op jit(solution)/shard_map/ppermute | solution.py:212
  6.5 2.7 %pack_queries.1 = bf16[4,1056,128]{2,1,0:T(8,128)(2,1)} custom-call(bf16[256,1024]{1,0:T(8,128)(2,1)} %queries.1, bf16[256,1024]{1,0:T(8,128)(2,1)} %attn_out.1, bf16[256,1024]{1,0:T(8,128)(2,1)} %grad_out.1, f32[8,256]{1,0:T(8,128)} %row_total.1), custom_call_target="tpu_custom_call" | custom-call | tf_op jit(solution)/shard_map/pack_queries/pallas_call | solution.py:214
  9.2 0.0 copy-start
  9.3 6.8 %collective-permute-done = bf16[2,256,128]{2,1,0:T(8,128)(2,1)S(1)} collective-permute-done((bf16[2,256,128]{2,1,0:T(8,128)(2,1)S(1)}, bf16[2,256,128]{2,1,0:T(8,128)(2,1)S(1)}, u32[]{:S(2)}, u32[]{:S(2)}) %collective-permute-start) | collective-permute-done | bytes 131104 | tf_op jit(solution)/shard_map/ppermute | solution.py:211
  16.1 0.5 collective-permute-done.1
  16.5 4.8 %all-to-all-start = ((bf16[4,1056,128]{2,1,0:T(8,128)(2,1)}), bf16[4,1056,128]{2,1,0:T(8,128)(2,1)S(1)}, u32[]{:S(2)}, u32[]{:S(2)}) async-start(bf16[4,1056,128]{2,1,0:T(8,128)(2,1)} %pack_queries.1), calls=%async_computation | async-start | bytes 2162688 | tf_op jit(solution)/shard_map/all_to_all | solution.py:230
  21.4 3.5 %collective-permute-start.4 = (bf16[2,2,256,128]{3,2,1,0:T(8,128)(2,1)S(1)}, bf16[2,2,256,128]{3,2,1,0:T(8,128)(2,1)S(1)}, u32[]{:S(2)}, u32[]{:S(2)}) collective-permute-start(bf16[2,2,256,128]{3,2,1,0:T(8,128)(2,1)S(1)} %pad_maximum_fusion.refs_3_), channel_id=1, source_target_pairs={{0,128},{128,256},{256,384},{384,0},{1,129},{129,257},{257,385},{3... | collective-permute-start | bytes 786440 | tf_op jit(solution)/shard_map/ppermute | solution.py:203
  24.9 3.6 %collective-permute-start.3 = (bf16[2,2,256,128]{3,2,1,0:T(8,128)(2,1)S(1)}, bf16[2,2,256,128]{3,2,1,0:T(8,128)(2,1)S(1)}, u32[]{:S(2)}, u32[]{:S(2)}) collective-permute-start(bf16[2,2,256,128]{3,2,1,0:T(8,128)(2,1)S(1)} %pad_maximum_fusion.refs_3_), channel_id=1, source_target_pairs={{0,384},{128,0},{256,128},{384,256},{1,385},{129,1},{257,129},{385... | collective-permute-start | bytes 786440 | tf_op jit(solution)/shard_map/ppermute | solution.py:203
  28.5 3.9 %collective-permute-start.2 = (bf16[2,2,256,128]{3,2,1,0:T(8,128)(2,1)S(1)}, bf16[2,2,256,128]{3,2,1,0:T(8,128)(2,1)S(1)}, u32[]{:S(2)}, u32[]{:S(2)}) collective-permute-start(bf16[2,2,256,128]{3,2,1,0:T(8,128)(2,1)S(1)} %pad_maximum_fusion.refs_3_), channel_id=1, source_target_pairs={{0,256},{128,384},{256,0},{384,128},{1,257},{129,385},{257,1},{385... | collective-permute-start | bytes 786440 | tf_op jit(solution)/shard_map/ppermute | solution.py:203
  32.4 0.1 stack.46.refs_0_.where
  32.4 1.1 %collective-permute-done.4.refs_3_ = bf16[2,2,256,128]{3,2,1,0:T(8,128)(2,1)S(1)} collective-permute-done((bf16[2,2,256,128]{3,2,1,0:T(8,128)(2,1)S(1)}, bf16[2,2,256,128]{3,2,1,0:T(8,128)(2,1)S(1)}, u32[]{:S(2)}, u32[]{:S(2)}) %collective-permute-start.4) | collective-permute-done | bytes 262176 | tf_op jit(solution)/shard_map/ppermute | solution.py:203
  33.6 0.0 all-to-all-done.refs_2_
  33.6 0.0 copy-done
  33.6 3.3 %attend_1.1 = (f32[128,2048]{1,0:T(8,128)S(1)}, bf16[2,2,256,128]{3,2,1,0:T(8,128)(2,1)S(1)}) custom-call(s32[5]{0:T(128)S(1)} %stack.46.refs_0_.where, s32[512]{0:T(512)S(1)} %copy-done, bf16[4,1056,128]{2,1,0:T(8,128)(2,1)S(1)} %all-to-all-done.refs_2_, bf16[2,2,256,128]{3,2,1,0:T(8,128)(2,1)S(1)} %collective-permute-done.4.refs_3_), custom_call_target="tpu_custom_call" | custom-call | tf_op jit(solution)/shard_map/attend_1/pallas_call | solution.py:239
  36.9 0.0 collective-permute-done.3.refs_3_
  36.9 3.3 %attend_3.1 = (f32[128,2048]{1,0:T(8,128)S(1)}, bf16[2,2,256,128]{3,2,1,0:T(8,128)(2,1)S(1)}) custom-call(s32[5]{0:T(128)S(1)} %stack.46.refs_0_.where, s32[512]{0:T(512)S(1)} %copy-done, bf16[4,1056,128]{2,1,0:T(8,128)(2,1)S(1)} %all-to-all-done.refs_2_, bf16[2,2,256,128]{3,2,1,0:T(8,128)(2,1)S(1)} %collective-permute-done.3.refs_3_, ...), custom_call_target="tpu_custom_call" | custom-call | tf_op jit(solution)/shard_map/attend_3/pallas_call | solution.py:239
  40.3 0.0 collective-permute-done.2.refs_3_
  40.3 3.3 %attend_2.1 = (f32[128,2048]{1,0:T(8,128)S(1)}, bf16[2,2,256,128]{3,2,1,0:T(8,128)(2,1)S(1)}) custom-call(s32[5]{0:T(128)S(1)} %stack.46.refs_0_.where, s32[512]{0:T(512)S(1)} %copy-done, bf16[4,1056,128]{2,1,0:T(8,128)(2,1)S(1)} %all-to-all-done.refs_2_, bf16[2,2,256,128]{3,2,1,0:T(8,128)(2,1)S(1)} %collective-permute-done.2.refs_3_, ...), custom_call_target="tpu_custom_call" | custom-call | tf_op jit(solution)/shard_map/attend_2/pallas_call | solution.py:239
  43.6 3.4 %collective-permute-start.7 = (bf16[2,2,256,128]{3,2,1,0:T(8,128)(2,1)S(1)}, bf16[2,2,256,128]{3,2,1,0:T(8,128)(2,1)S(1)}, u32[]{:S(2)}, u32[]{:S(2)}) collective-permute-start(bf16[2,2,256,128]{3,2,1,0:T(8,128)(2,1)S(1)} %get-tuple-element.27), channel_id=1, source_target_pairs={{0,256},{128,384},{256,0},{384,128},{1,257},{129,385},{257,1},{385... | collective-permute-start | bytes 786440 | tf_op jit(solution)/shard_map/ppermute | solution.py:203
  47.0 2.6 %collective-permute-start.6 = (bf16[2,2,256,128]{3,2,1,0:T(8,128)(2,1)S(1)}, bf16[2,2,256,128]{3,2,1,0:T(8,128)(2,1)S(1)}, u32[]{:S(2)}, u32[]{:S(2)}) collective-permute-start(bf16[2,2,256,128]{3,2,1,0:T(8,128)(2,1)S(1)} %get-tuple-element.26), channel_id=1, source_target_pairs={{0,128},{128,256},{256,384},{384,0},{1,129},{129,257},{257,385},{3... | collective-permute-start | bytes 786440 | tf_op jit(solution)/shard_map/ppermute | solution.py:203
  49.6 4.5 %collective-permute-start.5 = (bf16[2,2,256,128]{3,2,1,0:T(8,128)(2,1)S(1)}, bf16[2,2,256,128]{3,2,1,0:T(8,128)(2,1)S(1)}, u32[]{:S(2)}, u32[]{:S(2)}) collective-permute-start(bf16[2,2,256,128]{3,2,1,0:T(8,128)(2,1)S(1)} %get-tuple-element.25), channel_id=1, source_target_pairs={{0,384},{128,0},{256,128},{384,256},{1,385},{129,1},{257,129},{385... | collective-permute-start | bytes 786440 | tf_op jit(solution)/shard_map/ppermute | solution.py:203
  54.1 4.1 %attend_0.1 = (bf16[4,128,512]{2,1,0:T(8,128)(2,1)}, f32[2,2,256,128]{3,2,1,0:T(8,128)S(1)}) custom-call(s32[5]{0:T(128)S(1)} %stack.46.refs_0_.where, s32[512]{0:T(512)S(1)} %copy-done, bf16[4,1056,128]{2,1,0:T(8,128)(2,1)S(1)} %all-to-all-done.refs_2_, bf16[2,2,256,128]{3,2,1,0:T(8,128)(2,1)S(1)} %pad_maximum_fusion.refs_3_, ...), custom_call_target="tpu_custom_call" | custom-call | tf_op jit(solution)/shard_map/attend_0/pallas_call | solution.py:239
  58.2 4.8 %all-to-all-start.1 = ((bf16[4,128,512]{2,1,0:T(8,128)(2,1)}), bf16[4,128,512]{2,1,0:T(8,128)(2,1)S(1)}, u32[]{:S(2)}, u32[]{:S(2)}) async-start(bf16[4,128,512]{2,1,0:T(8,128)(2,1)} %get-tuple-element.24), calls=%async_computation.1 | async-start | bytes 1048576 | tf_op jit(solution)/shard_map/all_to_all | solution.py:252
  63.1 0.0 collective-permute-done.7.c
  63.1 0.0 collective-permute-done.6.b
  63.1 0.0 collective-permute-done.5.a
  63.1 0.1 add_partials.1
  63.2 6.8 %collective-permute-start.8 = (bf16[2,256,128]{2,1,0:T(8,128)(2,1)S(1)}, bf16[2,256,128]{2,1,0:T(8,128)(2,1)S(1)}, u32[]{:S(2)}, u32[]{:S(2)}) collective-permute-start(bf16[2,256,128]{2,1,0:T(8,128)(2,1)S(1)} %get-tuple-element.29), channel_id=1, source_target_pairs={{0,126},{1,127},{2,64},{3,65},{4,66},{5,67},{6,68},{7,69},{8,70},{... | collective-permute-start | bytes 393224 | tf_op jit(solution)/shard_map/ppermute | solution.py:261
  70.0 3.7 %collective-permute-start.9 = (bf16[2,256,128]{2,1,0:T(8,128)(2,1)S(1)}, bf16[2,256,128]{2,1,0:T(8,128)(2,1)S(1)}, u32[]{:S(2)}, u32[]{:S(2)}) collective-permute-start(bf16[2,256,128]{2,1,0:T(8,128)(2,1)S(1)} %get-tuple-element.30), channel_id=1, source_target_pairs={{0,62},{1,63},{2,0},{3,1},{4,2},{5,3},{6,4},{7,5},{8,6},{9,7},{10,... | collective-permute-start | bytes 393224 | tf_op jit(solution)/shard_map/ppermute | solution.py:262
  73.7 0.0 all-to-all-done.1.dq
  73.7 1.0 %unpack_queries.1 = bf16[256,1024]{1,0:T(8,128)(2,1)} custom-call(bf16[4,128,512]{2,1,0:T(8,128)(2,1)S(1)} %all-to-all-done.1.dq), custom_call_target="tpu_custom_call" | custom-call | tf_op jit(solution)/shard_map/unpack_queries/pallas_call | solution.py:263
  74.7 0.0 collective-permute-done.8.other
  74.7 1.5 %collective-permute-done.9.own = bf16[2,256,128]{2,1,0:T(8,128)(2,1)S(1)} collective-permute-done((bf16[2,256,128]{2,1,0:T(8,128)(2,1)S(1)}, bf16[2,256,128]{2,1,0:T(8,128)(2,1)S(1)}, u32[]{:S(2)}, u32[]{:S(2)}) %collective-permute-start.9) | collective-permute-done | bytes 131104 | tf_op jit(solution)/shard_map/ppermute | solution.py:262
  76.2 1.3 %unpack_kv.1 = (bf16[256,256]{1,0:T(8,128)(2,1)}, bf16[256,256]{1,0:T(8,128)(2,1)}) custom-call(s32[5]{0:T(128)S(1)} %stack.46.refs_0_.where, bf16[2,256,128]{2,1,0:T(8,128)(2,1)S(1)} %collective-permute-done.8.other, bf16[2,256,128]{2,1,0:T(8,128)(2,1)S(1)} %collective-permute-done.9.own), custom_call_target="tpu_custom_call" | custom-call | tf_op jit(solution)/shard_map/unpack_kv/pallas_call | solution.py:271
  (3 shorter events, 0.1 us)
Async XLA Ops:
  1.6 14.4 %collective-permute-start = (bf16[2,256,128]{2,1,0:T(8,128)(2,1)S(1)}, bf16[2,256,128]{2,1,0:T(8,128)(2,1)S(1)}, u32[]{:S(2)}, u32[]{:S(2)}) collective-permute-start(bf16[2,256,128]{2,1,0:T(8,128)(2,1)S(1)} %pad_maximum_fusion.1), channel_id=1, source_target_pairs={{0,67},{1,66},{2,69},{3,68},{4,71},{5,70},{6,73},{7,72},{8,75},{9,... | collective-permute-start | bytes 393224 | tf_op jit(solution)/shard_map/ppermute | solution.py:211
  4.5 12.0 %collective-permute-start.1 = (bf16[2,256,128]{2,1,0:T(8,128)(2,1)S(1)}, bf16[2,256,128]{2,1,0:T(8,128)(2,1)S(1)}, u32[]{:S(2)}, u32[]{:S(2)}) collective-permute-start(bf16[2,256,128]{2,1,0:T(8,128)(2,1)S(1)} %pad_maximum_fusion.2), channel_id=1, source_target_pairs={{0,2},{1,3},{2,4},{3,5},{4,6},{5,7},{6,8},{7,9},{8,10},{9,11},{10,... | collective-permute-start | bytes 393224 | tf_op jit(solution)/shard_map/ppermute | solution.py:212
  9.2 24.3 %copy-start = (s32[512]{0:T(512)S(1)}, s32[512]{0:T(512)}, u32[]{:S(2)}) copy-start(s32[512]{0:T(512)} %refs_1_.7) | copy-start | bytes 6148
  16.5 17.0 %all-to-all-start = ((bf16[4,1056,128]{2,1,0:T(8,128)(2,1)}), bf16[4,1056,128]{2,1,0:T(8,128)(2,1)S(1)}, u32[]{:S(2)}, u32[]{:S(2)}) async-start(bf16[4,1056,128]{2,1,0:T(8,128)(2,1)} %pack_queries.1), calls=%async_computation | async-start | bytes 2162688 | tf_op jit(solution)/shard_map/all_to_all | solution.py:230
  21.4 12.2 %collective-permute-start.4 = (bf16[2,2,256,128]{3,2,1,0:T(8,128)(2,1)S(1)}, bf16[2,2,256,128]{3,2,1,0:T(8,128)(2,1)S(1)}, u32[]{:S(2)}, u32[]{:S(2)}) collective-permute-start(bf16[2,2,256,128]{3,2,1,0:T(8,128)(2,1)S(1)} %pad_maximum_fusion.refs_3_), channel_id=1, source_target_pairs={{0,128},{128,256},{256,384},{384,0},{1,129},{129,257},{257,385},{3... | collective-permute-start | bytes 786440 | tf_op jit(solution)/shard_map/ppermute | solution.py:203
  24.9 12.0 %collective-permute-start.3 = (bf16[2,2,256,128]{3,2,1,0:T(8,128)(2,1)S(1)}, bf16[2,2,256,128]{3,2,1,0:T(8,128)(2,1)S(1)}, u32[]{:S(2)}, u32[]{:S(2)}) collective-permute-start(bf16[2,2,256,128]{3,2,1,0:T(8,128)(2,1)S(1)} %pad_maximum_fusion.refs_3_), channel_id=1, source_target_pairs={{0,384},{128,0},{256,128},{384,256},{1,385},{129,1},{257,129},{385... | collective-permute-start | bytes 786440 | tf_op jit(solution)/shard_map/ppermute | solution.py:203
  28.5 11.8 %collective-permute-start.2 = (bf16[2,2,256,128]{3,2,1,0:T(8,128)(2,1)S(1)}, bf16[2,2,256,128]{3,2,1,0:T(8,128)(2,1)S(1)}, u32[]{:S(2)}, u32[]{:S(2)}) collective-permute-start(bf16[2,2,256,128]{3,2,1,0:T(8,128)(2,1)S(1)} %pad_maximum_fusion.refs_3_), channel_id=1, source_target_pairs={{0,256},{128,384},{256,0},{384,128},{1,257},{129,385},{257,1},{385... | collective-permute-start | bytes 786440 | tf_op jit(solution)/shard_map/ppermute | solution.py:203
  43.6 19.4 %collective-permute-start.7 = (bf16[2,2,256,128]{3,2,1,0:T(8,128)(2,1)S(1)}, bf16[2,2,256,128]{3,2,1,0:T(8,128)(2,1)S(1)}, u32[]{:S(2)}, u32[]{:S(2)}) collective-permute-start(bf16[2,2,256,128]{3,2,1,0:T(8,128)(2,1)S(1)} %get-tuple-element.27), channel_id=1, source_target_pairs={{0,256},{128,384},{256,0},{384,128},{1,257},{129,385},{257,1},{385... | collective-permute-start | bytes 786440 | tf_op jit(solution)/shard_map/ppermute | solution.py:203
  47.0 16.0 %collective-permute-start.6 = (bf16[2,2,256,128]{3,2,1,0:T(8,128)(2,1)S(1)}, bf16[2,2,256,128]{3,2,1,0:T(8,128)(2,1)S(1)}, u32[]{:S(2)}, u32[]{:S(2)}) collective-permute-start(bf16[2,2,256,128]{3,2,1,0:T(8,128)(2,1)S(1)} %get-tuple-element.26), channel_id=1, source_target_pairs={{0,128},{128,256},{256,384},{384,0},{1,129},{129,257},{257,385},{3... | collective-permute-start | bytes 786440 | tf_op jit(solution)/shard_map/ppermute | solution.py:203
  49.6 13.5 %collective-permute-start.5 = (bf16[2,2,256,128]{3,2,1,0:T(8,128)(2,1)S(1)}, bf16[2,2,256,128]{3,2,1,0:T(8,128)(2,1)S(1)}, u32[]{:S(2)}, u32[]{:S(2)}) collective-permute-start(bf16[2,2,256,128]{3,2,1,0:T(8,128)(2,1)S(1)} %get-tuple-element.25), channel_id=1, source_target_pairs={{0,384},{128,0},{256,128},{384,256},{1,385},{129,1},{257,129},{385... | collective-permute-start | bytes 786440 | tf_op jit(solution)/shard_map/ppermute | solution.py:203
  58.2 15.5 %all-to-all-start.1 = ((bf16[4,128,512]{2,1,0:T(8,128)(2,1)}), bf16[4,128,512]{2,1,0:T(8,128)(2,1)S(1)}, u32[]{:S(2)}, u32[]{:S(2)}) async-start(bf16[4,128,512]{2,1,0:T(8,128)(2,1)} %get-tuple-element.24), calls=%async_computation.1 | async-start | bytes 1048576 | tf_op jit(solution)/shard_map/all_to_all | solution.py:252
  63.2 11.5 %collective-permute-start.8 = (bf16[2,256,128]{2,1,0:T(8,128)(2,1)S(1)}, bf16[2,256,128]{2,1,0:T(8,128)(2,1)S(1)}, u32[]{:S(2)}, u32[]{:S(2)}) collective-permute-start(bf16[2,256,128]{2,1,0:T(8,128)(2,1)S(1)} %get-tuple-element.29), channel_id=1, source_target_pairs={{0,126},{1,127},{2,64},{3,65},{4,66},{5,67},{6,68},{7,69},{8,70},{... | collective-permute-start | bytes 393224 | tf_op jit(solution)/shard_map/ppermute | solution.py:261
  70.0 6.2 %collective-permute-start.9 = (bf16[2,256,128]{2,1,0:T(8,128)(2,1)S(1)}, bf16[2,256,128]{2,1,0:T(8,128)(2,1)S(1)}, u32[]{:S(2)}, u32[]{:S(2)}) collective-permute-start(bf16[2,256,128]{2,1,0:T(8,128)(2,1)S(1)} %get-tuple-element.30), channel_id=1, source_target_pairs={{0,62},{1,63},{2,0},{3,1},{4,2},{5,3},{6,4},{7,5},{8,6},{9,7},{10,... | collective-permute-start | bytes 393224 | tf_op jit(solution)/shard_map/ppermute | solution.py:262

commit v4 on v3

--- a/solution.py
+++ b/solution.py
@@ -25,7 +25,7 @@
 SMEM = pl.BlockSpec(memory_space=pltpu.SMEM)
 f32 = jnp.float32
 bf16 = jnp.bfloat16
-FREE = pl.CostEstimate(flops=0, bytes_accessed=0, transcendentals=0)
+LONG = pl.CostEstimate(flops=2 * 10**10, bytes_accessed=0, transcendentals=0)
 LONG = pl.CostEstimate(flops=10**10, bytes_accessed=0, transcendentals=0)
 WIDE = pltpu.CompilerParams(vmem_limit_bytes=60 * 2**20)
 PARAMS = pltpu.CompilerParams(vmem_limit_bytes=24 * 2**20)
@@ -97,44 +97,38 @@
 
 
 def attend(turn, first, last, *refs):
-    where, ids, message, kv = refs[:4]
-    dq_in = None if first else refs[4]
-    dq_out, dkv = refs[-2:]
-    y, x_hi, o, outer = where[0], where[1], where[2], where[4]
-    key_y = (y - turn) & 3
-    key_o = jnp.where(o == 0, outer - 1, o - 1)
+    hide, message, kv = refs[:3]
+    dq_in = None if first else refs[3]
+    dq_out, dkv, rows = refs[-3:]
     k = kv[:, 0].reshape(2 * TOK, HD)
     v = kv[:, 1].reshape(2 * TOK, HD)
     kt = k.T
-    key_blocks = []
-    for j in range(2):
-        key_x = 1 - x_hi if j == 0 else x_hi
-        for half in range(2):
-            key_blocks.append(ids[((key_y * 2 + key_x) * outer + key_o) * 2 + half])
-    dk = jnp.zeros((2 * TOK, HD), f32)
-    dv = jnp.zeros((2 * TOK, HD), f32)
     for x in range(4):
         table = message[x, 2 * ROWS : 2 * ROWS + AUX, :].astype(f32)
         table = table[0:8] + table[8:16] + table[16:24]
-        shift = jnp.concatenate([table[i : i + 1] for i in range(4)], axis=1)
-        delta = jnp.concatenate([table[i : i + 1] for i in range(4, 8)], axis=1)
-        query_blocks = [ids[((y * 2 + x // 2) * outer + o) * 2 + half] for half in range(2)]
+        for c in range(4):
+            lanes = slice(c * HALF, (c + 1) * HALF)
+            for i in range(4):
+                rows[i, x : x + 1, lanes] = table[c : c + 1] + hide[turn, i, x : x + 1, lanes]
+            rows[4, x : x + 1, lanes] = table[4 + c : 5 + c]
+    dk = dv = None
+    for x in range(4):
         q = message[x, 0:ROWS, :]
         g = message[x, ROWS : 2 * ROWS, :]
         scores = dot(k, q, NT)
         dprob = dot(v, g, NT)
-        prob = []
-        for i in range(4):
-            hide = [
-                jnp.full((1, TOK), jnp.where(key_blocks[i] < query_blocks[half], 0.0, HIDDEN).astype(f32))
-                for half in range(2)
-            ]
-            row = shift + jnp.concatenate(hide, axis=1)
-            prob.append(jnp.exp2(scores[i * HALF : (i + 1) * HALF] * EXP2_SCALE - row))
-        prob = jnp.concatenate(prob, axis=0)
-        ds = (prob * (dprob - delta)).astype(bf16)
-        dv = dv + dot(prob.astype(bf16), g, NN)
-        dk = dk + dot(ds, q, NN)
+        prob = jnp.concatenate(
+            [
+                jnp.exp2(scores[i * HALF : (i + 1) * HALF] * EXP2_SCALE - rows[i, x : x + 1, :])
+                for i in range(4)
+            ],
+            axis=0,
+        )
+        ds = (prob * (dprob - rows[4, x : x + 1, :])).astype(bf16)
+        dv_part = dot(prob.astype(bf16), g, NN)
+        dk_part = dot(ds, q, NN)
+        dv = dv_part if dv is None else dv + dv_part
+        dk = dk_part if dk is None else dk + dk_part
         at = x * ROWS
         dq = dot(kt, ds, NN)
         if not first:
@@ -147,8 +141,8 @@
     dkv[:, 1] = dv.astype(dkv.dtype).reshape(2, TOK, HD)
 
 
-def add_partials(a, b, c, mine, other, own):
-    for j, out in ((0, other), (1, own)):
+def add_partials(mine, a, b, c, other, own):
+    for j, out in ((0, own), (1, other)):
         for i in range(2):
             out[i] = (a[j, i].astype(f32) + b[j, i].astype(f32) + c[j, i].astype(f32) + mine[j, i]).astype(bf16)
 
@@ -163,17 +157,11 @@
                 grad_queries[half * HALF : (half + 1) * HALF, h * HD : (h + 1) * HD] = part[at : at + HALF]
 
 
-def unpack_kv(where, other, own, grad_keys, grad_values, sems):
-    mine = pl.ds(pl.multiple_of(where[1] * HD, HD), HD)
-    rest = pl.ds(pl.multiple_of((1 - where[1]) * HD, HD), HD)
-    copies = []
+def unpack_kv(swap, other, own, grad_keys, grad_values):
+    second = swap[0:1, :] > 0
     for i, out in ((0, grad_keys), (1, grad_values)):
-        for columns, part in ((mine, own), (rest, other)):
-            copies.append(pltpu.make_async_copy(part.at[i], out.at[:, columns], sems.at[len(copies)]))
-    for copy in copies:
-        copy.start()
-    for copy in copies:
-        copy.wait()
+        out[:, 0:HD] = jnp.where(second, other[i], own[i])
+        out[:, HD : 2 * HD] = jnp.where(second, own[i], other[i])
 
 
 def shape(*dims):
@@ -187,7 +175,6 @@
     x_hi = lax.axis_index("x_hi")
     o = lax.axis_index("outer")
     x_lo = lax.axis_index("x_lo")
-    where = jnp.stack([y, x_hi, o, x_lo, jnp.int32(outer)]).astype(jnp.int32)
     names = ("x_hi", "outer", "x_lo")
 
     def route(step, turn):
@@ -208,8 +195,8 @@
 
     other = columns(2 * (1 - x_lo) + (1 - x_hi))
     own = columns(2 * x_lo + x_hi)
+    other, row_total = lax.optimization_barrier((other, row_total))
     other = lax.ppermute(other, names, route(1, lambda a, c: (1 - a, 1 - c)))
-    own = lax.ppermute(own, names, route(1, lambda a, c: (a, c)))
 
     message = pl.pallas_call(
         pack_queries,
@@ -226,29 +213,40 @@
         compiler_params=WIDE,
         name="pack_queries",
     )(queries, attn_out, grad_out, row_total)
-    other, own, message = lax.optimization_barrier((other, own, message))
+    own, other = lax.optimization_barrier((own, other))
+    own = lax.ppermute(own, names, route(1, lambda a, c: (a, c)))
     message = lax.all_to_all(message, ("x_hi", "x_lo"), 0, 0, tiled=True)
 
-    kv = jnp.stack([other, own])
+    kv = jnp.stack([own, other])
+    stored = block_ids.reshape(y_count, 2, outer, 2)
+    query_ids = lax.dynamic_slice(stored, (y, 0, o, 0), (1, 2, 1, 2)).reshape(2, 2)
+    key_ids = lax.dynamic_slice(stored, (0, 0, (o + outer - 1) % outer, 0), (y_count, 2, 1, 2)).reshape(y_count, 2, 2)
+    key_ids = jnp.concatenate([key_ids[::-1]] * 2)
+    key_ids = lax.dynamic_slice(key_ids, (y_count - 1 - y, 0, 0), (y_count, 2, 2))
+    key_ids = jnp.where(x_hi == 0, key_ids, key_ids[:, ::-1]).reshape(y_count, 4, 1, 1)
+    visible = key_ids < jnp.repeat(query_ids, 2, axis=0).reshape(1, 1, 4, 2)
+    hide = jnp.repeat(jnp.where(visible, f32(0.0), f32(HIDDEN)), TOK, axis=3)
+
     turns = (1, 3, 2)
-    blocks = [along_y(kv, turn) for turn in turns] + [kv]
+    blocks = [kv] + [along_y(kv, turn) for turn in turns]
     dq = None
     parts = []
-    for turn, block in zip(turns + (0,), blocks):
-        first, last = turn == turns[0], turn == 0
+    for turn, block in zip((0,) + turns, blocks):
+        first, last = turn == 0, turn == turns[-1]
         dq, dkv = pl.pallas_call(
             functools.partial(attend, turn, first, last),
             out_shape=(
                 shape(4, HD, ROWS) if last else jax.ShapeDtypeStruct((HD, 4 * ROWS), f32),
-                jax.ShapeDtypeStruct((2, 2, TOK, HD), f32 if last else bf16),
+                jax.ShapeDtypeStruct((2, 2, TOK, HD), f32 if first else bf16),
             ),
-            in_specs=[SMEM, SMEM] + [VMEM] * (2 if first else 3),
+            in_specs=[VMEM] * (3 if first else 4),
             out_specs=(VMEM, VMEM),
             compiler_params=PARAMS,
-            cost_estimate=FREE,
+            scratch_shapes=[pltpu.VMEM((5, 4, ROWS), f32)],
+            cost_estimate=LONG,
             name="attend_%d" % turn,
-        )(where, block_ids, message, block, *(() if first else (dq,)))
-        parts.append(dkv if last else along_y(dkv, -turn))
+        )(hide, message, block, *(() if first else (dq,)))
+        parts.append(dkv if first else along_y(dkv, -turn))
     dq = lax.all_to_all(dq, ("x_hi", "x_lo"), 0, 0, tiled=True)
     other, own = pl.pallas_call(
         add_partials,
@@ -271,12 +269,11 @@
     grad_keys, grad_values = pl.pallas_call(
         unpack_kv,
         out_shape=(shape(TOK, 2 * HD), shape(TOK, 2 * HD)),
-        in_specs=[SMEM, VMEM, VMEM],
-        out_specs=(HBM, HBM),
-        scratch_shapes=[pltpu.SemaphoreType.DMA((4,))],
+        in_specs=[VMEM] * 3,
+        out_specs=(VMEM, VMEM),
         compiler_params=PARAMS,
         name="unpack_kv",
-    )(where, other, own)
+    )(jnp.full((8, HD), x_hi, jnp.int32), other, own)
     return grad_queries, grad_keys, grad_values
 
 

time: 78 us -> 73.9 us (0.947)
  the two profiles are of different devices: /device:TPU:2 before, /device:TPU:1 now
where the time goes in v4:
time: 73.9 us; the launch traced here: 72.7 us
  starting transfers between devices  44.6 us (60%)
  Pallas kernels  16.5 us (22%)
  waiting for transfers between devices  8.8 us (12%)
  local copies, waits for them, and re-layouts  1.68 us (2%)
  between operations  0.93 us (1%)
    ppermute x6, starting transfers between devices, along_y(): lax.ppermute(block, 'y', [(i, (i + turn) % y_count) for i in range(y_coun...  21.3 us
    pallas_call x4, Pallas kernels, per_device(): pl.pallas_call(functools.partial(attend, turn, first, last), out_shape=(s...  11.9 us
    ppermute x1, starting transfers between devices, per_device(): other = lax.ppermute(other, names, route(-1, lambda a, c: (1 - a, c)))  8.59 us
    ppermute x1, starting transfers between devices, per_device(): other = lax.ppermute(other, names, route(1, lambda a, c: (1 - a, 1 - c)))  7.13 us
    ppermute x1, waiting for transfers between devices, per_device(): own = lax.ppermute(own, names, route(1, lambda a, c: (a, c)))  3.63 us
    all_to_all x1, starting transfers between devices, per_device(): message = lax.all_to_all(message, ('x_hi', 'x_lo'), 0, 0, tiled=True)  3.53 us
    all_to_all x1, starting transfers between devices, per_device(): dq = lax.all_to_all(dq, ('x_hi', 'x_lo'), 0, 0, tiled=True)  3.48 us
    ppermute x1, waiting for transfers between devices, per_device(): own = lax.ppermute(own, names, route(-1, lambda a, c: (a, c)))  2.77 us
  transfers between devices with their start and end apart: 12, of which 4 were waited for; matrix products, arithmetic and copies ran while one was open for 1% of the time, Pallas kernels for 17%

profile of v4, /device:TPU:1, one launch (start us, length us, event | category | flops | bytes accessed | tf_op | source)
XLA Modules:
  0.0 72.7 jit_solution(12074315939481085358)
XLA Ops:
  0.6 1.0 %dynamic-slice_bitcast_fusion = (bf16[1,256,128]{2,1,0:T(8,128)(2,1)S(1)}, bf16[1,256,128]{2,1,0:T(8,128)(2,1)S(1)}, bf16[1,256,128]{2,1,0:T(8,128)(2,1)S(1)}, bf16[1,256,128]{2,1,0:T(8,128)(2,1)S(1)}) fusion(bf16[256,512]{1,0:T(8,128)(2,1)} %param.9, s32[]{:T(128)S(6)} %select_n.48, s32[]{:T(128)S(6)} %select_n.47, bf16[256,512]{1,0:T(8,128)(2,1)} %param.8), kind=kLoop, calls=%fused_computation.3 | loop fusion | bytes 524296 | tf_op jit(solution)/shard_map/stack | solution.py:194
  1.6 7.1 %collective-permute-start = (bf16[2,256,128]{2,1,0:T(8,128)(2,1)S(1)}, bf16[2,256,128]{2,1,0:T(8,128)(2,1)S(1)}, u32[]{:S(2)}, u32[]{:S(2)}) collective-permute-start(bf16[2,256,128]{2,1,0:T(8,128)(2,1)S(1)} %pad_maximum_fusion.1), channel_id=1, source_target_pairs={{0,67},{1,66},{2,69},{3,68},{4,71},{5,70},{6,73},{7,72},{8,75},{9,... | collective-permute-start | bytes 393224 | tf_op jit(solution)/shard_map/ppermute | solution.py:199
  8.8 2.7 %pack_queries.1 = bf16[4,1056,128]{2,1,0:T(8,128)(2,1)} custom-call(bf16[256,1024]{1,0:T(8,128)(2,1)} %queries.1, bf16[256,1024]{1,0:T(8,128)(2,1)} %attn_out.1, bf16[256,1024]{1,0:T(8,128)(2,1)} %grad_out.1, f32[8,256]{1,0:T(8,128)} %row_total), custom_call_target="tpu_custom_call" | custom-call | tf_op jit(solution)/shard_map/pack_queries/pallas_call | solution.py:201
  11.5 0.0 copy-start
  11.5 3.5 %all-to-all-start = ((bf16[4,1056,128]{2,1,0:T(8,128)(2,1)}), bf16[4,1056,128]{2,1,0:T(8,128)(2,1)S(1)}, u32[]{:S(2)}, u32[]{:S(2)}) async-start(bf16[4,1056,128]{2,1,0:T(8,128)(2,1)} %pack_queries.1), calls=%async_computation | async-start | bytes 2162688 | tf_op jit(solution)/shard_map/all_to_all | solution.py:218
  15.0 0.0 copy-done
  15.0 0.1 reshape.21
  15.2 0.1 copy.14
  15.3 0.1 rev.6
  15.4 0.1 dynamic-slice_add_fusion
  15.5 0.1 copy.15
  15.6 0.0 collective-permute-done
  15.6 0.0 collective-permute-start.1
  15.7 0.1 compare_select_fusion
  15.8 0.1 broadcast_in_dim.20
  15.9 0.1 reshape.24.refs_0_
  16.0 3.6 %collective-permute-done.1 = bf16[2,256,128]{2,1,0:T(8,128)(2,1)S(1)} collective-permute-done((bf16[2,256,128]{2,1,0:T(8,128)(2,1)S(1)}, bf16[2,256,128]{2,1,0:T(8,128)(2,1)S(1)}, u32[]{:S(2)}, u32[]{:S(2)}) %collective-permute-start.1) | collective-permute-done | bytes 131104 | tf_op jit(solution)/shard_map/ppermute | solution.py:217
  19.7 3.2 %collective-permute-start.4 = (bf16[2,2,256,128]{3,2,1,0:T(8,128)(2,1)S(1)}, bf16[2,2,256,128]{3,2,1,0:T(8,128)(2,1)S(1)}, u32[]{:S(2)}, u32[]{:S(2)}) collective-permute-start(bf16[2,2,256,128]{3,2,1,0:T(8,128)(2,1)S(1)} %pad_maximum_fusion.refs_2_), channel_id=1, source_target_pairs={{0,128},{128,256},{256,384},{384,0},{1,129},{129,257},{257,385},{3... | collective-permute-start | bytes 786440 | tf_op jit(solution)/shard_map/ppermute | solution.py:190
  22.9 3.4 %collective-permute-start.3 = (bf16[2,2,256,128]{3,2,1,0:T(8,128)(2,1)S(1)}, bf16[2,2,256,128]{3,2,1,0:T(8,128)(2,1)S(1)}, u32[]{:S(2)}, u32[]{:S(2)}) collective-permute-start(bf16[2,2,256,128]{3,2,1,0:T(8,128)(2,1)S(1)} %pad_maximum_fusion.refs_2_), channel_id=1, source_target_pairs={{0,384},{128,0},{256,128},{384,256},{1,385},{129,1},{257,129},{385... | collective-permute-start | bytes 786440 | tf_op jit(solution)/shard_map/ppermute | solution.py:190
  26.3 3.5 %collective-permute-start.2 = (bf16[2,2,256,128]{3,2,1,0:T(8,128)(2,1)S(1)}, bf16[2,2,256,128]{3,2,1,0:T(8,128)(2,1)S(1)}, u32[]{:S(2)}, u32[]{:S(2)}) collective-permute-start(bf16[2,2,256,128]{3,2,1,0:T(8,128)(2,1)S(1)} %pad_maximum_fusion.refs_2_), channel_id=1, source_target_pairs={{0,256},{128,384},{256,0},{384,128},{1,257},{129,385},{257,1},{385... | collective-permute-start | bytes 786440 | tf_op jit(solution)/shard_map/ppermute | solution.py:190
  29.9 0.0 all-to-all-done.refs_1_
  29.9 2.8 %attend_0.1 = (f32[128,2048]{1,0:T(8,128)S(1)}, f32[2,2,256,128]{3,2,1,0:T(8,128)S(1)}) custom-call(f32[4,4,4,512]{3,2,1,0:T(4,128)S(1)} %reshape.24.refs_0_, bf16[4,1056,128]{2,1,0:T(8,128)(2,1)S(1)} %all-to-all-done.refs_1_, bf16[2,2,256,128]{3,2,1,0:T(8,128)(2,1)S(1)} %pad_maximum_fusion.refs_2_), custom_call_target="tpu_custom_call" | custom-call | flops 10000000000 | tf_op jit(solution)/shard_map/attend_0/pallas_call | solution.py:236
  32.7 0.0 collective-permute-done.4.refs_2_
  32.7 2.8 %attend_1.1 = (f32[128,2048]{1,0:T(8,128)S(1)}, bf16[2,2,256,128]{3,2,1,0:T(8,128)(2,1)S(1)}) custom-call(f32[4,4,4,512]{3,2,1,0:T(4,128)S(1)} %reshape.24.refs_0_, bf16[4,1056,128]{2,1,0:T(8,128)(2,1)S(1)} %all-to-all-done.refs_1_, bf16[2,2,256,128]{3,2,1,0:T(8,128)(2,1)S(1)} %collective-permute-done.4.refs_2_, f32[128,2048]{1,0:T(8,128)S(1)} %get-tuple-element.23.refs_3_), custom_call_target="tpu_custom_call" | custom-call | flops 10000000000 | tf_op jit(solution)/shard_map/attend_1/pallas_call | solution.py:236
  35.5 0.0 collective-permute-done.3.refs_2_
  35.5 2.8 %attend_3.1 = (f32[128,2048]{1,0:T(8,128)S(1)}, bf16[2,2,256,128]{3,2,1,0:T(8,128)(2,1)S(1)}) custom-call(f32[4,4,4,512]{3,2,1,0:T(4,128)S(1)} %reshape.24.refs_0_, bf16[4,1056,128]{2,1,0:T(8,128)(2,1)S(1)} %all-to-all-done.refs_1_, bf16[2,2,256,128]{3,2,1,0:T(8,128)(2,1)S(1)} %collective-permute-done.3.refs_2_, f32[128,2048]{1,0:T(8,128)S(1)} %get-tuple-element.24.refs_3_), custom_call_target="tpu_custom_call" | custom-call | flops 10000000000 | tf_op jit(solution)/shard_map/attend_3/pallas_call | solution.py:236
  38.3 0.0 collective-permute-done.2.refs_2_
  38.3 3.6 %attend_2.1 = (bf16[4,128,512]{2,1,0:T(8,128)(2,1)}, bf16[2,2,256,128]{3,2,1,0:T(8,128)(2,1)S(1)}) custom-call(f32[4,4,4,512]{3,2,1,0:T(4,128)S(1)} %reshape.24.refs_0_, bf16[4,1056,128]{2,1,0:T(8,128)(2,1)S(1)} %all-to-all-done.refs_1_, bf16[2,2,256,128]{3,2,1,0:T(8,128)(2,1)S(1)} %collective-permute-done.2.refs_2_, f32[128,2048]{1,0:T(8,128)S(1)} %get-tuple-element.25.refs_3_), custom_call_target="tpu_custom_call" | custom-call | flops 10000000000 | tf_op jit(solution)/shard_map/attend_2/pallas_call | solution.py:236
  41.9 4.7 %collective-permute-start.7 = (bf16[2,2,256,128]{3,2,1,0:T(8,128)(2,1)S(1)}, bf16[2,2,256,128]{3,2,1,0:T(8,128)(2,1)S(1)}, u32[]{:S(2)}, u32[]{:S(2)}) collective-permute-start(bf16[2,2,256,128]{3,2,1,0:T(8,128)(2,1)S(1)} %get-tuple-element.30), channel_id=1, source_target_pairs={{0,256},{128,384},{256,0},{384,128},{1,257},{129,385},{257,1},{385... | collective-permute-start | bytes 786440 | tf_op jit(solution)/shard_map/ppermute | solution.py:190
  46.5 2.3 %collective-permute-start.6 = (bf16[2,2,256,128]{3,2,1,0:T(8,128)(2,1)S(1)}, bf16[2,2,256,128]{3,2,1,0:T(8,128)(2,1)S(1)}, u32[]{:S(2)}, u32[]{:S(2)}) collective-permute-start(bf16[2,2,256,128]{3,2,1,0:T(8,128)(2,1)S(1)} %get-tuple-element.29), channel_id=1, source_target_pairs={{0,128},{128,256},{256,384},{384,0},{1,129},{129,257},{257,385},{3... | collective-permute-start | bytes 786440 | tf_op jit(solution)/shard_map/ppermute | solution.py:190
  48.8 4.2 %collective-permute-start.5 = (bf16[2,2,256,128]{3,2,1,0:T(8,128)(2,1)S(1)}, bf16[2,2,256,128]{3,2,1,0:T(8,128)(2,1)S(1)}, u32[]{:S(2)}, u32[]{:S(2)}) collective-permute-start(bf16[2,2,256,128]{3,2,1,0:T(8,128)(2,1)S(1)} %get-tuple-element.28), channel_id=1, source_target_pairs={{0,384},{128,0},{256,128},{384,256},{1,385},{129,1},{257,129},{385... | collective-permute-start | bytes 786440 | tf_op jit(solution)/shard_map/ppermute | solution.py:190
  53.0 3.5 %all-to-all-start.1 = ((bf16[4,128,512]{2,1,0:T(8,128)(2,1)}), bf16[4,128,512]{2,1,0:T(8,128)(2,1)S(1)}, u32[]{:S(2)}, u32[]{:S(2)}) async-start(bf16[4,128,512]{2,1,0:T(8,128)(2,1)} %get-tuple-element.26), calls=%async_computation.1 | async-start | bytes 1048576 | tf_op jit(solution)/shard_map/all_to_all | solution.py:250
  56.5 0.0 collective-permute-done.7.c
  56.5 2.0 %collective-permute-done.6.b = bf16[2,2,256,128]{3,2,1,0:T(8,128)(2,1)S(1)} collective-permute-done((bf16[2,2,256,128]{3,2,1,0:T(8,128)(2,1)S(1)}, bf16[2,2,256,128]{3,2,1,0:T(8,128)(2,1)S(1)}, u32[]{:S(2)}, u32[]{:S(2)}) %collective-permute-start.6) | collective-permute-done | bytes 262176 | tf_op jit(solution)/shard_map/ppermute | solution.py:190
  58.5 0.0 collective-permute-done.5.a
  58.5 0.1 add_partials.1
  58.6 8.6 %collective-permute-start.8 = (bf16[2,256,128]{2,1,0:T(8,128)(2,1)S(1)}, bf16[2,256,128]{2,1,0:T(8,128)(2,1)S(1)}, u32[]{:S(2)}, u32[]{:S(2)}) collective-permute-start(bf16[2,256,128]{2,1,0:T(8,128)(2,1)S(1)} %get-tuple-element.31), channel_id=1, source_target_pairs={{0,126},{1,127},{2,64},{3,65},{4,66},{5,67},{6,68},{7,69},{8,70},{... | collective-permute-start | bytes 393224 | tf_op jit(solution)/shard_map/ppermute | solution.py:259
  67.2 0.5 collective-permute-start.9
  67.8 0.0 all-to-all-done.1.dq
  67.8 1.0 %unpack_queries.1 = bf16[256,1024]{1,0:T(8,128)(2,1)} custom-call(bf16[4,128,512]{2,1,0:T(8,128)(2,1)S(1)} %all-to-all-done.1.dq), custom_call_target="tpu_custom_call" | custom-call | tf_op jit(solution)/shard_map/unpack_queries/pallas_call | solution.py:261
  68.8 0.4 collective-permute-done.8.other
  69.2 2.8 %collective-permute-done.9.own = bf16[2,256,128]{2,1,0:T(8,128)(2,1)S(1)} collective-permute-done((bf16[2,256,128]{2,1,0:T(8,128)(2,1)S(1)}, bf16[2,256,128]{2,1,0:T(8,128)(2,1)S(1)}, u32[]{:S(2)}, u32[]{:S(2)}) %collective-permute-start.9) | collective-permute-done | bytes 131104 | tf_op jit(solution)/shard_map/ppermute | solution.py:260
  71.9 0.7 %unpack_kv.1 = (bf16[256,256]{1,0:T(8,128)(2,1)}, bf16[256,256]{1,0:T(8,128)(2,1)}) custom-call(s32[8,128]{1,0:T(8,128)S(1)} %broadcast_in_dim.21.swap, bf16[2,256,128]{2,1,0:T(8,128)(2,1)S(1)} %collective-permute-done.8.other, bf16[2,256,128]{2,1,0:T(8,128)(2,1)S(1)} %collective-permute-done.9.own), custom_call_target="tpu_custom_call" | custom-call | tf_op jit(solution)/shard_map/unpack_kv/pallas_call | solution.py:269
  (8 shorter events, 0.1 us)
Async XLA Ops:
  1.6 14.0 %collective-permute-start = (bf16[2,256,128]{2,1,0:T(8,128)(2,1)S(1)}, bf16[2,256,128]{2,1,0:T(8,128)(2,1)S(1)}, u32[]{:S(2)}, u32[]{:S(2)}) collective-permute-start(bf16[2,256,128]{2,1,0:T(8,128)(2,1)S(1)} %pad_maximum_fusion.1), channel_id=1, source_target_pairs={{0,67},{1,66},{2,69},{3,68},{4,71},{5,70},{6,73},{7,72},{8,75},{9,... | collective-permute-start | bytes 393224 | tf_op jit(solution)/shard_map/ppermute | solution.py:199
  11.5 3.6 %copy-start = (s32[512]{0:T(512)S(1)}, s32[512]{0:T(512)}, u32[]{:S(2)}) copy-start(s32[512]{0:T(512)} %param.13) | copy-start | bytes 6148
  11.5 18.4 %all-to-all-start = ((bf16[4,1056,128]{2,1,0:T(8,128)(2,1)}), bf16[4,1056,128]{2,1,0:T(8,128)(2,1)S(1)}, u32[]{:S(2)}, u32[]{:S(2)}) async-start(bf16[4,1056,128]{2,1,0:T(8,128)(2,1)} %pack_queries.1), calls=%async_computation | async-start | bytes 2162688 | tf_op jit(solution)/shard_map/all_to_all | solution.py:218
  15.6 4.0 %collective-permute-start.1 = (bf16[2,256,128]{2,1,0:T(8,128)(2,1)S(1)}, bf16[2,256,128]{2,1,0:T(8,128)(2,1)S(1)}, u32[]{:S(2)}, u32[]{:S(2)}) collective-permute-start(bf16[2,256,128]{2,1,0:T(8,128)(2,1)S(1)} %pad_maximum_fusion.2), channel_id=1, source_target_pairs={{0,2},{1,3},{2,4},{3,5},{4,6},{5,7},{6,8},{7,9},{8,10},{9,11},{10,... | collective-permute-start | bytes 393224 | tf_op jit(solution)/shard_map/ppermute | solution.py:217
  19.7 13.0 %collective-permute-start.4 = (bf16[2,2,256,128]{3,2,1,0:T(8,128)(2,1)S(1)}, bf16[2,2,256,128]{3,2,1,0:T(8,128)(2,1)S(1)}, u32[]{:S(2)}, u32[]{:S(2)}) collective-permute-start(bf16[2,2,256,128]{3,2,1,0:T(8,128)(2,1)S(1)} %pad_maximum_fusion.refs_2_), channel_id=1, source_target_pairs={{0,128},{128,256},{256,384},{384,0},{1,129},{129,257},{257,385},{3... | collective-permute-start | bytes 786440 | tf_op jit(solution)/shard_map/ppermute | solution.py:190
  22.9 12.5 %collective-permute-start.3 = (bf16[2,2,256,128]{3,2,1,0:T(8,128)(2,1)S(1)}, bf16[2,2,256,128]{3,2,1,0:T(8,128)(2,1)S(1)}, u32[]{:S(2)}, u32[]{:S(2)}) collective-permute-start(bf16[2,2,256,128]{3,2,1,0:T(8,128)(2,1)S(1)} %pad_maximum_fusion.refs_2_), channel_id=1, source_target_pairs={{0,384},{128,0},{256,128},{384,256},{1,385},{129,1},{257,129},{385... | collective-permute-start | bytes 786440 | tf_op jit(solution)/shard_map/ppermute | solution.py:190
  26.3 12.0 %collective-permute-start.2 = (bf16[2,2,256,128]{3,2,1,0:T(8,128)(2,1)S(1)}, bf16[2,2,256,128]{3,2,1,0:T(8,128)(2,1)S(1)}, u32[]{:S(2)}, u32[]{:S(2)}) collective-permute-start(bf16[2,2,256,128]{3,2,1,0:T(8,128)(2,1)S(1)} %pad_maximum_fusion.refs_2_), channel_id=1, source_target_pairs={{0,256},{128,384},{256,0},{384,128},{1,257},{129,385},{257,1},{385... | collective-permute-start | bytes 786440 | tf_op jit(solution)/shard_map/ppermute | solution.py:190
  41.9 14.7 %collective-permute-start.7 = (bf16[2,2,256,128]{3,2,1,0:T(8,128)(2,1)S(1)}, bf16[2,2,256,128]{3,2,1,0:T(8,128)(2,1)S(1)}, u32[]{:S(2)}, u32[]{:S(2)}) collective-permute-start(bf16[2,2,256,128]{3,2,1,0:T(8,128)(2,1)S(1)} %get-tuple-element.30), channel_id=1, source_target_pairs={{0,256},{128,384},{256,0},{384,128},{1,257},{129,385},{257,1},{385... | collective-permute-start | bytes 786440 | tf_op jit(solution)/shard_map/ppermute | solution.py:190
  46.5 12.0 %collective-permute-start.6 = (bf16[2,2,256,128]{3,2,1,0:T(8,128)(2,1)S(1)}, bf16[2,2,256,128]{3,2,1,0:T(8,128)(2,1)S(1)}, u32[]{:S(2)}, u32[]{:S(2)}) collective-permute-start(bf16[2,2,256,128]{3,2,1,0:T(8,128)(2,1)S(1)} %get-tuple-element.29), channel_id=1, source_target_pairs={{0,128},{128,256},{256,384},{384,0},{1,129},{129,257},{257,385},{3... | collective-permute-start | bytes 786440 | tf_op jit(solution)/shard_map/ppermute | solution.py:190
  48.8 9.7 %collective-permute-start.5 = (bf16[2,2,256,128]{3,2,1,0:T(8,128)(2,1)S(1)}, bf16[2,2,256,128]{3,2,1,0:T(8,128)(2,1)S(1)}, u32[]{:S(2)}, u32[]{:S(2)}) collective-permute-start(bf16[2,2,256,128]{3,2,1,0:T(8,128)(2,1)S(1)} %get-tuple-element.28), channel_id=1, source_target_pairs={{0,384},{128,0},{256,128},{384,256},{1,385},{129,1},{257,129},{385... | collective-permute-start | bytes 786440 | tf_op jit(solution)/shard_map/ppermute | solution.py:190
  53.0 14.7 %all-to-all-start.1 = ((bf16[4,128,512]{2,1,0:T(8,128)(2,1)}), bf16[4,128,512]{2,1,0:T(8,128)(2,1)S(1)}, u32[]{:S(2)}, u32[]{:S(2)}) async-start(bf16[4,128,512]{2,1,0:T(8,128)(2,1)} %get-tuple-element.26), calls=%async_computation.1 | async-start | bytes 1048576 | tf_op jit(solution)/shard_map/all_to_all | solution.py:250
  58.6 10.5 %collective-permute-start.8 = (bf16[2,256,128]{2,1,0:T(8,128)(2,1)S(1)}, bf16[2,256,128]{2,1,0:T(8,128)(2,1)S(1)}, u32[]{:S(2)}, u32[]{:S(2)}) collective-permute-start(bf16[2,256,128]{2,1,0:T(8,128)(2,1)S(1)} %get-tuple-element.31), channel_id=1, source_target_pairs={{0,126},{1,127},{2,64},{3,65},{4,66},{5,67},{6,68},{7,69},{8,70},{... | collective-permute-start | bytes 393224 | tf_op jit(solution)/shard_map/ppermute | solution.py:259
  67.2 4.7 %collective-permute-start.9 = (bf16[2,256,128]{2,1,0:T(8,128)(2,1)S(1)}, bf16[2,256,128]{2,1,0:T(8,128)(2,1)S(1)}, u32[]{:S(2)}, u32[]{:S(2)}) collective-permute-start(bf16[2,256,128]{2,1,0:T(8,128)(2,1)S(1)} %get-tuple-element.32), channel_id=1, source_target_pairs={{0,62},{1,63},{2,0},{3,1},{4,2},{5,3},{6,4},{7,5},{8,6},{9,7},{10,... | collective-permute-start | bytes 393224 | tf_op jit(solution)/shard_map/ppermute | solution.py:260

commit v5 on v4

--- a/solution.py
+++ b/solution.py
@@ -213,8 +213,9 @@
         compiler_params=WIDE,
         name="pack_queries",
     )(queries, attn_out, grad_out, row_total)
-    own, other = lax.optimization_barrier((own, other))
+    own, message = lax.optimization_barrier((own, message))
     own = lax.ppermute(own, names, route(1, lambda a, c: (a, c)))
+    other, message = lax.optimization_barrier((other, message))
     message = lax.all_to_all(message, ("x_hi", "x_lo"), 0, 0, tiled=True)
 
     kv = jnp.stack([own, other])
@@ -227,17 +228,17 @@
     visible = key_ids < jnp.repeat(query_ids, 2, axis=0).reshape(1, 1, 4, 2)
     hide = jnp.repeat(jnp.where(visible, f32(0.0), f32(HIDDEN)), TOK, axis=3)
 
-    turns = (1, 3, 2)
-    blocks = [kv] + [along_y(kv, turn) for turn in turns]
+    turns = (1, 2, 3)
+    blocks = [along_y(kv, turn) for turn in turns] + [kv]
     dq = None
     parts = []
-    for turn, block in zip((0,) + turns, blocks):
-        first, last = turn == 0, turn == turns[-1]
+    for turn, block in zip(turns + (0,), blocks):
+        first, last = turn == turns[0], turn == 0
         dq, dkv = pl.pallas_call(
             functools.partial(attend, turn, first, last),
             out_shape=(
                 shape(4, HD, ROWS) if last else jax.ShapeDtypeStruct((HD, 4 * ROWS), f32),
-                jax.ShapeDtypeStruct((2, 2, TOK, HD), f32 if first else bf16),
+                jax.ShapeDtypeStruct((2, 2, TOK, HD), f32 if last else bf16),
             ),
             in_specs=[VMEM] * (3 if first else 4),
             out_specs=(VMEM, VMEM),
@@ -246,7 +247,24 @@
             cost_estimate=LONG,
             name="attend_%d" % turn,
         )(hide, message, block, *(() if first else (dq,)))
-        parts.append(dkv if first else along_y(dkv, -turn))
+        parts.append(dkv)
+    def along_cores(block, step):
+        axes = ("y", "outer")
+        pairs = []
+        for a in range(y_count):
+            for b in range(outer):
+                to_a, to_b = (a, b + 1) if b % 2 == 0 else ((a + 1) % y_count, b - 1)
+                pair = (a * outer + b, to_a * outer + to_b)
+                pairs.append(pair if step == 1 else pair[::-1])
+        return lax.ppermute(block, axes, pairs)
+
+    before, opposite, after, mine = parts
+    before = along_cores(before, -1)
+    after = along_cores(after, 1)
+    opposite = along_y(opposite, 2)
+    before, after, dq = lax.optimization_barrier((before, after, dq))
+    before = along_cores(before, -1)
+    after = along_cores(after, 1)
     dq = lax.all_to_all(dq, ("x_hi", "x_lo"), 0, 0, tiled=True)
     other, own = pl.pallas_call(
         add_partials,
@@ -255,7 +273,7 @@
         out_specs=(VMEM, VMEM),
         compiler_params=PARAMS,
         name="add_partials",
-    )(*parts)
+    )(mine, before, after, opposite)
     other = lax.ppermute(other, names, route(-1, lambda a, c: (1 - a, c)))
     own = lax.ppermute(own, names, route(-1, lambda a, c: (a, c)))
     grad_queries = pl.pallas_call(

time: 73.9 us -> 73.3 us (level)
  starting transfers between devices: 44.6 us -> 52.3 us
  waiting for transfers between devices: 8.8 us -> 1.17 us
    ppermute x0 -> x4, starting transfers between devices: none -> 12.1 us  [along_cores(): return lax.ppermute(block, axes, pairs)]
    ppermute x6 -> x4, starting transfers between devices: 21.3 us -> 13 us  [along_y(): lax.ppermute(block, 'y', [(i, (i + turn) % y_count) for i in range(y_coun...]
    ppermute x1, waiting for transfers between devices: 3.63 us -> 0.01 us  [per_device(): own = lax.ppermute(own, names, route(1, lambda a, c: (a, c)))]
    ppermute x1, waiting for transfers between devices: 2.77 us -> 0.02 us  [per_device(): own = lax.ppermute(own, names, route(-1, lambda a, c: (a, c)))]
    ppermute x1, starting transfers between devices: 0.54 us -> 3.18 us  [per_device(): own = lax.ppermute(own, names, route(-1, lambda a, c: (a, c)))]
    ppermute x6 -> x4, waiting for transfers between devices: 1.99 us -> 0.01 us  [along_y(): lax.ppermute(block, 'y', [(i, (i + turn) % y_count) for i in range(y_coun...]
    all_to_all x1, starting transfers between devices: 3.53 us -> 5.18 us  [per_device(): message = lax.all_to_all(message, ('x_hi', 'x_lo'), 0, 0, tiled=True)]
    ppermute x1, starting transfers between devices: 8.59 us -> 7.22 us  [per_device(): other = lax.ppermute(other, names, route(-1, lambda a, c: (1 - a, c)))]
  transfers between devices with their start and end apart: 12 -> 14, of which waited for: 4 -> 2; matrix products, arithmetic and copies ran while one was open for 1% -> 1% of each run, Pallas kernels for 17% -> 22%
where the time goes in v5:
time: 73.3 us; the launch traced here: 72.8 us
  starting transfers between devices  52.3 us (71%)
  Pallas kernels  16.5 us (23%)
  local copies, waits for them, and re-layouts  1.68 us (2%)
  waiting for transfers between devices  1.17 us (2%)
  between operations  0.9 us (1%)
    ppermute x4, starting transfers between devices, along_y(): lax.ppermute(block, 'y', [(i, (i + turn) % y_count) for i in range(y_coun...  13 us
    ppermute x4, starting transfers between devices, along_cores(): return lax.ppermute(block, axes, pairs)  12.1 us
    pallas_call x4, Pallas kernels, per_device(): pl.pallas_call(functools.partial(attend, turn, first, last), out_shape=(s...  11.9 us
    ppermute x1, starting transfers between devices, per_device(): other = lax.ppermute(other, names, route(-1, lambda a, c: (1 - a, c)))  7.22 us
    ppermute x1, starting transfers between devices, per_device(): other = lax.ppermute(other, names, route(1, lambda a, c: (1 - a, 1 - c)))  7.13 us
    all_to_all x1, starting transfers between devices, per_device(): message = lax.all_to_all(message, ('x_hi', 'x_lo'), 0, 0, tiled=True)  5.18 us
    all_to_all x1, starting transfers between devices, per_device(): dq = lax.all_to_all(dq, ('x_hi', 'x_lo'), 0, 0, tiled=True)  4.47 us
    ppermute x1, starting transfers between devices, per_device(): own = lax.ppermute(own, names, route(-1, lambda a, c: (a, c)))  3.18 us
  transfers between devices with their start and end apart: 14, of which 2 were waited for; matrix products, arithmetic and copies ran while one was open for 1% of the time, Pallas kernels for 22%

profile of v5, /device:TPU:1, one launch (start us, length us, event | category | flops | bytes accessed | tf_op | source)
XLA Modules:
  0.0 72.8 jit_solution(9720023452615875553)
XLA Ops:
  0.6 1.0 %dynamic-slice_bitcast_fusion = (bf16[1,256,128]{2,1,0:T(8,128)(2,1)S(1)}, bf16[1,256,128]{2,1,0:T(8,128)(2,1)S(1)}, bf16[1,256,128]{2,1,0:T(8,128)(2,1)S(1)}, bf16[1,256,128]{2,1,0:T(8,128)(2,1)S(1)}) fusion(bf16[256,512]{1,0:T(8,128)(2,1)} %param.9, s32[]{:T(128)S(6)} %select_n.48, s32[]{:T(128)S(6)} %select_n.47, bf16[256,512]{1,0:T(8,128)(2,1)} %param.8), kind=kLoop, calls=%fused_computation.3 | loop fusion | bytes 524296 | tf_op jit(solution)/shard_map/stack | solution.py:194
  1.6 0.0 copy-start
  1.6 7.1 %collective-permute-start = (bf16[2,256,128]{2,1,0:T(8,128)(2,1)S(1)}, bf16[2,256,128]{2,1,0:T(8,128)(2,1)S(1)}, u32[]{:S(2)}, u32[]{:S(2)}) collective-permute-start(bf16[2,256,128]{2,1,0:T(8,128)(2,1)S(1)} %pad_maximum_fusion.1), channel_id=1, source_target_pairs={{0,67},{1,66},{2,69},{3,68},{4,71},{5,70},{6,73},{7,72},{8,75},{9,... | collective-permute-start | bytes 393224 | tf_op jit(solution)/shard_map/ppermute | solution.py:199
  8.8 2.7 %pack_queries.1 = bf16[4,1056,128]{2,1,0:T(8,128)(2,1)} custom-call(bf16[256,1024]{1,0:T(8,128)(2,1)} %queries.1, bf16[256,1024]{1,0:T(8,128)(2,1)} %attn_out.1, bf16[256,1024]{1,0:T(8,128)(2,1)} %grad_out.1, f32[8,256]{1,0:T(8,128)} %row_total), custom_call_target="tpu_custom_call" | custom-call | tf_op jit(solution)/shard_map/pack_queries/pallas_call | solution.py:201
  11.5 0.0 collective-permute-start.1
  11.6 0.0 copy-done
  11.6 0.1 reshape.21
  11.7 0.0 collective-permute-done
  11.7 5.2 %all-to-all-start = ((bf16[4,1056,128]{2,1,0:T(8,128)(2,1)}), bf16[4,1056,128]{2,1,0:T(8,128)(2,1)S(1)}, u32[]{:S(2)}, u32[]{:S(2)}) async-start(bf16[4,1056,128]{2,1,0:T(8,128)(2,1)} %pack_queries.1), calls=%async_computation | async-start | bytes 2162688 | tf_op jit(solution)/shard_map/all_to_all | solution.py:219
  16.9 0.1 copy.14
  17.0 0.1 rev.6
  17.1 0.1 dynamic-slice_add_fusion
  17.2 0.0 collective-permute-done.1
  17.3 1.9 %collective-permute-start.2 = (bf16[2,2,256,128]{3,2,1,0:T(8,128)(2,1)S(1)}, bf16[2,2,256,128]{3,2,1,0:T(8,128)(2,1)S(1)}, u32[]{:S(2)}, u32[]{:S(2)}) collective-permute-start(bf16[2,2,256,128]{3,2,1,0:T(8,128)(2,1)S(1)} %pad_maximum_fusion.refs_2_), channel_id=1, source_target_pairs={{0,128},{128,256},{256,384},{384,0},{1,129},{129,257},{257,385},{3... | collective-permute-start | bytes 786440 | tf_op jit(solution)/shard_map/ppermute | solution.py:190
  19.2 0.1 copy.15
  19.3 0.1 compare_select_fusion
  19.4 0.1 broadcast_in_dim.20
  19.5 0.1 reshape.24.refs_0_
  19.7 4.6 %collective-permute-start.4 = (bf16[2,2,256,128]{3,2,1,0:T(8,128)(2,1)S(1)}, bf16[2,2,256,128]{3,2,1,0:T(8,128)(2,1)S(1)}, u32[]{:S(2)}, u32[]{:S(2)}) collective-permute-start(bf16[2,2,256,128]{3,2,1,0:T(8,128)(2,1)S(1)} %pad_maximum_fusion.refs_2_), channel_id=1, source_target_pairs={{0,384},{128,0},{256,128},{384,256},{1,385},{129,1},{257,129},{385... | collective-permute-start | bytes 786440 | tf_op jit(solution)/shard_map/ppermute | solution.py:190
  24.2 2.0 %collective-permute-start.5 = (bf16[2,2,256,128]{3,2,1,0:T(8,128)(2,1)S(1)}, bf16[2,2,256,128]{3,2,1,0:T(8,128)(2,1)S(1)}, u32[]{:S(2)}, u32[]{:S(2)}) collective-permute-start(bf16[2,2,256,128]{3,2,1,0:T(8,128)(2,1)S(1)} %pad_maximum_fusion.refs_2_), channel_id=1, source_target_pairs={{0,256},{128,384},{256,0},{384,128},{1,257},{129,385},{257,1},{385... | collective-permute-start | bytes 786440 | tf_op jit(solution)/shard_map/ppermute | solution.py:190
  26.2 0.0 collective-permute-done.2.refs_2_
  26.2 0.6 all-to-all-done.refs_1_
  26.9 2.8 %attend_1.1 = (f32[128,2048]{1,0:T(8,128)S(1)}, bf16[2,2,256,128]{3,2,1,0:T(8,128)(2,1)S(1)}) custom-call(f32[4,4,4,512]{3,2,1,0:T(4,128)S(1)} %reshape.24.refs_0_, bf16[4,1056,128]{2,1,0:T(8,128)(2,1)S(1)} %all-to-all-done.refs_1_, bf16[2,2,256,128]{3,2,1,0:T(8,128)(2,1)S(1)} %collective-permute-done.2.refs_2_), custom_call_target="tpu_custom_call" | custom-call | flops 10000000000 | tf_op jit(solution)/shard_map/attend_1/pallas_call | solution.py:237
  29.6 7.3 %collective-permute-start.3 = (bf16[2,2,256,128]{3,2,1,0:T(8,128)(2,1)S(1)}, bf16[2,2,256,128]{3,2,1,0:T(8,128)(2,1)S(1)}, u32[]{:S(2)}, u32[]{:S(2)}) collective-permute-start(bf16[2,2,256,128]{3,2,1,0:T(8,128)(2,1)S(1)} %get-tuple-element.30), channel_id=1, source_target_pairs={{2,0},{128,2},{6,4},{132,6},{10,8},{136,10},{14,12},{140,14},{18,1... | collective-permute-start | bytes 786440 | tf_op jit(solution)/shard_map/ppermute | solution.py:259
  37.0 0.0 collective-permute-done.5.refs_2_
  37.0 2.8 %attend_2.1 = (f32[128,2048]{1,0:T(8,128)S(1)}, bf16[2,2,256,128]{3,2,1,0:T(8,128)(2,1)S(1)}) custom-call(f32[4,4,4,512]{3,2,1,0:T(4,128)S(1)} %reshape.24.refs_0_, bf16[4,1056,128]{2,1,0:T(8,128)(2,1)S(1)} %all-to-all-done.refs_1_, bf16[2,2,256,128]{3,2,1,0:T(8,128)(2,1)S(1)} %collective-permute-done.5.refs_2_, f32[128,2048]{1,0:T(8,128)S(1)} %get-tuple-element.31.refs_3_), custom_call_target="tpu_custom_call" | custom-call | flops 10000000000 | tf_op jit(solution)/shard_map/attend_2/pallas_call | solution.py:237
  39.8 0.0 collective-permute-done.4.refs_2_
  39.8 2.8 %attend_3.1 = (f32[128,2048]{1,0:T(8,128)S(1)}, bf16[2,2,256,128]{3,2,1,0:T(8,128)(2,1)S(1)}) custom-call(f32[4,4,4,512]{3,2,1,0:T(4,128)S(1)} %reshape.24.refs_0_, bf16[4,1056,128]{2,1,0:T(8,128)(2,1)S(1)} %all-to-all-done.refs_1_, bf16[2,2,256,128]{3,2,1,0:T(8,128)(2,1)S(1)} %collective-permute-done.4.refs_2_, f32[128,2048]{1,0:T(8,128)S(1)} %get-tuple-element.32.refs_3_), custom_call_target="tpu_custom_call" | custom-call | flops 10000000000 | tf_op jit(solution)/shard_map/attend_3/pallas_call | solution.py:237
  42.6 3.0 %collective-permute-start.6 = (bf16[2,2,256,128]{3,2,1,0:T(8,128)(2,1)S(1)}, bf16[2,2,256,128]{3,2,1,0:T(8,128)(2,1)S(1)}, u32[]{:S(2)}, u32[]{:S(2)}) collective-permute-start(bf16[2,2,256,128]{3,2,1,0:T(8,128)(2,1)S(1)} %get-tuple-element.33), channel_id=1, source_target_pairs={{0,2},{2,128},{4,6},{6,132},{8,10},{10,136},{12,14},{14,140},{16,1... | collective-permute-start | bytes 786440 | tf_op jit(solution)/shard_map/ppermute | solution.py:259
  45.6 4.5 %collective-permute-start.9 = (bf16[2,2,256,128]{3,2,1,0:T(8,128)(2,1)S(1)}, bf16[2,2,256,128]{3,2,1,0:T(8,128)(2,1)S(1)}, u32[]{:S(2)}, u32[]{:S(2)}) collective-permute-start(bf16[2,2,256,128]{3,2,1,0:T(8,128)(2,1)S(1)} %get-tuple-element.40), channel_id=1, source_target_pairs={{0,256},{128,384},{256,0},{384,128},{1,257},{129,385},{257,1},{385... | collective-permute-start | bytes 786440 | tf_op jit(solution)/shard_map/ppermute | solution.py:190
  50.1 3.6 %attend_0.1 = (bf16[4,128,512]{2,1,0:T(8,128)(2,1)}, f32[2,2,256,128]{3,2,1,0:T(8,128)S(1)}) custom-call(f32[4,4,4,512]{3,2,1,0:T(4,128)S(1)} %reshape.24.refs_0_, bf16[4,1056,128]{2,1,0:T(8,128)(2,1)S(1)} %all-to-all-done.refs_1_, bf16[2,2,256,128]{3,2,1,0:T(8,128)(2,1)S(1)} %pad_maximum_fusion.refs_2_, f32[128,2048]{1,0:T(8,128)S(1)} %get-tuple-element.34.refs_3_), custom_call_target="tpu_custom_call" | custom-call | flops 10000000000 | tf_op jit(solution)/shard_map/attend_0/pallas_call | solution.py:237
  53.7 0.0 collective-permute-done.3
  53.7 0.0 collective-permute-done.6
  53.7 0.0 collective-permute-start.7
  53.7 1.7 %collective-permute-start.8 = (bf16[2,2,256,128]{3,2,1,0:T(8,128)(2,1)S(1)}, bf16[2,2,256,128]{3,2,1,0:T(8,128)(2,1)S(1)}, u32[]{:S(2)}, u32[]{:S(2)}) collective-permute-start(bf16[2,2,256,128]{3,2,1,0:T(8,128)(2,1)S(1)} %collective-permute-done.6), channel_id=1, source_target_pairs={{0,2},{2,128},{4,6},{6,132},{8,10},{10,136},{12,14},{14,140},{16,1... | collective-permute-start | bytes 786440 | tf_op jit(solution)/shard_map/ppermute | solution.py:259
  55.5 4.5 %all-to-all-start.1 = ((bf16[4,128,512]{2,1,0:T(8,128)(2,1)}), bf16[4,128,512]{2,1,0:T(8,128)(2,1)S(1)}, u32[]{:S(2)}, u32[]{:S(2)}) async-start(bf16[4,128,512]{2,1,0:T(8,128)(2,1)} %get-tuple-element.36), calls=%async_computation.1 | async-start | bytes 1048576 | tf_op jit(solution)/shard_map/all_to_all | solution.py:268
  60.0 0.0 collective-permute-done.9.c
  60.0 0.0 collective-permute-done.7.a
  60.0 0.0 collective-permute-done.8.b
  60.0 0.1 add_partials.1
  60.1 7.2 %collective-permute-start.10 = (bf16[2,256,128]{2,1,0:T(8,128)(2,1)S(1)}, bf16[2,256,128]{2,1,0:T(8,128)(2,1)S(1)}, u32[]{:S(2)}, u32[]{:S(2)}) collective-permute-start(bf16[2,256,128]{2,1,0:T(8,128)(2,1)S(1)} %get-tuple-element.41), channel_id=1, source_target_pairs={{0,126},{1,127},{2,64},{3,65},{4,66},{5,67},{6,68},{7,69},{8,70},{... | collective-permute-start | bytes 393224 | tf_op jit(solution)/shard_map/ppermute | solution.py:277
  67.3 3.2 %collective-permute-start.11 = (bf16[2,256,128]{2,1,0:T(8,128)(2,1)S(1)}, bf16[2,256,128]{2,1,0:T(8,128)(2,1)S(1)}, u32[]{:S(2)}, u32[]{:S(2)}) collective-permute-start(bf16[2,256,128]{2,1,0:T(8,128)(2,1)S(1)} %get-tuple-element.42), channel_id=1, source_target_pairs={{0,62},{1,63},{2,0},{3,1},{4,2},{5,3},{6,4},{7,5},{8,6},{9,7},{10,... | collective-permute-start | bytes 393224 | tf_op jit(solution)/shard_map/ppermute | solution.py:278
  70.5 0.5 all-to-all-done.1.dq
  71.0 1.0 %unpack_queries.1 = bf16[256,1024]{1,0:T(8,128)(2,1)} custom-call(bf16[4,128,512]{2,1,0:T(8,128)(2,1)S(1)} %all-to-all-done.1.dq), custom_call_target="tpu_custom_call" | custom-call | tf_op jit(solution)/shard_map/unpack_queries/pallas_call | solution.py:279
  72.0 0.0 collective-permute-done.10.other
  72.0 0.0 collective-permute-done.11.own
  72.0 0.7 %unpack_kv.1 = (bf16[256,256]{1,0:T(8,128)(2,1)}, bf16[256,256]{1,0:T(8,128)(2,1)}) custom-call(s32[8,128]{1,0:T(8,128)S(1)} %broadcast_in_dim.21.swap, bf16[2,256,128]{2,1,0:T(8,128)(2,1)S(1)} %collective-permute-done.10.other, bf16[2,256,128]{2,1,0:T(8,128)(2,1)S(1)} %collective-permute-done.11.own), custom_call_target="tpu_custom_call" | custom-call | tf_op jit(solution)/shard_map/unpack_kv/pallas_call | solution.py:287
  (8 shorter events, 0.1 us)
Async XLA Ops:
  1.6 9.9 %copy-start = (s32[512]{0:T(512)S(1)}, s32[512]{0:T(512)}, u32[]{:S(2)}) copy-start(s32[512]{0:T(512)} %param.13) | copy-start | bytes 6148
  1.6 10.1 %collective-permute-start = (bf16[2,256,128]{2,1,0:T(8,128)(2,1)S(1)}, bf16[2,256,128]{2,1,0:T(8,128)(2,1)S(1)}, u32[]{:S(2)}, u32[]{:S(2)}) collective-permute-start(bf16[2,256,128]{2,1,0:T(8,128)(2,1)S(1)} %pad_maximum_fusion.1), channel_id=1, source_target_pairs={{0,67},{1,66},{2,69},{3,68},{4,71},{5,70},{6,73},{7,72},{8,75},{9,... | collective-permute-start | bytes 393224 | tf_op jit(solution)/shard_map/ppermute | solution.py:199
  11.5 5.7 %collective-permute-start.1 = (bf16[2,256,128]{2,1,0:T(8,128)(2,1)S(1)}, bf16[2,256,128]{2,1,0:T(8,128)(2,1)S(1)}, u32[]{:S(2)}, u32[]{:S(2)}) collective-permute-start(bf16[2,256,128]{2,1,0:T(8,128)(2,1)S(1)} %pad_maximum_fusion.2), channel_id=1, source_target_pairs={{0,2},{1,3},{2,4},{3,5},{4,6},{5,7},{6,8},{7,9},{8,10},{9,11},{10,... | collective-permute-start | bytes 393224 | tf_op jit(solution)/shard_map/ppermute | solution.py:217
  11.7 15.1 %all-to-all-start = ((bf16[4,1056,128]{2,1,0:T(8,128)(2,1)}), bf16[4,1056,128]{2,1,0:T(8,128)(2,1)S(1)}, u32[]{:S(2)}, u32[]{:S(2)}) async-start(bf16[4,1056,128]{2,1,0:T(8,128)(2,1)} %pack_queries.1), calls=%async_computation | async-start | bytes 2162688 | tf_op jit(solution)/shard_map/all_to_all | solution.py:219
  17.3 9.0 %collective-permute-start.2 = (bf16[2,2,256,128]{3,2,1,0:T(8,128)(2,1)S(1)}, bf16[2,2,256,128]{3,2,1,0:T(8,128)(2,1)S(1)}, u32[]{:S(2)}, u32[]{:S(2)}) collective-permute-start(bf16[2,2,256,128]{3,2,1,0:T(8,128)(2,1)S(1)} %pad_maximum_fusion.refs_2_), channel_id=1, source_target_pairs={{0,128},{128,256},{256,384},{384,0},{1,129},{129,257},{257,385},{3... | collective-permute-start | bytes 786440 | tf_op jit(solution)/shard_map/ppermute | solution.py:190
  19.7 20.1 %collective-permute-start.4 = (bf16[2,2,256,128]{3,2,1,0:T(8,128)(2,1)S(1)}, bf16[2,2,256,128]{3,2,1,0:T(8,128)(2,1)S(1)}, u32[]{:S(2)}, u32[]{:S(2)}) collective-permute-start(bf16[2,2,256,128]{3,2,1,0:T(8,128)(2,1)S(1)} %pad_maximum_fusion.refs_2_), channel_id=1, source_target_pairs={{0,384},{128,0},{256,128},{384,256},{1,385},{129,1},{257,129},{385... | collective-permute-start | bytes 786440 | tf_op jit(solution)/shard_map/ppermute | solution.py:190
  24.2 12.7 %collective-permute-start.5 = (bf16[2,2,256,128]{3,2,1,0:T(8,128)(2,1)S(1)}, bf16[2,2,256,128]{3,2,1,0:T(8,128)(2,1)S(1)}, u32[]{:S(2)}, u32[]{:S(2)}) collective-permute-start(bf16[2,2,256,128]{3,2,1,0:T(8,128)(2,1)S(1)} %pad_maximum_fusion.refs_2_), channel_id=1, source_target_pairs={{0,256},{128,384},{256,0},{384,128},{1,257},{129,385},{257,1},{385... | collective-permute-start | bytes 786440 | tf_op jit(solution)/shard_map/ppermute | solution.py:190
  29.6 24.1 %collective-permute-start.3 = (bf16[2,2,256,128]{3,2,1,0:T(8,128)(2,1)S(1)}, bf16[2,2,256,128]{3,2,1,0:T(8,128)(2,1)S(1)}, u32[]{:S(2)}, u32[]{:S(2)}) collective-permute-start(bf16[2,2,256,128]{3,2,1,0:T(8,128)(2,1)S(1)} %get-tuple-element.30), channel_id=1, source_target_pairs={{2,0},{128,2},{6,4},{132,6},{10,8},{136,10},{14,12},{140,14},{18,1... | collective-permute-start | bytes 786440 | tf_op jit(solution)/shard_map/ppermute | solution.py:259
  42.6 11.1 %collective-permute-start.6 = (bf16[2,2,256,128]{3,2,1,0:T(8,128)(2,1)S(1)}, bf16[2,2,256,128]{3,2,1,0:T(8,128)(2,1)S(1)}, u32[]{:S(2)}, u32[]{:S(2)}) collective-permute-start(bf16[2,2,256,128]{3,2,1,0:T(8,128)(2,1)S(1)} %get-tuple-element.33), channel_id=1, source_target_pairs={{0,2},{2,128},{4,6},{6,132},{8,10},{10,136},{12,14},{14,140},{16,1... | collective-permute-start | bytes 786440 | tf_op jit(solution)/shard_map/ppermute | solution.py:259
  45.6 14.3 %collective-permute-start.9 = (bf16[2,2,256,128]{3,2,1,0:T(8,128)(2,1)S(1)}, bf16[2,2,256,128]{3,2,1,0:T(8,128)(2,1)S(1)}, u32[]{:S(2)}, u32[]{:S(2)}) collective-permute-start(bf16[2,2,256,128]{3,2,1,0:T(8,128)(2,1)S(1)} %get-tuple-element.40), channel_id=1, source_target_pairs={{0,256},{128,384},{256,0},{384,128},{1,257},{129,385},{257,1},{385... | collective-permute-start | bytes 786440 | tf_op jit(solution)/shard_map/ppermute | solution.py:190
  53.7 6.2 %collective-permute-start.7 = (bf16[2,2,256,128]{3,2,1,0:T(8,128)(2,1)S(1)}, bf16[2,2,256,128]{3,2,1,0:T(8,128)(2,1)S(1)}, u32[]{:S(2)}, u32[]{:S(2)}) collective-permute-start(bf16[2,2,256,128]{3,2,1,0:T(8,128)(2,1)S(1)} %collective-permute-done.3), channel_id=1, source_target_pairs={{2,0},{128,2},{6,4},{132,6},{10,8},{136,10},{14,12},{140,14},{18,1... | collective-permute-start | bytes 786440 | tf_op jit(solution)/shard_map/ppermute | solution.py:259
  53.7 6.2 %collective-permute-start.8 = (bf16[2,2,256,128]{3,2,1,0:T(8,128)(2,1)S(1)}, bf16[2,2,256,128]{3,2,1,0:T(8,128)(2,1)S(1)}, u32[]{:S(2)}, u32[]{:S(2)}) collective-permute-start(bf16[2,2,256,128]{3,2,1,0:T(8,128)(2,1)S(1)} %collective-permute-done.6), channel_id=1, source_target_pairs={{0,2},{2,128},{4,6},{6,132},{8,10},{10,136},{12,14},{14,140},{16,1... | collective-permute-start | bytes 786440 | tf_op jit(solution)/shard_map/ppermute | solution.py:259
  55.5 15.5 %all-to-all-start.1 = ((bf16[4,128,512]{2,1,0:T(8,128)(2,1)}), bf16[4,128,512]{2,1,0:T(8,128)(2,1)S(1)}, u32[]{:S(2)}, u32[]{:S(2)}) async-start(bf16[4,128,512]{2,1,0:T(8,128)(2,1)} %get-tuple-element.36), calls=%async_computation.1 | async-start | bytes 1048576 | tf_op jit(solution)/shard_map/all_to_all | solution.py:268
  60.1 11.9 %collective-permute-start.10 = (bf16[2,256,128]{2,1,0:T(8,128)(2,1)S(1)}, bf16[2,256,128]{2,1,0:T(8,128)(2,1)S(1)}, u32[]{:S(2)}, u32[]{:S(2)}) collective-permute-start(bf16[2,256,128]{2,1,0:T(8,128)(2,1)S(1)} %get-tuple-element.41), channel_id=1, source_target_pairs={{0,126},{1,127},{2,64},{3,65},{4,66},{5,67},{6,68},{7,69},{8,70},{... | collective-permute-start | bytes 393224 | tf_op jit(solution)/shard_map/ppermute | solution.py:277
  67.3 4.7 %collective-permute-start.11 = (bf16[2,256,128]{2,1,0:T(8,128)(2,1)S(1)}, bf16[2,256,128]{2,1,0:T(8,128)(2,1)S(1)}, u32[]{:S(2)}, u32[]{:S(2)}) collective-permute-start(bf16[2,256,128]{2,1,0:T(8,128)(2,1)S(1)} %get-tuple-element.42), channel_id=1, source_target_pairs={{0,62},{1,63},{2,0},{3,1},{4,2},{5,3},{6,4},{7,5},{8,6},{9,7},{10,... | collective-permute-start | bytes 393224 | tf_op jit(solution)/shard_map/ppermute | solution.py:278

commit v6 on v5

--- a/solution.py
+++ b/solution.py
@@ -142,7 +142,7 @@
 
 
 def add_partials(mine, a, b, c, other, own):
-    for j, out in ((0, own), (1, other)):
+    for j, out in ((0, other), (1, own)):
         for i in range(2):
             out[i] = (a[j, i].astype(f32) + b[j, i].astype(f32) + c[j, i].astype(f32) + mine[j, i]).astype(bf16)
 
@@ -195,8 +195,8 @@
 
     other = columns(2 * (1 - x_lo) + (1 - x_hi))
     own = columns(2 * x_lo + x_hi)
-    other, row_total = lax.optimization_barrier((other, row_total))
     other = lax.ppermute(other, names, route(1, lambda a, c: (1 - a, 1 - c)))
+    own = lax.ppermute(own, names, route(1, lambda a, c: (a, c)))
 
     message = pl.pallas_call(
         pack_queries,
@@ -214,17 +214,15 @@
         name="pack_queries",
     )(queries, attn_out, grad_out, row_total)
     own, message = lax.optimization_barrier((own, message))
-    own = lax.ppermute(own, names, route(1, lambda a, c: (a, c)))
-    other, message = lax.optimization_barrier((other, message))
     message = lax.all_to_all(message, ("x_hi", "x_lo"), 0, 0, tiled=True)
 
-    kv = jnp.stack([own, other])
+    kv = jnp.stack([other, own])
     stored = block_ids.reshape(y_count, 2, outer, 2)
     query_ids = lax.dynamic_slice(stored, (y, 0, o, 0), (1, 2, 1, 2)).reshape(2, 2)
     key_ids = lax.dynamic_slice(stored, (0, 0, (o + outer - 1) % outer, 0), (y_count, 2, 1, 2)).reshape(y_count, 2, 2)
     key_ids = jnp.concatenate([key_ids[::-1]] * 2)
     key_ids = lax.dynamic_slice(key_ids, (y_count - 1 - y, 0, 0), (y_count, 2, 2))
-    key_ids = jnp.where(x_hi == 0, key_ids, key_ids[:, ::-1]).reshape(y_count, 4, 1, 1)
+    key_ids = jnp.where(x_hi == 0, key_ids[:, ::-1], key_ids).reshape(y_count, 4, 1, 1)
     visible = key_ids < jnp.repeat(query_ids, 2, axis=0).reshape(1, 1, 4, 2)
     hide = jnp.repeat(jnp.where(visible, f32(0.0), f32(HIDDEN)), TOK, axis=3)
 

time: 73.3 us -> 70.6 us (0.963)
  starting transfers between devices: 52.3 us -> 49.2 us
    ppermute x1, starting transfers between devices: 0.02 us -> 3.04 us  [per_device(): own = lax.ppermute(own, names, route(1, lambda a, c: (a, c)))]
    ppermute x1, starting transfers between devices: 7.13 us -> 4.12 us  [per_device(): other = lax.ppermute(other, names, route(1, lambda a, c: (1 - a, 1 - c)))]
    ppermute x4, starting transfers between devices: 12.1 us -> 9.88 us  [along_cores(): return lax.ppermute(block, axes, pairs)]
    ppermute x4, starting transfers between devices: 13 us -> 14.7 us  [along_y(): lax.ppermute(block, 'y', [(i, (i + turn) % y_count) for i in range(y_coun...]
    all_to_all x1, starting transfers between devices: 5.18 us -> 3.53 us  [per_device(): message = lax.all_to_all(message, ('x_hi', 'x_lo'), 0, 0, tiled=True)]
  transfers between devices with their start and end apart: 14 -> 14, of which waited for: 2 -> 3; matrix products, arithmetic and copies ran while one was open for 1% -> 1% of each run, Pallas kernels for 22% -> 22%
where the time goes in v6:
time: 70.6 us; the launch traced here: 70.2 us
  starting transfers between devices  49.2 us (70%)
  Pallas kernels  16.5 us (23%)
  waiting for transfers between devices  1.71 us (2%)
  local copies, waits for them, and re-layouts  1.69 us (2%)
  between operations  0.9 us (1%)
    ppermute x4, starting transfers between devices, along_y(): lax.ppermute(block, 'y', [(i, (i + turn) % y_count) for i in range(y_coun...  14.7 us
    pallas_call x4, Pallas kernels, per_device(): pl.pallas_call(functools.partial(attend, turn, first, last), out_shape=(s...  11.9 us
    ppermute x4, starting transfers between devices, along_cores(): return lax.ppermute(block, axes, pairs)  9.88 us
    ppermute x1, starting transfers between devices, per_device(): other = lax.ppermute(other, names, route(-1, lambda a, c: (1 - a, c)))  6.49 us
    all_to_all x1, starting transfers between devices, per_device(): dq = lax.all_to_all(dq, ('x_hi', 'x_lo'), 0, 0, tiled=True)  4.19 us
    ppermute x1, starting transfers between devices, per_device(): other = lax.ppermute(other, names, route(1, lambda a, c: (1 - a, 1 - c)))  4.12 us
    all_to_all x1, starting transfers between devices, per_device(): message = lax.all_to_all(message, ('x_hi', 'x_lo'), 0, 0, tiled=True)  3.53 us
    ppermute x1, starting transfers between devices, per_device(): own = lax.ppermute(own, names, route(-1, lambda a, c: (a, c)))  3.2 us
  transfers between devices with their start and end apart: 14, of which 3 were waited for; matrix products, arithmetic and copies ran while one was open for 1% of the time, Pallas kernels for 22%

profile of v6, /device:TPU:1, one launch (start us, length us, event | category | flops | bytes accessed | tf_op | source)
XLA Modules:
  0.0 70.2 jit_solution(12948298927688525087)
XLA Ops:
  0.6 0.0 copy-start
  0.7 1.0 %dynamic-slice_bitcast_fusion = (bf16[1,256,128]{2,1,0:T(8,128)(2,1)S(1)}, bf16[1,256,128]{2,1,0:T(8,128)(2,1)S(1)}, bf16[1,256,128]{2,1,0:T(8,128)(2,1)S(1)}, bf16[1,256,128]{2,1,0:T(8,128)(2,1)S(1)}) fusion(bf16[256,512]{1,0:T(8,128)(2,1)} %param.9, s32[]{:T(128)S(6)} %select_n.48, s32[]{:T(128)S(6)} %select_n.47, bf16[256,512]{1,0:T(8,128)(2,1)} %param.8), kind=kLoop, calls=%fused_computation.3 | loop fusion | bytes 524296 | tf_op jit(solution)/shard_map/stack | solution.py:194
  1.6 3.0 %collective-permute-start = (bf16[2,256,128]{2,1,0:T(8,128)(2,1)S(1)}, bf16[2,256,128]{2,1,0:T(8,128)(2,1)S(1)}, u32[]{:S(2)}, u32[]{:S(2)}) collective-permute-start(bf16[2,256,128]{2,1,0:T(8,128)(2,1)S(1)} %pad_maximum_fusion.1), channel_id=1, source_target_pairs={{0,2},{1,3},{2,4},{3,5},{4,6},{5,7},{6,8},{7,9},{8,10},{9,11},{10,... | collective-permute-start | bytes 393224 | tf_op jit(solution)/shard_map/ppermute | solution.py:199
  4.7 4.1 %collective-permute-start.1 = (bf16[2,256,128]{2,1,0:T(8,128)(2,1)S(1)}, bf16[2,256,128]{2,1,0:T(8,128)(2,1)S(1)}, u32[]{:S(2)}, u32[]{:S(2)}) collective-permute-start(bf16[2,256,128]{2,1,0:T(8,128)(2,1)S(1)} %pad_maximum_fusion.2), channel_id=1, source_target_pairs={{0,67},{1,66},{2,69},{3,68},{4,71},{5,70},{6,73},{7,72},{8,75},{9,... | collective-permute-start | bytes 393224 | tf_op jit(solution)/shard_map/ppermute | solution.py:198
  8.8 0.0 copy-done
  8.9 0.1 reshape.21
  9.0 2.7 %pack_queries.1 = bf16[4,1056,128]{2,1,0:T(8,128)(2,1)} custom-call(bf16[256,1024]{1,0:T(8,128)(2,1)} %queries.1, bf16[256,1024]{1,0:T(8,128)(2,1)} %attn_out.1, bf16[256,1024]{1,0:T(8,128)(2,1)} %grad_out.1, f32[8,256]{1,0:T(8,128)} %row_total.1), custom_call_target="tpu_custom_call" | custom-call | tf_op jit(solution)/shard_map/pack_queries/pallas_call | solution.py:201
  11.7 0.0 collective-permute-done
  11.7 3.5 %all-to-all-start = ((bf16[4,1056,128]{2,1,0:T(8,128)(2,1)}), bf16[4,1056,128]{2,1,0:T(8,128)(2,1)S(1)}, u32[]{:S(2)}, u32[]{:S(2)}) async-start(bf16[4,1056,128]{2,1,0:T(8,128)(2,1)} %pack_queries.1), calls=%async_computation | async-start | bytes 2162688 | tf_op jit(solution)/shard_map/all_to_all | solution.py:217
  15.3 0.1 copy.14
  15.4 0.1 rev.6
  15.5 0.1 dynamic-slice_add_fusion
  15.6 0.0 collective-permute-done.1
  15.6 3.2 %collective-permute-start.2 = (bf16[2,2,256,128]{3,2,1,0:T(8,128)(2,1)S(1)}, bf16[2,2,256,128]{3,2,1,0:T(8,128)(2,1)S(1)}, u32[]{:S(2)}, u32[]{:S(2)}) collective-permute-start(bf16[2,2,256,128]{3,2,1,0:T(8,128)(2,1)S(1)} %pad_maximum_fusion.refs_2_), channel_id=1, source_target_pairs={{0,128},{128,256},{256,384},{384,0},{1,129},{129,257},{257,385},{3... | collective-permute-start | bytes 786440 | tf_op jit(solution)/shard_map/ppermute | solution.py:190
  18.9 0.1 copy.15
  18.9 0.1 compare_select_fusion
  19.0 0.1 broadcast_in_dim.20
  19.2 0.1 reshape.24.refs_0_
  19.3 3.4 %collective-permute-start.4 = (bf16[2,2,256,128]{3,2,1,0:T(8,128)(2,1)S(1)}, bf16[2,2,256,128]{3,2,1,0:T(8,128)(2,1)S(1)}, u32[]{:S(2)}, u32[]{:S(2)}) collective-permute-start(bf16[2,2,256,128]{3,2,1,0:T(8,128)(2,1)S(1)} %pad_maximum_fusion.refs_2_), channel_id=1, source_target_pairs={{0,384},{128,0},{256,128},{384,256},{1,385},{129,1},{257,129},{385... | collective-permute-start | bytes 786440 | tf_op jit(solution)/shard_map/ppermute | solution.py:190
  22.7 3.5 %collective-permute-start.5 = (bf16[2,2,256,128]{3,2,1,0:T(8,128)(2,1)S(1)}, bf16[2,2,256,128]{3,2,1,0:T(8,128)(2,1)S(1)}, u32[]{:S(2)}, u32[]{:S(2)}) collective-permute-start(bf16[2,2,256,128]{3,2,1,0:T(8,128)(2,1)S(1)} %pad_maximum_fusion.refs_2_), channel_id=1, source_target_pairs={{0,256},{128,384},{256,0},{384,128},{1,257},{129,385},{257,1},{385... | collective-permute-start | bytes 786440 | tf_op jit(solution)/shard_map/ppermute | solution.py:190
  26.2 0.0 collective-permute-done.2.refs_2_
  26.2 0.4 all-to-all-done.refs_1_
  26.6 2.8 %attend_1.1 = (f32[128,2048]{1,0:T(8,128)S(1)}, bf16[2,2,256,128]{3,2,1,0:T(8,128)(2,1)S(1)}) custom-call(f32[4,4,4,512]{3,2,1,0:T(4,128)S(1)} %reshape.24.refs_0_, bf16[4,1056,128]{2,1,0:T(8,128)(2,1)S(1)} %all-to-all-done.refs_1_, bf16[2,2,256,128]{3,2,1,0:T(8,128)(2,1)S(1)} %collective-permute-done.2.refs_2_), custom_call_target="tpu_custom_call" | custom-call | flops 10000000000 | tf_op jit(solution)/shard_map/attend_1/pallas_call | solution.py:235
  29.4 5.0 %collective-permute-start.3 = (bf16[2,2,256,128]{3,2,1,0:T(8,128)(2,1)S(1)}, bf16[2,2,256,128]{3,2,1,0:T(8,128)(2,1)S(1)}, u32[]{:S(2)}, u32[]{:S(2)}) collective-permute-start(bf16[2,2,256,128]{3,2,1,0:T(8,128)(2,1)S(1)} %get-tuple-element.22), channel_id=1, source_target_pairs={{2,0},{128,2},{6,4},{132,6},{10,8},{136,10},{14,12},{140,14},{18,1... | collective-permute-start | bytes 786440 | tf_op jit(solution)/shard_map/ppermute | solution.py:257
  34.4 0.0 collective-permute-done.5.refs_2_
  34.4 2.8 %attend_2.1 = (f32[128,2048]{1,0:T(8,128)S(1)}, bf16[2,2,256,128]{3,2,1,0:T(8,128)(2,1)S(1)}) custom-call(f32[4,4,4,512]{3,2,1,0:T(4,128)S(1)} %reshape.24.refs_0_, bf16[4,1056,128]{2,1,0:T(8,128)(2,1)S(1)} %all-to-all-done.refs_1_, bf16[2,2,256,128]{3,2,1,0:T(8,128)(2,1)S(1)} %collective-permute-done.5.refs_2_, f32[128,2048]{1,0:T(8,128)S(1)} %get-tuple-element.23.refs_3_), custom_call_target="tpu_custom_call" | custom-call | flops 10000000000 | tf_op jit(solution)/shard_map/attend_2/pallas_call | solution.py:235
  37.2 0.0 collective-permute-done.4.refs_2_
  37.2 2.8 %attend_3.1 = (f32[128,2048]{1,0:T(8,128)S(1)}, bf16[2,2,256,128]{3,2,1,0:T(8,128)(2,1)S(1)}) custom-call(f32[4,4,4,512]{3,2,1,0:T(4,128)S(1)} %reshape.24.refs_0_, bf16[4,1056,128]{2,1,0:T(8,128)(2,1)S(1)} %all-to-all-done.refs_1_, bf16[2,2,256,128]{3,2,1,0:T(8,128)(2,1)S(1)} %collective-permute-done.4.refs_2_, f32[128,2048]{1,0:T(8,128)S(1)} %get-tuple-element.24.refs_3_), custom_call_target="tpu_custom_call" | custom-call | flops 10000000000 | tf_op jit(solution)/shard_map/attend_3/pallas_call | solution.py:235
  40.0 3.1 %collective-permute-start.6 = (bf16[2,2,256,128]{3,2,1,0:T(8,128)(2,1)S(1)}, bf16[2,2,256,128]{3,2,1,0:T(8,128)(2,1)S(1)}, u32[]{:S(2)}, u32[]{:S(2)}) collective-permute-start(bf16[2,2,256,128]{3,2,1,0:T(8,128)(2,1)S(1)} %get-tuple-element.25), channel_id=1, source_target_pairs={{0,2},{2,128},{4,6},{6,132},{8,10},{10,136},{12,14},{14,140},{16,1... | collective-permute-start | bytes 786440 | tf_op jit(solution)/shard_map/ppermute | solution.py:257
  43.1 4.6 %collective-permute-start.9 = (bf16[2,2,256,128]{3,2,1,0:T(8,128)(2,1)S(1)}, bf16[2,2,256,128]{3,2,1,0:T(8,128)(2,1)S(1)}, u32[]{:S(2)}, u32[]{:S(2)}) collective-permute-start(bf16[2,2,256,128]{3,2,1,0:T(8,128)(2,1)S(1)} %get-tuple-element.32), channel_id=1, source_target_pairs={{0,256},{128,384},{256,0},{384,128},{1,257},{129,385},{257,1},{385... | collective-permute-start | bytes 786440 | tf_op jit(solution)/shard_map/ppermute | solution.py:190
  47.7 3.6 %attend_0.1 = (bf16[4,128,512]{2,1,0:T(8,128)(2,1)}, f32[2,2,256,128]{3,2,1,0:T(8,128)S(1)}) custom-call(f32[4,4,4,512]{3,2,1,0:T(4,128)S(1)} %reshape.24.refs_0_, bf16[4,1056,128]{2,1,0:T(8,128)(2,1)S(1)} %all-to-all-done.refs_1_, bf16[2,2,256,128]{3,2,1,0:T(8,128)(2,1)S(1)} %pad_maximum_fusion.refs_2_, f32[128,2048]{1,0:T(8,128)S(1)} %get-tuple-element.26.refs_3_), custom_call_target="tpu_custom_call" | custom-call | flops 10000000000 | tf_op jit(solution)/shard_map/attend_0/pallas_call | solution.py:235
  51.3 0.0 collective-permute-done.3
  51.3 0.0 collective-permute-done.6
  51.3 0.0 collective-permute-start.7
  51.3 1.7 %collective-permute-start.8 = (bf16[2,2,256,128]{3,2,1,0:T(8,128)(2,1)S(1)}, bf16[2,2,256,128]{3,2,1,0:T(8,128)(2,1)S(1)}, u32[]{:S(2)}, u32[]{:S(2)}) collective-permute-start(bf16[2,2,256,128]{3,2,1,0:T(8,128)(2,1)S(1)} %collective-permute-done.6), channel_id=1, source_target_pairs={{0,2},{2,128},{4,6},{6,132},{8,10},{10,136},{12,14},{14,140},{16,1... | collective-permute-start | bytes 786440 | tf_op jit(solution)/shard_map/ppermute | solution.py:257
  53.1 4.2 %all-to-all-start.1 = ((bf16[4,128,512]{2,1,0:T(8,128)(2,1)}), bf16[4,128,512]{2,1,0:T(8,128)(2,1)S(1)}, u32[]{:S(2)}, u32[]{:S(2)}) async-start(bf16[4,128,512]{2,1,0:T(8,128)(2,1)} %get-tuple-element.28), calls=%async_computation.1 | async-start | bytes 1048576 | tf_op jit(solution)/shard_map/all_to_all | solution.py:266
  57.3 0.0 collective-permute-done.9.c
  57.3 0.1 collective-permute-done.7.a
  57.4 0.0 collective-permute-done.8.b
  57.4 0.1 add_partials.1
  57.5 6.5 %collective-permute-start.10 = (bf16[2,256,128]{2,1,0:T(8,128)(2,1)S(1)}, bf16[2,256,128]{2,1,0:T(8,128)(2,1)S(1)}, u32[]{:S(2)}, u32[]{:S(2)}) collective-permute-start(bf16[2,256,128]{2,1,0:T(8,128)(2,1)S(1)} %get-tuple-element.33), channel_id=1, source_target_pairs={{0,126},{1,127},{2,64},{3,65},{4,66},{5,67},{6,68},{7,69},{8,70},{... | collective-permute-start | bytes 393224 | tf_op jit(solution)/shard_map/ppermute | solution.py:275
  64.0 3.2 %collective-permute-start.11 = (bf16[2,256,128]{2,1,0:T(8,128)(2,1)S(1)}, bf16[2,256,128]{2,1,0:T(8,128)(2,1)S(1)}, u32[]{:S(2)}, u32[]{:S(2)}) collective-permute-start(bf16[2,256,128]{2,1,0:T(8,128)(2,1)S(1)} %get-tuple-element.34), channel_id=1, source_target_pairs={{0,62},{1,63},{2,0},{3,1},{4,2},{5,3},{6,4},{7,5},{8,6},{9,7},{10,... | collective-permute-start | bytes 393224 | tf_op jit(solution)/shard_map/ppermute | solution.py:276
  67.2 1.2 %all-to-all-done.1.dq = bf16[4,128,512]{2,1,0:T(8,128)(2,1)S(1)} async-done(((bf16[4,128,512]{2,1,0:T(8,128)(2,1)}), bf16[4,128,512]{2,1,0:T(8,128)(2,1)S(1)}, u32[]{:S(2)}, u32[]{:S(2)}) %all-to-all-start.1) | async-done | bytes 524320 | tf_op jit(solution)/shard_map/all_to_all | solution.py:266
  68.4 1.0 %unpack_queries.1 = bf16[256,1024]{1,0:T(8,128)(2,1)} custom-call(bf16[4,128,512]{2,1,0:T(8,128)(2,1)S(1)} %all-to-all-done.1.dq), custom_call_target="tpu_custom_call" | custom-call | tf_op jit(solution)/shard_map/unpack_queries/pallas_call | solution.py:277
  69.4 0.0 collective-permute-done.10.other
  69.4 0.0 collective-permute-done.11.own
  69.4 0.7 %unpack_kv.1 = (bf16[256,256]{1,0:T(8,128)(2,1)}, bf16[256,256]{1,0:T(8,128)(2,1)}) custom-call(s32[8,128]{1,0:T(8,128)S(1)} %broadcast_in_dim.21.swap, bf16[2,256,128]{2,1,0:T(8,128)(2,1)S(1)} %collective-permute-done.10.other, bf16[2,256,128]{2,1,0:T(8,128)(2,1)S(1)} %collective-permute-done.11.own), custom_call_target="tpu_custom_call" | custom-call | tf_op jit(solution)/shard_map/unpack_kv/pallas_call | solution.py:285
  (8 shorter events, 0.1 us)
Async XLA Ops:
  0.6 8.2 %copy-start = (s32[512]{0:T(512)S(1)}, s32[512]{0:T(512)}, u32[]{:S(2)}) copy-start(s32[512]{0:T(512)} %param.13) | copy-start | bytes 6148
  1.6 10.1 %collective-permute-start = (bf16[2,256,128]{2,1,0:T(8,128)(2,1)S(1)}, bf16[2,256,128]{2,1,0:T(8,128)(2,1)S(1)}, u32[]{:S(2)}, u32[]{:S(2)}) collective-permute-start(bf16[2,256,128]{2,1,0:T(8,128)(2,1)S(1)} %pad_maximum_fusion.1), channel_id=1, source_target_pairs={{0,2},{1,3},{2,4},{3,5},{4,6},{5,7},{6,8},{7,9},{8,10},{9,11},{10,... | collective-permute-start | bytes 393224 | tf_op jit(solution)/shard_map/ppermute | solution.py:199
  4.7 10.9 %collective-permute-start.1 = (bf16[2,256,128]{2,1,0:T(8,128)(2,1)S(1)}, bf16[2,256,128]{2,1,0:T(8,128)(2,1)S(1)}, u32[]{:S(2)}, u32[]{:S(2)}) collective-permute-start(bf16[2,256,128]{2,1,0:T(8,128)(2,1)S(1)} %pad_maximum_fusion.2), channel_id=1, source_target_pairs={{0,67},{1,66},{2,69},{3,68},{4,71},{5,70},{6,73},{7,72},{8,75},{9,... | collective-permute-start | bytes 393224 | tf_op jit(solution)/shard_map/ppermute | solution.py:198
  11.7 14.9 %all-to-all-start = ((bf16[4,1056,128]{2,1,0:T(8,128)(2,1)}), bf16[4,1056,128]{2,1,0:T(8,128)(2,1)S(1)}, u32[]{:S(2)}, u32[]{:S(2)}) async-start(bf16[4,1056,128]{2,1,0:T(8,128)(2,1)} %pack_queries.1), calls=%async_computation | async-start | bytes 2162688 | tf_op jit(solution)/shard_map/all_to_all | solution.py:217
  15.6 10.6 %collective-permute-start.2 = (bf16[2,2,256,128]{3,2,1,0:T(8,128)(2,1)S(1)}, bf16[2,2,256,128]{3,2,1,0:T(8,128)(2,1)S(1)}, u32[]{:S(2)}, u32[]{:S(2)}) collective-permute-start(bf16[2,2,256,128]{3,2,1,0:T(8,128)(2,1)S(1)} %pad_maximum_fusion.refs_2_), channel_id=1, source_target_pairs={{0,128},{128,256},{256,384},{384,0},{1,129},{129,257},{257,385},{3... | collective-permute-start | bytes 786440 | tf_op jit(solution)/shard_map/ppermute | solution.py:190
  19.3 17.9 %collective-permute-start.4 = (bf16[2,2,256,128]{3,2,1,0:T(8,128)(2,1)S(1)}, bf16[2,2,256,128]{3,2,1,0:T(8,128)(2,1)S(1)}, u32[]{:S(2)}, u32[]{:S(2)}) collective-permute-start(bf16[2,2,256,128]{3,2,1,0:T(8,128)(2,1)S(1)} %pad_maximum_fusion.refs_2_), channel_id=1, source_target_pairs={{0,384},{128,0},{256,128},{384,256},{1,385},{129,1},{257,129},{385... | collective-permute-start | bytes 786440 | tf_op jit(solution)/shard_map/ppermute | solution.py:190
  22.7 11.8 %collective-permute-start.5 = (bf16[2,2,256,128]{3,2,1,0:T(8,128)(2,1)S(1)}, bf16[2,2,256,128]{3,2,1,0:T(8,128)(2,1)S(1)}, u32[]{:S(2)}, u32[]{:S(2)}) collective-permute-start(bf16[2,2,256,128]{3,2,1,0:T(8,128)(2,1)S(1)} %pad_maximum_fusion.refs_2_), channel_id=1, source_target_pairs={{0,256},{128,384},{256,0},{384,128},{1,257},{129,385},{257,1},{385... | collective-permute-start | bytes 786440 | tf_op jit(solution)/shard_map/ppermute | solution.py:190
  29.4 21.9 %collective-permute-start.3 = (bf16[2,2,256,128]{3,2,1,0:T(8,128)(2,1)S(1)}, bf16[2,2,256,128]{3,2,1,0:T(8,128)(2,1)S(1)}, u32[]{:S(2)}, u32[]{:S(2)}) collective-permute-start(bf16[2,2,256,128]{3,2,1,0:T(8,128)(2,1)S(1)} %get-tuple-element.22), channel_id=1, source_target_pairs={{2,0},{128,2},{6,4},{132,6},{10,8},{136,10},{14,12},{140,14},{18,1... | collective-permute-start | bytes 786440 | tf_op jit(solution)/shard_map/ppermute | solution.py:257
  40.0 11.3 %collective-permute-start.6 = (bf16[2,2,256,128]{3,2,1,0:T(8,128)(2,1)S(1)}, bf16[2,2,256,128]{3,2,1,0:T(8,128)(2,1)S(1)}, u32[]{:S(2)}, u32[]{:S(2)}) collective-permute-start(bf16[2,2,256,128]{3,2,1,0:T(8,128)(2,1)S(1)} %get-tuple-element.25), channel_id=1, source_target_pairs={{0,2},{2,128},{4,6},{6,132},{8,10},{10,136},{12,14},{14,140},{16,1... | collective-permute-start | bytes 786440 | tf_op jit(solution)/shard_map/ppermute | solution.py:257
  43.1 14.2 %collective-permute-start.9 = (bf16[2,2,256,128]{3,2,1,0:T(8,128)(2,1)S(1)}, bf16[2,2,256,128]{3,2,1,0:T(8,128)(2,1)S(1)}, u32[]{:S(2)}, u32[]{:S(2)}) collective-permute-start(bf16[2,2,256,128]{3,2,1,0:T(8,128)(2,1)S(1)} %get-tuple-element.32), channel_id=1, source_target_pairs={{0,256},{128,384},{256,0},{384,128},{1,257},{129,385},{257,1},{385... | collective-permute-start | bytes 786440 | tf_op jit(solution)/shard_map/ppermute | solution.py:190
  51.3 6.1 %collective-permute-start.7 = (bf16[2,2,256,128]{3,2,1,0:T(8,128)(2,1)S(1)}, bf16[2,2,256,128]{3,2,1,0:T(8,128)(2,1)S(1)}, u32[]{:S(2)}, u32[]{:S(2)}) collective-permute-start(bf16[2,2,256,128]{3,2,1,0:T(8,128)(2,1)S(1)} %collective-permute-done.3), channel_id=1, source_target_pairs={{2,0},{128,2},{6,4},{132,6},{10,8},{136,10},{14,12},{140,14},{18,1... | collective-permute-start | bytes 786440 | tf_op jit(solution)/shard_map/ppermute | solution.py:257
  51.3 6.1 %collective-permute-start.8 = (bf16[2,2,256,128]{3,2,1,0:T(8,128)(2,1)S(1)}, bf16[2,2,256,128]{3,2,1,0:T(8,128)(2,1)S(1)}, u32[]{:S(2)}, u32[]{:S(2)}) collective-permute-start(bf16[2,2,256,128]{3,2,1,0:T(8,128)(2,1)S(1)} %collective-permute-done.6), channel_id=1, source_target_pairs={{0,2},{2,128},{4,6},{6,132},{8,10},{10,136},{12,14},{14,140},{16,1... | collective-permute-start | bytes 786440 | tf_op jit(solution)/shard_map/ppermute | solution.py:257
  53.1 15.3 %all-to-all-start.1 = ((bf16[4,128,512]{2,1,0:T(8,128)(2,1)}), bf16[4,128,512]{2,1,0:T(8,128)(2,1)S(1)}, u32[]{:S(2)}, u32[]{:S(2)}) async-start(bf16[4,128,512]{2,1,0:T(8,128)(2,1)} %get-tuple-element.28), calls=%async_computation.1 | async-start | bytes 1048576 | tf_op jit(solution)/shard_map/all_to_all | solution.py:266
  57.5 11.9 %collective-permute-start.10 = (bf16[2,256,128]{2,1,0:T(8,128)(2,1)S(1)}, bf16[2,256,128]{2,1,0:T(8,128)(2,1)S(1)}, u32[]{:S(2)}, u32[]{:S(2)}) collective-permute-start(bf16[2,256,128]{2,1,0:T(8,128)(2,1)S(1)} %get-tuple-element.33), channel_id=1, source_target_pairs={{0,126},{1,127},{2,64},{3,65},{4,66},{5,67},{6,68},{7,69},{8,70},{... | collective-permute-start | bytes 393224 | tf_op jit(solution)/shard_map/ppermute | solution.py:275
  64.0 5.4 %collective-permute-start.11 = (bf16[2,256,128]{2,1,0:T(8,128)(2,1)S(1)}, bf16[2,256,128]{2,1,0:T(8,128)(2,1)S(1)}, u32[]{:S(2)}, u32[]{:S(2)}) collective-permute-start(bf16[2,256,128]{2,1,0:T(8,128)(2,1)S(1)} %get-tuple-element.34), channel_id=1, source_target_pairs={{0,62},{1,63},{2,0},{3,1},{4,2},{5,3},{6,4},{7,5},{8,6},{9,7},{10,... | collective-permute-start | bytes 393224 | tf_op jit(solution)/shard_map/ppermute | solution.py:276

commit v7 on v6

--- a/solution.py
+++ b/solution.py
@@ -226,7 +226,7 @@
     visible = key_ids < jnp.repeat(query_ids, 2, axis=0).reshape(1, 1, 4, 2)
     hide = jnp.repeat(jnp.where(visible, f32(0.0), f32(HIDDEN)), TOK, axis=3)
 
-    turns = (1, 2, 3)
+    turns = (1, 3, 2)
     blocks = [along_y(kv, turn) for turn in turns] + [kv]
     dq = None
     parts = []
@@ -256,7 +256,7 @@
                 pairs.append(pair if step == 1 else pair[::-1])
         return lax.ppermute(block, axes, pairs)
 
-    before, opposite, after, mine = parts
+    before, after, opposite, mine = parts
     before = along_cores(before, -1)
     after = along_cores(after, 1)
     opposite = along_y(opposite, 2)

time: 70.6 us -> 70.2 us (level)
    ppermute x1, starting transfers between devices: 3.2 us -> 5.77 us  [per_device(): own = lax.ppermute(own, names, route(-1, lambda a, c: (a, c)))]
    ppermute x1, starting transfers between devices: 6.49 us -> 3.96 us  [per_device(): other = lax.ppermute(other, names, route(-1, lambda a, c: (1 - a, c)))]
    ppermute x4, starting transfers between devices: 14.7 us -> 16.6 us  [along_y(): lax.ppermute(block, 'y', [(i, (i + turn) % y_count) for i in range(y_coun...]
    ppermute x4, starting transfers between devices: 9.88 us -> 8.01 us  [along_cores(): return lax.ppermute(block, axes, pairs)]
  transfers between devices with their start and end apart: 14 -> 14, of which waited for: 3 -> 3; matrix products, arithmetic and copies ran while one was open for 1% -> 1% of each run, Pallas kernels for 22% -> 23%
where the time goes in v7:
time: 70.2 us; the launch traced here: 69.7 us
  starting transfers between devices  49.2 us (70%)
  Pallas kernels  16.5 us (24%)
  local copies, waits for them, and re-layouts  1.69 us (2%)
  waiting for transfers between devices  1.19 us (2%)
  between operations  0.89 us (1%)
    ppermute x4, starting transfers between devices, along_y(): lax.ppermute(block, 'y', [(i, (i + turn) % y_count) for i in range(y_coun...  16.6 us
    pallas_call x4, Pallas kernels, per_device(): pl.pallas_call(functools.partial(attend, turn, first, last), out_shape=(s...  11.9 us
    ppermute x4, starting transfers between devices, along_cores(): return lax.ppermute(block, axes, pairs)  8.01 us
    ppermute x1, starting transfers between devices, per_device(): own = lax.ppermute(own, names, route(-1, lambda a, c: (a, c)))  5.77 us
    all_to_all x1, starting transfers between devices, per_device(): dq = lax.all_to_all(dq, ('x_hi', 'x_lo'), 0, 0, tiled=True)  4.17 us
    ppermute x1, starting transfers between devices, per_device(): other = lax.ppermute(other, names, route(1, lambda a, c: (1 - a, 1 - c)))  4.12 us
    ppermute x1, starting transfers between devices, per_device(): other = lax.ppermute(other, names, route(-1, lambda a, c: (1 - a, c)))  3.96 us
    all_to_all x1, starting transfers between devices, per_device(): message = lax.all_to_all(message, ('x_hi', 'x_lo'), 0, 0, tiled=True)  3.53 us
  transfers between devices with their start and end apart: 14, of which 3 were waited for; matrix products, arithmetic and copies ran while one was open for 1% of the time, Pallas kernels for 23%

profile of v7, /device:TPU:1, one launch (start us, length us, event | category | flops | bytes accessed | tf_op | source)
XLA Modules:
  0.0 69.7 jit_solution(12944629998220426195)
XLA Ops:
  0.6 0.0 copy-start
  0.7 1.0 %dynamic-slice_bitcast_fusion = (bf16[1,256,128]{2,1,0:T(8,128)(2,1)S(1)}, bf16[1,256,128]{2,1,0:T(8,128)(2,1)S(1)}, bf16[1,256,128]{2,1,0:T(8,128)(2,1)S(1)}, bf16[1,256,128]{2,1,0:T(8,128)(2,1)S(1)}) fusion(bf16[256,512]{1,0:T(8,128)(2,1)} %param.9, s32[]{:T(128)S(6)} %select_n.48, s32[]{:T(128)S(6)} %select_n.47, bf16[256,512]{1,0:T(8,128)(2,1)} %param.8), kind=kLoop, calls=%fused_computation.3 | loop fusion | bytes 524296 | tf_op jit(solution)/shard_map/stack | solution.py:194
  1.6 3.0 %collective-permute-start = (bf16[2,256,128]{2,1,0:T(8,128)(2,1)S(1)}, bf16[2,256,128]{2,1,0:T(8,128)(2,1)S(1)}, u32[]{:S(2)}, u32[]{:S(2)}) collective-permute-start(bf16[2,256,128]{2,1,0:T(8,128)(2,1)S(1)} %pad_maximum_fusion.1), channel_id=1, source_target_pairs={{0,2},{1,3},{2,4},{3,5},{4,6},{5,7},{6,8},{7,9},{8,10},{9,11},{10,... | collective-permute-start | bytes 393224 | tf_op jit(solution)/shard_map/ppermute | solution.py:199
  4.7 4.1 %collective-permute-start.1 = (bf16[2,256,128]{2,1,0:T(8,128)(2,1)S(1)}, bf16[2,256,128]{2,1,0:T(8,128)(2,1)S(1)}, u32[]{:S(2)}, u32[]{:S(2)}) collective-permute-start(bf16[2,256,128]{2,1,0:T(8,128)(2,1)S(1)} %pad_maximum_fusion.2), channel_id=1, source_target_pairs={{0,67},{1,66},{2,69},{3,68},{4,71},{5,70},{6,73},{7,72},{8,75},{9,... | collective-permute-start | bytes 393224 | tf_op jit(solution)/shard_map/ppermute | solution.py:198
  8.8 0.0 copy-done
  8.9 0.1 reshape.21
  9.0 2.7 %pack_queries.1 = bf16[4,1056,128]{2,1,0:T(8,128)(2,1)} custom-call(bf16[256,1024]{1,0:T(8,128)(2,1)} %queries.1, bf16[256,1024]{1,0:T(8,128)(2,1)} %attn_out.1, bf16[256,1024]{1,0:T(8,128)(2,1)} %grad_out.1, f32[8,256]{1,0:T(8,128)} %row_total.1), custom_call_target="tpu_custom_call" | custom-call | tf_op jit(solution)/shard_map/pack_queries/pallas_call | solution.py:201
  11.7 0.0 collective-permute-done
  11.7 3.5 %all-to-all-start = ((bf16[4,1056,128]{2,1,0:T(8,128)(2,1)}), bf16[4,1056,128]{2,1,0:T(8,128)(2,1)S(1)}, u32[]{:S(2)}, u32[]{:S(2)}) async-start(bf16[4,1056,128]{2,1,0:T(8,128)(2,1)} %pack_queries.1), calls=%async_computation | async-start | bytes 2162688 | tf_op jit(solution)/shard_map/all_to_all | solution.py:217
  15.3 0.1 copy.14
  15.4 0.1 rev.6
  15.5 0.1 dynamic-slice_add_fusion
  15.6 0.0 collective-permute-done.1
  15.6 3.2 %collective-permute-start.2 = (bf16[2,2,256,128]{3,2,1,0:T(8,128)(2,1)S(1)}, bf16[2,2,256,128]{3,2,1,0:T(8,128)(2,1)S(1)}, u32[]{:S(2)}, u32[]{:S(2)}) collective-permute-start(bf16[2,2,256,128]{3,2,1,0:T(8,128)(2,1)S(1)} %pad_maximum_fusion.refs_2_), channel_id=1, source_target_pairs={{0,128},{128,256},{256,384},{384,0},{1,129},{129,257},{257,385},{3... | collective-permute-start | bytes 786440 | tf_op jit(solution)/shard_map/ppermute | solution.py:190
  18.9 0.1 copy.15
  18.9 0.1 compare_select_fusion
  19.0 0.1 broadcast_in_dim.20
  19.2 0.1 reshape.24.refs_0_
  19.3 3.4 %collective-permute-start.4 = (bf16[2,2,256,128]{3,2,1,0:T(8,128)(2,1)S(1)}, bf16[2,2,256,128]{3,2,1,0:T(8,128)(2,1)S(1)}, u32[]{:S(2)}, u32[]{:S(2)}) collective-permute-start(bf16[2,2,256,128]{3,2,1,0:T(8,128)(2,1)S(1)} %pad_maximum_fusion.refs_2_), channel_id=1, source_target_pairs={{0,384},{128,0},{256,128},{384,256},{1,385},{129,1},{257,129},{385... | collective-permute-start | bytes 786440 | tf_op jit(solution)/shard_map/ppermute | solution.py:190
  22.7 3.5 %collective-permute-start.6 = (bf16[2,2,256,128]{3,2,1,0:T(8,128)(2,1)S(1)}, bf16[2,2,256,128]{3,2,1,0:T(8,128)(2,1)S(1)}, u32[]{:S(2)}, u32[]{:S(2)}) collective-permute-start(bf16[2,2,256,128]{3,2,1,0:T(8,128)(2,1)S(1)} %pad_maximum_fusion.refs_2_), channel_id=1, source_target_pairs={{0,256},{128,384},{256,0},{384,128},{1,257},{129,385},{257,1},{385... | collective-permute-start | bytes 786440 | tf_op jit(solution)/shard_map/ppermute | solution.py:190
  26.2 0.0 collective-permute-done.2.refs_2_
  26.2 0.4 all-to-all-done.refs_1_
  26.6 2.8 %attend_1.1 = (f32[128,2048]{1,0:T(8,128)S(1)}, bf16[2,2,256,128]{3,2,1,0:T(8,128)(2,1)S(1)}) custom-call(f32[4,4,4,512]{3,2,1,0:T(4,128)S(1)} %reshape.24.refs_0_, bf16[4,1056,128]{2,1,0:T(8,128)(2,1)S(1)} %all-to-all-done.refs_1_, bf16[2,2,256,128]{3,2,1,0:T(8,128)(2,1)S(1)} %collective-permute-done.2.refs_2_), custom_call_target="tpu_custom_call" | custom-call | flops 10000000000 | tf_op jit(solution)/shard_map/attend_1/pallas_call | solution.py:235
  29.4 5.0 %collective-permute-start.3 = (bf16[2,2,256,128]{3,2,1,0:T(8,128)(2,1)S(1)}, bf16[2,2,256,128]{3,2,1,0:T(8,128)(2,1)S(1)}, u32[]{:S(2)}, u32[]{:S(2)}) collective-permute-start(bf16[2,2,256,128]{3,2,1,0:T(8,128)(2,1)S(1)} %get-tuple-element.22), channel_id=1, source_target_pairs={{2,0},{128,2},{6,4},{132,6},{10,8},{136,10},{14,12},{140,14},{18,1... | collective-permute-start | bytes 786440 | tf_op jit(solution)/shard_map/ppermute | solution.py:257
  34.4 0.0 collective-permute-done.4.refs_2_
  34.4 2.8 %attend_3.1 = (f32[128,2048]{1,0:T(8,128)S(1)}, bf16[2,2,256,128]{3,2,1,0:T(8,128)(2,1)S(1)}) custom-call(f32[4,4,4,512]{3,2,1,0:T(4,128)S(1)} %reshape.24.refs_0_, bf16[4,1056,128]{2,1,0:T(8,128)(2,1)S(1)} %all-to-all-done.refs_1_, bf16[2,2,256,128]{3,2,1,0:T(8,128)(2,1)S(1)} %collective-permute-done.4.refs_2_, f32[128,2048]{1,0:T(8,128)S(1)} %get-tuple-element.23.refs_3_), custom_call_target="tpu_custom_call" | custom-call | flops 10000000000 | tf_op jit(solution)/shard_map/attend_3/pallas_call | solution.py:235
  37.2 1.2 %collective-permute-start.5 = (bf16[2,2,256,128]{3,2,1,0:T(8,128)(2,1)S(1)}, bf16[2,2,256,128]{3,2,1,0:T(8,128)(2,1)S(1)}, u32[]{:S(2)}, u32[]{:S(2)}) collective-permute-start(bf16[2,2,256,128]{3,2,1,0:T(8,128)(2,1)S(1)} %get-tuple-element.24), channel_id=1, source_target_pairs={{0,2},{2,128},{4,6},{6,132},{8,10},{10,136},{12,14},{14,140},{16,1... | collective-permute-start | bytes 786440 | tf_op jit(solution)/shard_map/ppermute | solution.py:257
  38.4 0.0 collective-permute-done.6.refs_2_
  38.4 2.8 %attend_2.1 = (f32[128,2048]{1,0:T(8,128)S(1)}, bf16[2,2,256,128]{3,2,1,0:T(8,128)(2,1)S(1)}) custom-call(f32[4,4,4,512]{3,2,1,0:T(4,128)S(1)} %reshape.24.refs_0_, bf16[4,1056,128]{2,1,0:T(8,128)(2,1)S(1)} %all-to-all-done.refs_1_, bf16[2,2,256,128]{3,2,1,0:T(8,128)(2,1)S(1)} %collective-permute-done.6.refs_2_, f32[128,2048]{1,0:T(8,128)S(1)} %get-tuple-element.25.refs_3_), custom_call_target="tpu_custom_call" | custom-call | flops 10000000000 | tf_op jit(solution)/shard_map/attend_2/pallas_call | solution.py:235
  41.2 6.5 %collective-permute-start.9 = (bf16[2,2,256,128]{3,2,1,0:T(8,128)(2,1)S(1)}, bf16[2,2,256,128]{3,2,1,0:T(8,128)(2,1)S(1)}, u32[]{:S(2)}, u32[]{:S(2)}) collective-permute-start(bf16[2,2,256,128]{3,2,1,0:T(8,128)(2,1)S(1)} %get-tuple-element.32), channel_id=1, source_target_pairs={{0,256},{128,384},{256,0},{384,128},{1,257},{129,385},{257,1},{385... | collective-permute-start | bytes 786440 | tf_op jit(solution)/shard_map/ppermute | solution.py:190
  47.8 3.6 %attend_0.1 = (bf16[4,128,512]{2,1,0:T(8,128)(2,1)}, f32[2,2,256,128]{3,2,1,0:T(8,128)S(1)}) custom-call(f32[4,4,4,512]{3,2,1,0:T(4,128)S(1)} %reshape.24.refs_0_, bf16[4,1056,128]{2,1,0:T(8,128)(2,1)S(1)} %all-to-all-done.refs_1_, bf16[2,2,256,128]{3,2,1,0:T(8,128)(2,1)S(1)} %pad_maximum_fusion.refs_2_, f32[128,2048]{1,0:T(8,128)S(1)} %get-tuple-element.26.refs_3_), custom_call_target="tpu_custom_call" | custom-call | flops 10000000000 | tf_op jit(solution)/shard_map/attend_0/pallas_call | solution.py:235
  51.4 0.0 collective-permute-done.3
  51.4 0.0 collective-permute-done.5
  51.4 0.0 collective-permute-start.7
  51.4 1.7 %collective-permute-start.8 = (bf16[2,2,256,128]{3,2,1,0:T(8,128)(2,1)S(1)}, bf16[2,2,256,128]{3,2,1,0:T(8,128)(2,1)S(1)}, u32[]{:S(2)}, u32[]{:S(2)}) collective-permute-start(bf16[2,2,256,128]{3,2,1,0:T(8,128)(2,1)S(1)} %collective-permute-done.5), channel_id=1, source_target_pairs={{0,2},{2,128},{4,6},{6,132},{8,10},{10,136},{12,14},{14,140},{16,1... | collective-permute-start | bytes 786440 | tf_op jit(solution)/shard_map/ppermute | solution.py:257
  53.1 4.2 %all-to-all-start.1 = ((bf16[4,128,512]{2,1,0:T(8,128)(2,1)}), bf16[4,128,512]{2,1,0:T(8,128)(2,1)S(1)}, u32[]{:S(2)}, u32[]{:S(2)}) async-start(bf16[4,128,512]{2,1,0:T(8,128)(2,1)} %get-tuple-element.28), calls=%async_computation.1 | async-start | bytes 1048576 | tf_op jit(solution)/shard_map/all_to_all | solution.py:266
  57.3 0.0 collective-permute-done.9.c
  57.3 0.2 collective-permute-done.7.a
  57.4 0.0 collective-permute-done.8.b
  57.4 0.1 add_partials.1
  57.6 4.0 %collective-permute-start.10 = (bf16[2,256,128]{2,1,0:T(8,128)(2,1)S(1)}, bf16[2,256,128]{2,1,0:T(8,128)(2,1)S(1)}, u32[]{:S(2)}, u32[]{:S(2)}) collective-permute-start(bf16[2,256,128]{2,1,0:T(8,128)(2,1)S(1)} %get-tuple-element.33), channel_id=1, source_target_pairs={{0,126},{1,127},{2,64},{3,65},{4,66},{5,67},{6,68},{7,69},{8,70},{... | collective-permute-start | bytes 393224 | tf_op jit(solution)/shard_map/ppermute | solution.py:275
  61.5 5.8 %collective-permute-start.11 = (bf16[2,256,128]{2,1,0:T(8,128)(2,1)S(1)}, bf16[2,256,128]{2,1,0:T(8,128)(2,1)S(1)}, u32[]{:S(2)}, u32[]{:S(2)}) collective-permute-start(bf16[2,256,128]{2,1,0:T(8,128)(2,1)S(1)} %get-tuple-element.34), channel_id=1, source_target_pairs={{0,62},{1,63},{2,0},{3,1},{4,2},{5,3},{6,4},{7,5},{8,6},{9,7},{10,... | collective-permute-start | bytes 393224 | tf_op jit(solution)/shard_map/ppermute | solution.py:276
  67.3 0.7 all-to-all-done.1.dq
  68.0 1.0 %unpack_queries.1 = bf16[256,1024]{1,0:T(8,128)(2,1)} custom-call(bf16[4,128,512]{2,1,0:T(8,128)(2,1)S(1)} %all-to-all-done.1.dq), custom_call_target="tpu_custom_call" | custom-call | tf_op jit(solution)/shard_map/unpack_queries/pallas_call | solution.py:277
  68.9 0.0 collective-permute-done.10.other
  68.9 0.0 collective-permute-done.11.own
  69.0 0.7 %unpack_kv.1 = (bf16[256,256]{1,0:T(8,128)(2,1)}, bf16[256,256]{1,0:T(8,128)(2,1)}) custom-call(s32[8,128]{1,0:T(8,128)S(1)} %broadcast_in_dim.21.swap, bf16[2,256,128]{2,1,0:T(8,128)(2,1)S(1)} %collective-permute-done.10.other, bf16[2,256,128]{2,1,0:T(8,128)(2,1)S(1)} %collective-permute-done.11.own), custom_call_target="tpu_custom_call" | custom-call | tf_op jit(solution)/shard_map/unpack_kv/pallas_call | solution.py:285
  (8 shorter events, 0.1 us)
Async XLA Ops:
  0.6 8.2 %copy-start = (s32[512]{0:T(512)S(1)}, s32[512]{0:T(512)}, u32[]{:S(2)}) copy-start(s32[512]{0:T(512)} %param.13) | copy-start | bytes 6148
  1.6 10.1 %collective-permute-start = (bf16[2,256,128]{2,1,0:T(8,128)(2,1)S(1)}, bf16[2,256,128]{2,1,0:T(8,128)(2,1)S(1)}, u32[]{:S(2)}, u32[]{:S(2)}) collective-permute-start(bf16[2,256,128]{2,1,0:T(8,128)(2,1)S(1)} %pad_maximum_fusion.1), channel_id=1, source_target_pairs={{0,2},{1,3},{2,4},{3,5},{4,6},{5,7},{6,8},{7,9},{8,10},{9,11},{10,... | collective-permute-start | bytes 393224 | tf_op jit(solution)/shard_map/ppermute | solution.py:199
  4.7 10.9 %collective-permute-start.1 = (bf16[2,256,128]{2,1,0:T(8,128)(2,1)S(1)}, bf16[2,256,128]{2,1,0:T(8,128)(2,1)S(1)}, u32[]{:S(2)}, u32[]{:S(2)}) collective-permute-start(bf16[2,256,128]{2,1,0:T(8,128)(2,1)S(1)} %pad_maximum_fusion.2), channel_id=1, source_target_pairs={{0,67},{1,66},{2,69},{3,68},{4,71},{5,70},{6,73},{7,72},{8,75},{9,... | collective-permute-start | bytes 393224 | tf_op jit(solution)/shard_map/ppermute | solution.py:198
  11.7 14.9 %all-to-all-start = ((bf16[4,1056,128]{2,1,0:T(8,128)(2,1)}), bf16[4,1056,128]{2,1,0:T(8,128)(2,1)S(1)}, u32[]{:S(2)}, u32[]{:S(2)}) async-start(bf16[4,1056,128]{2,1,0:T(8,128)(2,1)} %pack_queries.1), calls=%async_computation | async-start | bytes 2162688 | tf_op jit(solution)/shard_map/all_to_all | solution.py:217
  15.6 10.6 %collective-permute-start.2 = (bf16[2,2,256,128]{3,2,1,0:T(8,128)(2,1)S(1)}, bf16[2,2,256,128]{3,2,1,0:T(8,128)(2,1)S(1)}, u32[]{:S(2)}, u32[]{:S(2)}) collective-permute-start(bf16[2,2,256,128]{3,2,1,0:T(8,128)(2,1)S(1)} %pad_maximum_fusion.refs_2_), channel_id=1, source_target_pairs={{0,128},{128,256},{256,384},{384,0},{1,129},{129,257},{257,385},{3... | collective-permute-start | bytes 786440 | tf_op jit(solution)/shard_map/ppermute | solution.py:190
  19.3 15.1 %collective-permute-start.4 = (bf16[2,2,256,128]{3,2,1,0:T(8,128)(2,1)S(1)}, bf16[2,2,256,128]{3,2,1,0:T(8,128)(2,1)S(1)}, u32[]{:S(2)}, u32[]{:S(2)}) collective-permute-start(bf16[2,2,256,128]{3,2,1,0:T(8,128)(2,1)S(1)} %pad_maximum_fusion.refs_2_), channel_id=1, source_target_pairs={{0,384},{128,0},{256,128},{384,256},{1,385},{129,1},{257,129},{385... | collective-permute-start | bytes 786440 | tf_op jit(solution)/shard_map/ppermute | solution.py:190
  22.7 15.8 %collective-permute-start.6 = (bf16[2,2,256,128]{3,2,1,0:T(8,128)(2,1)S(1)}, bf16[2,2,256,128]{3,2,1,0:T(8,128)(2,1)S(1)}, u32[]{:S(2)}, u32[]{:S(2)}) collective-permute-start(bf16[2,2,256,128]{3,2,1,0:T(8,128)(2,1)S(1)} %pad_maximum_fusion.refs_2_), channel_id=1, source_target_pairs={{0,256},{128,384},{256,0},{384,128},{1,257},{129,385},{257,1},{385... | collective-permute-start | bytes 786440 | tf_op jit(solution)/shard_map/ppermute | solution.py:190
  29.4 22.0 %collective-permute-start.3 = (bf16[2,2,256,128]{3,2,1,0:T(8,128)(2,1)S(1)}, bf16[2,2,256,128]{3,2,1,0:T(8,128)(2,1)S(1)}, u32[]{:S(2)}, u32[]{:S(2)}) collective-permute-start(bf16[2,2,256,128]{3,2,1,0:T(8,128)(2,1)S(1)} %get-tuple-element.22), channel_id=1, source_target_pairs={{2,0},{128,2},{6,4},{132,6},{10,8},{136,10},{14,12},{140,14},{18,1... | collective-permute-start | bytes 786440 | tf_op jit(solution)/shard_map/ppermute | solution.py:257
  37.2 14.1 %collective-permute-start.5 = (bf16[2,2,256,128]{3,2,1,0:T(8,128)(2,1)S(1)}, bf16[2,2,256,128]{3,2,1,0:T(8,128)(2,1)S(1)}, u32[]{:S(2)}, u32[]{:S(2)}) collective-permute-start(bf16[2,2,256,128]{3,2,1,0:T(8,128)(2,1)S(1)} %get-tuple-element.24), channel_id=1, source_target_pairs={{0,2},{2,128},{4,6},{6,132},{8,10},{10,136},{12,14},{14,140},{16,1... | collective-permute-start | bytes 786440 | tf_op jit(solution)/shard_map/ppermute | solution.py:257
  41.2 16.0 %collective-permute-start.9 = (bf16[2,2,256,128]{3,2,1,0:T(8,128)(2,1)S(1)}, bf16[2,2,256,128]{3,2,1,0:T(8,128)(2,1)S(1)}, u32[]{:S(2)}, u32[]{:S(2)}) collective-permute-start(bf16[2,2,256,128]{3,2,1,0:T(8,128)(2,1)S(1)} %get-tuple-element.32), channel_id=1, source_target_pairs={{0,256},{128,384},{256,0},{384,128},{1,257},{129,385},{257,1},{385... | collective-permute-start | bytes 786440 | tf_op jit(solution)/shard_map/ppermute | solution.py:190
  51.4 6.1 %collective-permute-start.7 = (bf16[2,2,256,128]{3,2,1,0:T(8,128)(2,1)S(1)}, bf16[2,2,256,128]{3,2,1,0:T(8,128)(2,1)S(1)}, u32[]{:S(2)}, u32[]{:S(2)}) collective-permute-start(bf16[2,2,256,128]{3,2,1,0:T(8,128)(2,1)S(1)} %collective-permute-done.3), channel_id=1, source_target_pairs={{2,0},{128,2},{6,4},{132,6},{10,8},{136,10},{14,12},{140,14},{18,1... | collective-permute-start | bytes 786440 | tf_op jit(solution)/shard_map/ppermute | solution.py:257
  51.4 6.1 %collective-permute-start.8 = (bf16[2,2,256,128]{3,2,1,0:T(8,128)(2,1)S(1)}, bf16[2,2,256,128]{3,2,1,0:T(8,128)(2,1)S(1)}, u32[]{:S(2)}, u32[]{:S(2)}) collective-permute-start(bf16[2,2,256,128]{3,2,1,0:T(8,128)(2,1)S(1)} %collective-permute-done.5), channel_id=1, source_target_pairs={{0,2},{2,128},{4,6},{6,132},{8,10},{10,136},{12,14},{14,140},{16,1... | collective-permute-start | bytes 786440 | tf_op jit(solution)/shard_map/ppermute | solution.py:257
  53.1 14.8 %all-to-all-start.1 = ((bf16[4,128,512]{2,1,0:T(8,128)(2,1)}), bf16[4,128,512]{2,1,0:T(8,128)(2,1)S(1)}, u32[]{:S(2)}, u32[]{:S(2)}) async-start(bf16[4,128,512]{2,1,0:T(8,128)(2,1)} %get-tuple-element.28), calls=%async_computation.1 | async-start | bytes 1048576 | tf_op jit(solution)/shard_map/all_to_all | solution.py:266
  57.6 11.4 %collective-permute-start.10 = (bf16[2,256,128]{2,1,0:T(8,128)(2,1)S(1)}, bf16[2,256,128]{2,1,0:T(8,128)(2,1)S(1)}, u32[]{:S(2)}, u32[]{:S(2)}) collective-permute-start(bf16[2,256,128]{2,1,0:T(8,128)(2,1)S(1)} %get-tuple-element.33), channel_id=1, source_target_pairs={{0,126},{1,127},{2,64},{3,65},{4,66},{5,67},{6,68},{7,69},{8,70},{... | collective-permute-start | bytes 393224 | tf_op jit(solution)/shard_map/ppermute | solution.py:275
  61.5 7.4 %collective-permute-start.11 = (bf16[2,256,128]{2,1,0:T(8,128)(2,1)S(1)}, bf16[2,256,128]{2,1,0:T(8,128)(2,1)S(1)}, u32[]{:S(2)}, u32[]{:S(2)}) collective-permute-start(bf16[2,256,128]{2,1,0:T(8,128)(2,1)S(1)} %get-tuple-element.34), channel_id=1, source_target_pairs={{0,62},{1,63},{2,0},{3,1},{4,2},{5,3},{6,4},{7,5},{8,6},{9,7},{10,... | collective-permute-start | bytes 393224 | tf_op jit(solution)/shard_map/ppermute | solution.py:276

commit v8 on v7

--- a/solution.py
+++ b/solution.py
@@ -260,8 +260,8 @@
     before = along_cores(before, -1)
     after = along_cores(after, 1)
     opposite = along_y(opposite, 2)
-    before, after, dq = lax.optimization_barrier((before, after, dq))
     before = along_cores(before, -1)
+    after, dq = lax.optimization_barrier((after, dq))
     after = along_cores(after, 1)
     dq = lax.all_to_all(dq, ("x_hi", "x_lo"), 0, 0, tiled=True)
     other, own = pl.pallas_call(

time: 70.2 us -> 70.2 us (level)
    ppermute x1, starting transfers between devices: 5.77 us -> 4.64 us  [per_device(): own = lax.ppermute(own, names, route(-1, lambda a, c: (a, c)))]
    ppermute x1, starting transfers between devices: 3.96 us -> 5.07 us  [per_device(): other = lax.ppermute(other, names, route(-1, lambda a, c: (1 - a, c)))]
where the time goes in v8:
time: 70.2 us; the launch traced here: 69.7 us
  starting transfers between devices  49.2 us (70%)
  Pallas kernels  16.5 us (24%)
  local copies, waits for them, and re-layouts  1.69 us (2%)
  waiting for transfers between devices  1.21 us (2%)
  between operations  0.9 us (1%)
    ppermute x4, starting transfers between devices, along_y(): lax.ppermute(block, 'y', [(i, (i + turn) % y_count) for i in range(y_coun...  16.7 us
    pallas_call x4, Pallas kernels, per_device(): pl.pallas_call(functools.partial(attend, turn, first, last), out_shape=(s...  11.9 us
    ppermute x4, starting transfers between devices, along_cores(): return lax.ppermute(block, axes, pairs)  7.97 us
    ppermute x1, starting transfers between devices, per_device(): other = lax.ppermute(other, names, route(-1, lambda a, c: (1 - a, c)))  5.07 us
    ppermute x1, starting transfers between devices, per_device(): own = lax.ppermute(own, names, route(-1, lambda a, c: (a, c)))  4.64 us
    all_to_all x1, starting transfers between devices, per_device(): dq = lax.all_to_all(dq, ('x_hi', 'x_lo'), 0, 0, tiled=True)  4.17 us
    ppermute x1, starting transfers between devices, per_device(): other = lax.ppermute(other, names, route(1, lambda a, c: (1 - a, 1 - c)))  4.12 us
    all_to_all x1, starting transfers between devices, per_device(): message = lax.all_to_all(message, ('x_hi', 'x_lo'), 0, 0, tiled=True)  3.53 us
  transfers between devices with their start and end apart: 14, of which 3 were waited for; matrix products, arithmetic and copies ran while one was open for 1% of the time, Pallas kernels for 23%

profile of v8, /device:TPU:1, one launch (start us, length us, event | category | flops | bytes accessed | tf_op | source)
XLA Modules:
  0.0 69.7 jit_solution(6030462135587122496)
XLA Ops:
  0.6 0.0 copy-start
  0.7 1.0 %dynamic-slice_bitcast_fusion = (bf16[1,256,128]{2,1,0:T(8,128)(2,1)S(1)}, bf16[1,256,128]{2,1,0:T(8,128)(2,1)S(1)}, bf16[1,256,128]{2,1,0:T(8,128)(2,1)S(1)}, bf16[1,256,128]{2,1,0:T(8,128)(2,1)S(1)}) fusion(bf16[256,512]{1,0:T(8,128)(2,1)} %param.9, s32[]{:T(128)S(6)} %select_n.48, s32[]{:T(128)S(6)} %select_n.47, bf16[256,512]{1,0:T(8,128)(2,1)} %param.8), kind=kLoop, calls=%fused_computation.3 | loop fusion | bytes 524296 | tf_op jit(solution)/shard_map/stack | solution.py:194
  1.6 3.0 %collective-permute-start = (bf16[2,256,128]{2,1,0:T(8,128)(2,1)S(1)}, bf16[2,256,128]{2,1,0:T(8,128)(2,1)S(1)}, u32[]{:S(2)}, u32[]{:S(2)}) collective-permute-start(bf16[2,256,128]{2,1,0:T(8,128)(2,1)S(1)} %pad_maximum_fusion.1), channel_id=1, source_target_pairs={{0,2},{1,3},{2,4},{3,5},{4,6},{5,7},{6,8},{7,9},{8,10},{9,11},{10,... | collective-permute-start | bytes 393224 | tf_op jit(solution)/shard_map/ppermute | solution.py:199
  4.7 4.1 %collective-permute-start.1 = (bf16[2,256,128]{2,1,0:T(8,128)(2,1)S(1)}, bf16[2,256,128]{2,1,0:T(8,128)(2,1)S(1)}, u32[]{:S(2)}, u32[]{:S(2)}) collective-permute-start(bf16[2,256,128]{2,1,0:T(8,128)(2,1)S(1)} %pad_maximum_fusion.2), channel_id=1, source_target_pairs={{0,67},{1,66},{2,69},{3,68},{4,71},{5,70},{6,73},{7,72},{8,75},{9,... | collective-permute-start | bytes 393224 | tf_op jit(solution)/shard_map/ppermute | solution.py:198
  8.8 0.0 copy-done
  8.9 0.1 reshape.21
  9.0 2.7 %pack_queries.1 = bf16[4,1056,128]{2,1,0:T(8,128)(2,1)} custom-call(bf16[256,1024]{1,0:T(8,128)(2,1)} %queries.1, bf16[256,1024]{1,0:T(8,128)(2,1)} %attn_out.1, bf16[256,1024]{1,0:T(8,128)(2,1)} %grad_out.1, f32[8,256]{1,0:T(8,128)} %row_total.1), custom_call_target="tpu_custom_call" | custom-call | tf_op jit(solution)/shard_map/pack_queries/pallas_call | solution.py:201
  11.7 0.0 collective-permute-done
  11.7 3.5 %all-to-all-start = ((bf16[4,1056,128]{2,1,0:T(8,128)(2,1)}), bf16[4,1056,128]{2,1,0:T(8,128)(2,1)S(1)}, u32[]{:S(2)}, u32[]{:S(2)}) async-start(bf16[4,1056,128]{2,1,0:T(8,128)(2,1)} %pack_queries.1), calls=%async_computation | async-start | bytes 2162688 | tf_op jit(solution)/shard_map/all_to_all | solution.py:217
  15.3 0.1 copy.14
  15.4 0.1 rev.6
  15.5 0.1 dynamic-slice_add_fusion
  15.6 0.0 collective-permute-done.1
  15.6 3.2 %collective-permute-start.3 = (bf16[2,2,256,128]{3,2,1,0:T(8,128)(2,1)S(1)}, bf16[2,2,256,128]{3,2,1,0:T(8,128)(2,1)S(1)}, u32[]{:S(2)}, u32[]{:S(2)}) collective-permute-start(bf16[2,2,256,128]{3,2,1,0:T(8,128)(2,1)S(1)} %pad_maximum_fusion.refs_2_), channel_id=1, source_target_pairs={{0,128},{128,256},{256,384},{384,0},{1,129},{129,257},{257,385},{3... | collective-permute-start | bytes 786440 | tf_op jit(solution)/shard_map/ppermute | solution.py:190
  18.9 0.1 copy.15
  18.9 0.1 compare_select_fusion
  19.0 0.1 broadcast_in_dim.20
  19.2 0.1 reshape.24.refs_0_
  19.3 3.4 %collective-permute-start.2 = (bf16[2,2,256,128]{3,2,1,0:T(8,128)(2,1)S(1)}, bf16[2,2,256,128]{3,2,1,0:T(8,128)(2,1)S(1)}, u32[]{:S(2)}, u32[]{:S(2)}) collective-permute-start(bf16[2,2,256,128]{3,2,1,0:T(8,128)(2,1)S(1)} %pad_maximum_fusion.refs_2_), channel_id=1, source_target_pairs={{0,384},{128,0},{256,128},{384,256},{1,385},{129,1},{257,129},{385... | collective-permute-start | bytes 786440 | tf_op jit(solution)/shard_map/ppermute | solution.py:190
  22.7 3.5 %collective-permute-start.5 = (bf16[2,2,256,128]{3,2,1,0:T(8,128)(2,1)S(1)}, bf16[2,2,256,128]{3,2,1,0:T(8,128)(2,1)S(1)}, u32[]{:S(2)}, u32[]{:S(2)}) collective-permute-start(bf16[2,2,256,128]{3,2,1,0:T(8,128)(2,1)S(1)} %pad_maximum_fusion.refs_2_), channel_id=1, source_target_pairs={{0,256},{128,384},{256,0},{384,128},{1,257},{129,385},{257,1},{385... | collective-permute-start | bytes 786440 | tf_op jit(solution)/shard_map/ppermute | solution.py:190
  26.2 0.0 collective-permute-done.3.refs_2_
  26.2 0.4 all-to-all-done.refs_1_
  26.6 2.8 %attend_1.1 = (f32[128,2048]{1,0:T(8,128)S(1)}, bf16[2,2,256,128]{3,2,1,0:T(8,128)(2,1)S(1)}) custom-call(f32[4,4,4,512]{3,2,1,0:T(4,128)S(1)} %reshape.24.refs_0_, bf16[4,1056,128]{2,1,0:T(8,128)(2,1)S(1)} %all-to-all-done.refs_1_, bf16[2,2,256,128]{3,2,1,0:T(8,128)(2,1)S(1)} %collective-permute-done.3.refs_2_), custom_call_target="tpu_custom_call" | custom-call | flops 10000000000 | tf_op jit(solution)/shard_map/attend_1/pallas_call | solution.py:235
  29.4 0.0 collective-permute-done.2.refs_2_
  29.4 2.8 %attend_3.1 = (f32[128,2048]{1,0:T(8,128)S(1)}, bf16[2,2,256,128]{3,2,1,0:T(8,128)(2,1)S(1)}) custom-call(f32[4,4,4,512]{3,2,1,0:T(4,128)S(1)} %reshape.24.refs_0_, bf16[4,1056,128]{2,1,0:T(8,128)(2,1)S(1)} %all-to-all-done.refs_1_, bf16[2,2,256,128]{3,2,1,0:T(8,128)(2,1)S(1)} %collective-permute-done.2.refs_2_, f32[128,2048]{1,0:T(8,128)S(1)} %get-tuple-element.21.refs_3_), custom_call_target="tpu_custom_call" | custom-call | flops 10000000000 | tf_op jit(solution)/shard_map/attend_3/pallas_call | solution.py:235
  32.2 6.2 %collective-permute-start.4 = (bf16[2,2,256,128]{3,2,1,0:T(8,128)(2,1)S(1)}, bf16[2,2,256,128]{3,2,1,0:T(8,128)(2,1)S(1)}, u32[]{:S(2)}, u32[]{:S(2)}) collective-permute-start(bf16[2,2,256,128]{3,2,1,0:T(8,128)(2,1)S(1)} %get-tuple-element.22), channel_id=1, source_target_pairs={{0,2},{2,128},{4,6},{6,132},{8,10},{10,136},{12,14},{14,140},{16,1... | collective-permute-start | bytes 786440 | tf_op jit(solution)/shard_map/ppermute | solution.py:257
  38.4 0.0 collective-permute-start.6
  38.4 0.0 collective-permute-done.5.refs_2_
  38.4 2.8 %attend_2.1 = (f32[128,2048]{1,0:T(8,128)S(1)}, bf16[2,2,256,128]{3,2,1,0:T(8,128)(2,1)S(1)}) custom-call(f32[4,4,4,512]{3,2,1,0:T(4,128)S(1)} %reshape.24.refs_0_, bf16[4,1056,128]{2,1,0:T(8,128)(2,1)S(1)} %all-to-all-done.refs_1_, bf16[2,2,256,128]{3,2,1,0:T(8,128)(2,1)S(1)} %collective-permute-done.5.refs_2_, f32[128,2048]{1,0:T(8,128)S(1)} %get-tuple-element.23.refs_3_), custom_call_target="tpu_custom_call" | custom-call | flops 10000000000 | tf_op jit(solution)/shard_map/attend_2/pallas_call | solution.py:235
  41.2 6.6 %collective-permute-start.9 = (bf16[2,2,256,128]{3,2,1,0:T(8,128)(2,1)S(1)}, bf16[2,2,256,128]{3,2,1,0:T(8,128)(2,1)S(1)}, u32[]{:S(2)}, u32[]{:S(2)}) collective-permute-start(bf16[2,2,256,128]{3,2,1,0:T(8,128)(2,1)S(1)} %get-tuple-element.30), channel_id=1, source_target_pairs={{0,256},{128,384},{256,0},{384,128},{1,257},{129,385},{257,1},{385... | collective-permute-start | bytes 786440 | tf_op jit(solution)/shard_map/ppermute | solution.py:190
  47.8 3.6 %attend_0.1 = (bf16[4,128,512]{2,1,0:T(8,128)(2,1)}, f32[2,2,256,128]{3,2,1,0:T(8,128)S(1)}) custom-call(f32[4,4,4,512]{3,2,1,0:T(4,128)S(1)} %reshape.24.refs_0_, bf16[4,1056,128]{2,1,0:T(8,128)(2,1)S(1)} %all-to-all-done.refs_1_, bf16[2,2,256,128]{3,2,1,0:T(8,128)(2,1)S(1)} %pad_maximum_fusion.refs_2_, f32[128,2048]{1,0:T(8,128)S(1)} %get-tuple-element.24.refs_3_), custom_call_target="tpu_custom_call" | custom-call | flops 10000000000 | tf_op jit(solution)/shard_map/attend_0/pallas_call | solution.py:235
  51.4 0.0 collective-permute-done.4
  51.4 0.0 collective-permute-done.6
  51.4 0.0 collective-permute-start.7
  51.4 1.7 %collective-permute-start.8 = (bf16[2,2,256,128]{3,2,1,0:T(8,128)(2,1)S(1)}, bf16[2,2,256,128]{3,2,1,0:T(8,128)(2,1)S(1)}, u32[]{:S(2)}, u32[]{:S(2)}) collective-permute-start(bf16[2,2,256,128]{3,2,1,0:T(8,128)(2,1)S(1)} %collective-permute-done.4), channel_id=1, source_target_pairs={{0,2},{2,128},{4,6},{6,132},{8,10},{10,136},{12,14},{14,140},{16,1... | collective-permute-start | bytes 786440 | tf_op jit(solution)/shard_map/ppermute | solution.py:257
  53.1 4.2 %all-to-all-start.1 = ((bf16[4,128,512]{2,1,0:T(8,128)(2,1)}), bf16[4,128,512]{2,1,0:T(8,128)(2,1)S(1)}, u32[]{:S(2)}, u32[]{:S(2)}) async-start(bf16[4,128,512]{2,1,0:T(8,128)(2,1)} %get-tuple-element.26), calls=%async_computation.1 | async-start | bytes 1048576 | tf_op jit(solution)/shard_map/all_to_all | solution.py:266
  57.3 0.0 collective-permute-done.9.c
  57.3 0.2 collective-permute-done.7.a
  57.5 0.0 collective-permute-done.8.b
  57.5 0.1 add_partials.1
  57.6 5.1 %collective-permute-start.10 = (bf16[2,256,128]{2,1,0:T(8,128)(2,1)S(1)}, bf16[2,256,128]{2,1,0:T(8,128)(2,1)S(1)}, u32[]{:S(2)}, u32[]{:S(2)}) collective-permute-start(bf16[2,256,128]{2,1,0:T(8,128)(2,1)S(1)} %get-tuple-element.31), channel_id=1, source_target_pairs={{0,126},{1,127},{2,64},{3,65},{4,66},{5,67},{6,68},{7,69},{8,70},{... | collective-permute-start | bytes 393224 | tf_op jit(solution)/shard_map/ppermute | solution.py:275
  62.7 4.6 %collective-permute-start.11 = (bf16[2,256,128]{2,1,0:T(8,128)(2,1)S(1)}, bf16[2,256,128]{2,1,0:T(8,128)(2,1)S(1)}, u32[]{:S(2)}, u32[]{:S(2)}) collective-permute-start(bf16[2,256,128]{2,1,0:T(8,128)(2,1)S(1)} %get-tuple-element.32), channel_id=1, source_target_pairs={{0,62},{1,63},{2,0},{3,1},{4,2},{5,3},{6,4},{7,5},{8,6},{9,7},{10,... | collective-permute-start | bytes 393224 | tf_op jit(solution)/shard_map/ppermute | solution.py:276
  67.3 0.7 all-to-all-done.1.dq
  68.0 1.0 %unpack_queries.1 = bf16[256,1024]{1,0:T(8,128)(2,1)} custom-call(bf16[4,128,512]{2,1,0:T(8,128)(2,1)S(1)} %all-to-all-done.1.dq), custom_call_target="tpu_custom_call" | custom-call | tf_op jit(solution)/shard_map/unpack_queries/pallas_call | solution.py:277
  68.9 0.0 collective-permute-done.10.other
  68.9 0.0 collective-permute-done.11.own
  69.0 0.7 %unpack_kv.1 = (bf16[256,256]{1,0:T(8,128)(2,1)}, bf16[256,256]{1,0:T(8,128)(2,1)}) custom-call(s32[8,128]{1,0:T(8,128)S(1)} %broadcast_in_dim.21.swap, bf16[2,256,128]{2,1,0:T(8,128)(2,1)S(1)} %collective-permute-done.10.other, bf16[2,256,128]{2,1,0:T(8,128)(2,1)S(1)} %collective-permute-done.11.own), custom_call_target="tpu_custom_call" | custom-call | tf_op jit(solution)/shard_map/unpack_kv/pallas_call | solution.py:285
  (8 shorter events, 0.1 us)
Async XLA Ops:
  0.6 8.2 %copy-start = (s32[512]{0:T(512)S(1)}, s32[512]{0:T(512)}, u32[]{:S(2)}) copy-start(s32[512]{0:T(512)} %param.13) | copy-start | bytes 6148
  1.6 10.1 %collective-permute-start = (bf16[2,256,128]{2,1,0:T(8,128)(2,1)S(1)}, bf16[2,256,128]{2,1,0:T(8,128)(2,1)S(1)}, u32[]{:S(2)}, u32[]{:S(2)}) collective-permute-start(bf16[2,256,128]{2,1,0:T(8,128)(2,1)S(1)} %pad_maximum_fusion.1), channel_id=1, source_target_pairs={{0,2},{1,3},{2,4},{3,5},{4,6},{5,7},{6,8},{7,9},{8,10},{9,11},{10,... | collective-permute-start | bytes 393224 | tf_op jit(solution)/shard_map/ppermute | solution.py:199
  4.7 10.9 %collective-permute-start.1 = (bf16[2,256,128]{2,1,0:T(8,128)(2,1)S(1)}, bf16[2,256,128]{2,1,0:T(8,128)(2,1)S(1)}, u32[]{:S(2)}, u32[]{:S(2)}) collective-permute-start(bf16[2,256,128]{2,1,0:T(8,128)(2,1)S(1)} %pad_maximum_fusion.2), channel_id=1, source_target_pairs={{0,67},{1,66},{2,69},{3,68},{4,71},{5,70},{6,73},{7,72},{8,75},{9,... | collective-permute-start | bytes 393224 | tf_op jit(solution)/shard_map/ppermute | solution.py:198
  11.7 14.9 %all-to-all-start = ((bf16[4,1056,128]{2,1,0:T(8,128)(2,1)}), bf16[4,1056,128]{2,1,0:T(8,128)(2,1)S(1)}, u32[]{:S(2)}, u32[]{:S(2)}) async-start(bf16[4,1056,128]{2,1,0:T(8,128)(2,1)} %pack_queries.1), calls=%async_computation | async-start | bytes 2162688 | tf_op jit(solution)/shard_map/all_to_all | solution.py:217
  15.6 10.6 %collective-permute-start.3 = (bf16[2,2,256,128]{3,2,1,0:T(8,128)(2,1)S(1)}, bf16[2,2,256,128]{3,2,1,0:T(8,128)(2,1)S(1)}, u32[]{:S(2)}, u32[]{:S(2)}) collective-permute-start(bf16[2,2,256,128]{3,2,1,0:T(8,128)(2,1)S(1)} %pad_maximum_fusion.refs_2_), channel_id=1, source_target_pairs={{0,128},{128,256},{256,384},{384,0},{1,129},{129,257},{257,385},{3... | collective-permute-start | bytes 786440 | tf_op jit(solution)/shard_map/ppermute | solution.py:190
  19.3 10.1 %collective-permute-start.2 = (bf16[2,2,256,128]{3,2,1,0:T(8,128)(2,1)S(1)}, bf16[2,2,256,128]{3,2,1,0:T(8,128)(2,1)S(1)}, u32[]{:S(2)}, u32[]{:S(2)}) collective-permute-start(bf16[2,2,256,128]{3,2,1,0:T(8,128)(2,1)S(1)} %pad_maximum_fusion.refs_2_), channel_id=1, source_target_pairs={{0,384},{128,0},{256,128},{384,256},{1,385},{129,1},{257,129},{385... | collective-permute-start | bytes 786440 | tf_op jit(solution)/shard_map/ppermute | solution.py:190
  22.7 15.7 %collective-permute-start.5 = (bf16[2,2,256,128]{3,2,1,0:T(8,128)(2,1)S(1)}, bf16[2,2,256,128]{3,2,1,0:T(8,128)(2,1)S(1)}, u32[]{:S(2)}, u32[]{:S(2)}) collective-permute-start(bf16[2,2,256,128]{3,2,1,0:T(8,128)(2,1)S(1)} %pad_maximum_fusion.refs_2_), channel_id=1, source_target_pairs={{0,256},{128,384},{256,0},{384,128},{1,257},{129,385},{257,1},{385... | collective-permute-start | bytes 786440 | tf_op jit(solution)/shard_map/ppermute | solution.py:190
  32.2 19.2 %collective-permute-start.4 = (bf16[2,2,256,128]{3,2,1,0:T(8,128)(2,1)S(1)}, bf16[2,2,256,128]{3,2,1,0:T(8,128)(2,1)S(1)}, u32[]{:S(2)}, u32[]{:S(2)}) collective-permute-start(bf16[2,2,256,128]{3,2,1,0:T(8,128)(2,1)S(1)} %get-tuple-element.22), channel_id=1, source_target_pairs={{0,2},{2,128},{4,6},{6,132},{8,10},{10,136},{12,14},{14,140},{16,1... | collective-permute-start | bytes 786440 | tf_op jit(solution)/shard_map/ppermute | solution.py:257
  38.4 12.9 %collective-permute-start.6 = (bf16[2,2,256,128]{3,2,1,0:T(8,128)(2,1)S(1)}, bf16[2,2,256,128]{3,2,1,0:T(8,128)(2,1)S(1)}, u32[]{:S(2)}, u32[]{:S(2)}) collective-permute-start(bf16[2,2,256,128]{3,2,1,0:T(8,128)(2,1)S(1)} %get-tuple-element.28), channel_id=1, source_target_pairs={{2,0},{128,2},{6,4},{132,6},{10,8},{136,10},{14,12},{140,14},{18,1... | collective-permute-start | bytes 786440 | tf_op jit(solution)/shard_map/ppermute | solution.py:257
  41.2 16.1 %collective-permute-start.9 = (bf16[2,2,256,128]{3,2,1,0:T(8,128)(2,1)S(1)}, bf16[2,2,256,128]{3,2,1,0:T(8,128)(2,1)S(1)}, u32[]{:S(2)}, u32[]{:S(2)}) collective-permute-start(bf16[2,2,256,128]{3,2,1,0:T(8,128)(2,1)S(1)} %get-tuple-element.30), channel_id=1, source_target_pairs={{0,256},{128,384},{256,0},{384,128},{1,257},{129,385},{257,1},{385... | collective-permute-start | bytes 786440 | tf_op jit(solution)/shard_map/ppermute | solution.py:190
  51.4 6.1 %collective-permute-start.7 = (bf16[2,2,256,128]{3,2,1,0:T(8,128)(2,1)S(1)}, bf16[2,2,256,128]{3,2,1,0:T(8,128)(2,1)S(1)}, u32[]{:S(2)}, u32[]{:S(2)}) collective-permute-start(bf16[2,2,256,128]{3,2,1,0:T(8,128)(2,1)S(1)} %collective-permute-done.6), channel_id=1, source_target_pairs={{2,0},{128,2},{6,4},{132,6},{10,8},{136,10},{14,12},{140,14},{18,1... | collective-permute-start | bytes 786440 | tf_op jit(solution)/shard_map/ppermute | solution.py:257
  51.4 6.1 %collective-permute-start.8 = (bf16[2,2,256,128]{3,2,1,0:T(8,128)(2,1)S(1)}, bf16[2,2,256,128]{3,2,1,0:T(8,128)(2,1)S(1)}, u32[]{:S(2)}, u32[]{:S(2)}) collective-permute-start(bf16[2,2,256,128]{3,2,1,0:T(8,128)(2,1)S(1)} %collective-permute-done.4), channel_id=1, source_target_pairs={{0,2},{2,128},{4,6},{6,132},{8,10},{10,136},{12,14},{14,140},{16,1... | collective-permute-start | bytes 786440 | tf_op jit(solution)/shard_map/ppermute | solution.py:257
  53.1 14.8 %all-to-all-start.1 = ((bf16[4,128,512]{2,1,0:T(8,128)(2,1)}), bf16[4,128,512]{2,1,0:T(8,128)(2,1)S(1)}, u32[]{:S(2)}, u32[]{:S(2)}) async-start(bf16[4,128,512]{2,1,0:T(8,128)(2,1)} %get-tuple-element.26), calls=%async_computation.1 | async-start | bytes 1048576 | tf_op jit(solution)/shard_map/all_to_all | solution.py:266
  57.6 11.4 %collective-permute-start.10 = (bf16[2,256,128]{2,1,0:T(8,128)(2,1)S(1)}, bf16[2,256,128]{2,1,0:T(8,128)(2,1)S(1)}, u32[]{:S(2)}, u32[]{:S(2)}) collective-permute-start(bf16[2,256,128]{2,1,0:T(8,128)(2,1)S(1)} %get-tuple-element.31), channel_id=1, source_target_pairs={{0,126},{1,127},{2,64},{3,65},{4,66},{5,67},{6,68},{7,69},{8,70},{... | collective-permute-start | bytes 393224 | tf_op jit(solution)/shard_map/ppermute | solution.py:275
  62.7 6.3 %collective-permute-start.11 = (bf16[2,256,128]{2,1,0:T(8,128)(2,1)S(1)}, bf16[2,256,128]{2,1,0:T(8,128)(2,1)S(1)}, u32[]{:S(2)}, u32[]{:S(2)}) collective-permute-start(bf16[2,256,128]{2,1,0:T(8,128)(2,1)S(1)} %get-tuple-element.32), channel_id=1, source_target_pairs={{0,62},{1,63},{2,0},{3,1},{4,2},{5,3},{6,4},{7,5},{8,6},{9,7},{10,... | collective-permute-start | bytes 393224 | tf_op jit(solution)/shard_map/ppermute | solution.py:276
